TPU v7x, 32 devices: a whole 2x2x4 slice. The times are simulated.
32 devices in a mesh: wide: 8 (over z, y), narrow: 4 (over x, core).
Axes of the slice: x: 2, y: 2, z: 4, core: 2. Of those that a mesh axis runs over, the one named last changes fastest.
Arguments:
- hist_features: float32 [16, 131072], P(None, ('wide', 'narrow')), may hold values from -6 to 6
- hist_weights: float32 [8, 131072], P(None, ('wide', 'narrow')), may hold values from -6 to 6
- anal_features: float32 [16, 8192], P(None, 'narrow'), may hold values from -6 to 6
- anal_weights: float32 [8, 8192], P(None, 'narrow'), may hold values from -6 to 6
- lengthscale: float32 [16], replicated, may hold values from 1.2 to 3
- amplitude: float32 [8], replicated, may hold values from 4 to 16
Outputs:
- anal_out: float32 [8, 8192], P(None, 'narrow')
- hist_out: float32 [8, 131072], P(None, ('wide', 'narrow'))
All inputs are finite; a program needn't handle non-finite values.
Results may differ from a plain program's by a relative error of at most 0.00029.
Values sent between devices are 32-bit elements; how exact they have to be, the bound alone decides.
No kernel may reach another device: no remote copies, remote signals or barrier semaphores. Data moves between devices by JAX's collectives and lax.ppermute only.
A program may use at most 64 MiB of HBM per device.

v0:
```python
import math

import jax
import jax.numpy as jnp
from jax import lax
from jax.sharding import PartitionSpec as P


def scaled_rows(features, lengthscale):
    scaled = features / lengthscale[:, None]
    return (scaled, jnp.sum(scaled * scaled, axis=0))


def kernel_tile(left, left_norms, right, right_norms):
    cross = jnp.einsum("fa,fh->ah", left, right, precision=lax.Precision.HIGHEST)
    return jnp.exp(-0.5 * (left_norms[:, None] + right_norms[None, :] - 2.0 * cross))


def product(left, right):
    return jnp.dot(left, right, precision=lax.Precision.HIGHEST, preferred_element_type=jnp.float32)


def on_device(hist_features, hist_weights, anal_features, anal_weights, lengthscale, amplitude):
    hist_count = hist_features.shape[1]
    anal_count = anal_features.shape[1]
    targets = hist_weights.shape[0]
    narrow_size = lax.axis_size("narrow")
    hist_total = hist_count * lax.axis_size("wide") * narrow_size
    anal_total = anal_count * narrow_size
    hist_scaled, hist_norms = scaled_rows(hist_features, lengthscale)
    initial = (
        jnp.zeros((targets, hist_count), jnp.float32),
        jnp.zeros((targets, anal_total), jnp.float32),
    )
    piece_features = lax.all_gather(anal_features, "narrow", axis=1, tiled=True)
    piece_weights = lax.all_gather(anal_weights, "narrow", axis=1, tiled=True)
    piece_scaled, piece_norms = scaled_rows(piece_features, lengthscale)
    length = piece_features.shape[1]
    block = math.gcd(length, 512)

    def step(index, inner):
        trans_acc, fwd_acc = inner
        offset = index * block
        left = lax.dynamic_slice_in_dim(piece_scaled, offset, block, 1)
        left_norms = lax.dynamic_slice_in_dim(piece_norms, offset, block, 0)
        left_weights = lax.dynamic_slice_in_dim(piece_weights, offset, block, 1)
        tile = kernel_tile(left, left_norms, hist_scaled, hist_norms)
        trans_acc = trans_acc + product(left_weights, tile)
        values = product(hist_weights, tile.T)
        fwd_acc = lax.dynamic_update_slice_in_dim(fwd_acc, values, offset, 1)
        return (trans_acc, fwd_acc)

    transposed, partial_sums = lax.fori_loop(0, length // block, step, initial)
    totals = lax.psum(partial_sums, ("wide", "narrow"))
    forward = lax.dynamic_slice_in_dim(totals, lax.axis_index("narrow") * anal_count, anal_count, 1)
    anal_out = forward * (amplitude[:, None] / math.sqrt(hist_total))
    hist_out = transposed * (amplitude[:, None] / math.sqrt(anal_total))
    return (anal_out, hist_out)


def solution(mesh):
    in_specs = (
        P(None, ("wide", "narrow")),
        P(None, ("wide", "narrow")),
        P(None, "narrow"),
        P(None, "narrow"),
        P(),
        P(),
    )
    out_specs = (P(None, "narrow"), P(None, ("wide", "narrow")))
    return jax.shard_map(
        on_device, mesh=mesh, in_specs=in_specs, out_specs=out_specs, check_vma=False
    )
```

profile of v0, /device:TPU:0, one launch (start us, length us, event | category | flops | bytes accessed | tf_op | source)
XLA Modules:
  0.0 543.1 jit_solution(6105677572942454110)
XLA Ops:
  7.2 7.4 %all_gather.6 = f32[8,8192]{1,0:T(8,128)S(1)} all-gather(f32[8,2048]{1,0:T(8,128)} %param.11), channel_id=1, replica_groups=mesh['wide'=8,'narrow'=4] {'narrow'}, dimensions={1}, use_global_device_ids=true | all-gather | bytes 327680 | tf_op jit(solution)/shard_map/all_gather | solution.py:36
  14.6 7.5 %all_gather.7 = f32[16,8192]{1,0:T(8,128)S(1)} all-gather(f32[16,2048]{1,0:T(8,128)} %param.10), channel_id=1, replica_groups=mesh['wide'=8,'narrow'=4] {'narrow'}, dimensions={1}, use_global_device_ids=true | all-gather | bytes 655360 | tf_op jit(solution)/shard_map/all_gather | solution.py:35
  22.1 0.8 multiply_reduce_fusion
  23.0 1.1 multiply_reduce_fusion.1
  24.1 383.3 %while.16 = (s32[]{:T(128)}, f32[8,4096]{1,0:T(8,128)S(1)}, f32[8,8192]{1,0:T(8,128)S(1)}, f32[8,8192]{1,0:T(8,128)S(1)}, f32[8192]{0:T(1024)S(1)}, /*index=5*/f...) while((s32[]{:T(128)}, f32[8,4096]{1,0:T(8,128)S(1)}, ...), condition=%wide.region_3.0_spmd.clone, body=%wide.region_2.0_spmd.clone.sunk | while | flops 813760512 | bytes 59988228 | solution.py:53
  24.2 10.2 %multiply_exponential_fusion.2 = f32[512,4096]{1,0:T(8,128)} fusion(f32[16,4096]{1,0:T(8,128)S(1)} %get-tuple-element.301, f32[4096]{0:T(1024)S(1)} %get-tuple-element.299, f32[512]{0:T(512)S(1)} %dynamic_slice.38, f32[16,8192]{1,0:T(8,128)S(1)} %get-tuple-element.300, s32[]{:T(128)S(6)} %select_n.16), kind=kOutput, calls=%fused_computation.clone.1 | convolution fusion | flops 411041792 | bytes 8701956 | tf_op jit(solution)/shard_map/while/body/eval_jaxpr/fa,fh->ah/dot_general | solution.py:15
  34.4 6.5 %convolution_add_fusion.2 = f32[8,4096]{1,0:T(8,128)S(1)} fusion(f32[512,4096]{1,0:T(8,128)} %multiply_exponential_fusion.2, f32[8,4096]{1,0:T(8,128)S(1)} %get-tuple-element.282, pred[]{:T(512)S(6)} %compare.3, f32[8,8192]{1,0:T(8,128)S(1)} %get-tuple-element.297, s32[]{:T(128)S(6)} %select_n.16), kind=kOutput, calls=%fused_computation.1.clone.1 | convolution fusion | flops 201392128 | bytes 8667141 | tf_op jit(solution)/shard_map/while/body/eval_jaxpr/dot_general | solution.py:20
  40.9 7.2 %fusion.22 = f32[8,8192]{1,0:T(8,128)S(1)} fusion(f32[8,8192]{1,0:T(8,128)S(1)} %get-tuple-element.283, s32[]{:T(128)S(6)} %select_n.16, f32[512,4096]{1,0:T(8,128)S(1)} %copy-done, f32[8,4096]{1,0:T(8,128)S(1)} %copy-done.1), kind=kOutput, calls=%fused_computation.3.clone.1 | convolution fusion | flops 201326592 | bytes 8536068 | tf_op jit(solution)/shard_map/while/body/eval_jaxpr/dot_general | solution.py:20
  48.1 10.2 %multiply_exponential_fusion.2 = f32[512,4096]{1,0:T(8,128)} fusion(f32[16,4096]{1,0:T(8,128)S(1)} %get-tuple-element.301, f32[4096]{0:T(1024)S(1)} %get-tuple-element.299, f32[512]{0:T(512)S(1)} %dynamic_slice.38, f32[16,8192]{1,0:T(8,128)S(1)} %get-tuple-element.300, s32[]{:T(128)S(6)} %select_n.16), kind=kOutput, calls=%fused_computation.clone.1 | convolution fusion | flops 411041792 | bytes 8701956 | tf_op jit(solution)/shard_map/while/body/eval_jaxpr/fa,fh->ah/dot_general | solution.py:15
  58.3 6.5 %convolution_add_fusion.2 = f32[8,4096]{1,0:T(8,128)S(1)} fusion(f32[512,4096]{1,0:T(8,128)} %multiply_exponential_fusion.2, f32[8,4096]{1,0:T(8,128)S(1)} %get-tuple-element.282, pred[]{:T(512)S(6)} %compare.3, f32[8,8192]{1,0:T(8,128)S(1)} %get-tuple-element.297, s32[]{:T(128)S(6)} %select_n.16), kind=kOutput, calls=%fused_computation.1.clone.1 | convolution fusion | flops 201392128 | bytes 8667141 | tf_op jit(solution)/shard_map/while/body/eval_jaxpr/dot_general | solution.py:20
  64.8 7.2 %fusion.22 = f32[8,8192]{1,0:T(8,128)S(1)} fusion(f32[8,8192]{1,0:T(8,128)S(1)} %get-tuple-element.283, s32[]{:T(128)S(6)} %select_n.16, f32[512,4096]{1,0:T(8,128)S(1)} %copy-done, f32[8,4096]{1,0:T(8,128)S(1)} %copy-done.1), kind=kOutput, calls=%fused_computation.3.clone.1 | convolution fusion | flops 201326592 | bytes 8536068 | tf_op jit(solution)/shard_map/while/body/eval_jaxpr/dot_general | solution.py:20
  72.0 0.1 dynamic_slice.38
  72.1 10.2 %multiply_exponential_fusion.2 = f32[512,4096]{1,0:T(8,128)} fusion(f32[16,4096]{1,0:T(8,128)S(1)} %get-tuple-element.301, f32[4096]{0:T(1024)S(1)} %get-tuple-element.299, f32[512]{0:T(512)S(1)} %dynamic_slice.38, f32[16,8192]{1,0:T(8,128)S(1)} %get-tuple-element.300, s32[]{:T(128)S(6)} %select_n.16), kind=kOutput, calls=%fused_computation.clone.1 | convolution fusion | flops 411041792 | bytes 8701956 | tf_op jit(solution)/shard_map/while/body/eval_jaxpr/fa,fh->ah/dot_general | solution.py:15
  82.3 6.5 %convolution_add_fusion.2 = f32[8,4096]{1,0:T(8,128)S(1)} fusion(f32[512,4096]{1,0:T(8,128)} %multiply_exponential_fusion.2, f32[8,4096]{1,0:T(8,128)S(1)} %get-tuple-element.282, pred[]{:T(512)S(6)} %compare.3, f32[8,8192]{1,0:T(8,128)S(1)} %get-tuple-element.297, s32[]{:T(128)S(6)} %select_n.16), kind=kOutput, calls=%fused_computation.1.clone.1 | convolution fusion | flops 201392128 | bytes 8667141 | tf_op jit(solution)/shard_map/while/body/eval_jaxpr/dot_general | solution.py:20
  88.8 7.2 %fusion.22 = f32[8,8192]{1,0:T(8,128)S(1)} fusion(f32[8,8192]{1,0:T(8,128)S(1)} %get-tuple-element.283, s32[]{:T(128)S(6)} %select_n.16, f32[512,4096]{1,0:T(8,128)S(1)} %copy-done, f32[8,4096]{1,0:T(8,128)S(1)} %copy-done.1), kind=kOutput, calls=%fused_computation.3.clone.1 | convolution fusion | flops 201326592 | bytes 8536068 | tf_op jit(solution)/shard_map/while/body/eval_jaxpr/dot_general | solution.py:20
  96.0 0.1 dynamic_slice.38
  96.0 10.2 %multiply_exponential_fusion.2 = f32[512,4096]{1,0:T(8,128)} fusion(f32[16,4096]{1,0:T(8,128)S(1)} %get-tuple-element.301, f32[4096]{0:T(1024)S(1)} %get-tuple-element.299, f32[512]{0:T(512)S(1)} %dynamic_slice.38, f32[16,8192]{1,0:T(8,128)S(1)} %get-tuple-element.300, s32[]{:T(128)S(6)} %select_n.16), kind=kOutput, calls=%fused_computation.clone.1 | convolution fusion | flops 411041792 | bytes 8701956 | tf_op jit(solution)/shard_map/while/body/eval_jaxpr/fa,fh->ah/dot_general | solution.py:15
  106.2 6.5 %convolution_add_fusion.2 = f32[8,4096]{1,0:T(8,128)S(1)} fusion(f32[512,4096]{1,0:T(8,128)} %multiply_exponential_fusion.2, f32[8,4096]{1,0:T(8,128)S(1)} %get-tuple-element.282, pred[]{:T(512)S(6)} %compare.3, f32[8,8192]{1,0:T(8,128)S(1)} %get-tuple-element.297, s32[]{:T(128)S(6)} %select_n.16), kind=kOutput, calls=%fused_computation.1.clone.1 | convolution fusion | flops 201392128 | bytes 8667141 | tf_op jit(solution)/shard_map/while/body/eval_jaxpr/dot_general | solution.py:20
  112.7 7.2 %fusion.22 = f32[8,8192]{1,0:T(8,128)S(1)} fusion(f32[8,8192]{1,0:T(8,128)S(1)} %get-tuple-element.283, s32[]{:T(128)S(6)} %select_n.16, f32[512,4096]{1,0:T(8,128)S(1)} %copy-done, f32[8,4096]{1,0:T(8,128)S(1)} %copy-done.1), kind=kOutput, calls=%fused_computation.3.clone.1 | convolution fusion | flops 201326592 | bytes 8536068 | tf_op jit(solution)/shard_map/while/body/eval_jaxpr/dot_general | solution.py:20
  120.0 10.2 %multiply_exponential_fusion.2 = f32[512,4096]{1,0:T(8,128)} fusion(f32[16,4096]{1,0:T(8,128)S(1)} %get-tuple-element.301, f32[4096]{0:T(1024)S(1)} %get-tuple-element.299, f32[512]{0:T(512)S(1)} %dynamic_slice.38, f32[16,8192]{1,0:T(8,128)S(1)} %get-tuple-element.300, s32[]{:T(128)S(6)} %select_n.16), kind=kOutput, calls=%fused_computation.clone.1 | convolution fusion | flops 411041792 | bytes 8701956 | tf_op jit(solution)/shard_map/while/body/eval_jaxpr/fa,fh->ah/dot_general | solution.py:15
  130.2 6.5 %convolution_add_fusion.2 = f32[8,4096]{1,0:T(8,128)S(1)} fusion(f32[512,4096]{1,0:T(8,128)} %multiply_exponential_fusion.2, f32[8,4096]{1,0:T(8,128)S(1)} %get-tuple-element.282, pred[]{:T(512)S(6)} %compare.3, f32[8,8192]{1,0:T(8,128)S(1)} %get-tuple-element.297, s32[]{:T(128)S(6)} %select_n.16), kind=kOutput, calls=%fused_computation.1.clone.1 | convolution fusion | flops 201392128 | bytes 8667141 | tf_op jit(solution)/shard_map/while/body/eval_jaxpr/dot_general | solution.py:20
  136.7 7.2 %fusion.22 = f32[8,8192]{1,0:T(8,128)S(1)} fusion(f32[8,8192]{1,0:T(8,128)S(1)} %get-tuple-element.283, s32[]{:T(128)S(6)} %select_n.16, f32[512,4096]{1,0:T(8,128)S(1)} %copy-done, f32[8,4096]{1,0:T(8,128)S(1)} %copy-done.1), kind=kOutput, calls=%fused_computation.3.clone.1 | convolution fusion | flops 201326592 | bytes 8536068 | tf_op jit(solution)/shard_map/while/body/eval_jaxpr/dot_general | solution.py:20
  143.9 10.2 %multiply_exponential_fusion.2 = f32[512,4096]{1,0:T(8,128)} fusion(f32[16,4096]{1,0:T(8,128)S(1)} %get-tuple-element.301, f32[4096]{0:T(1024)S(1)} %get-tuple-element.299, f32[512]{0:T(512)S(1)} %dynamic_slice.38, f32[16,8192]{1,0:T(8,128)S(1)} %get-tuple-element.300, s32[]{:T(128)S(6)} %select_n.16), kind=kOutput, calls=%fused_computation.clone.1 | convolution fusion | flops 411041792 | bytes 8701956 | tf_op jit(solution)/shard_map/while/body/eval_jaxpr/fa,fh->ah/dot_general | solution.py:15
  154.1 6.5 %convolution_add_fusion.2 = f32[8,4096]{1,0:T(8,128)S(1)} fusion(f32[512,4096]{1,0:T(8,128)} %multiply_exponential_fusion.2, f32[8,4096]{1,0:T(8,128)S(1)} %get-tuple-element.282, pred[]{:T(512)S(6)} %compare.3, f32[8,8192]{1,0:T(8,128)S(1)} %get-tuple-element.297, s32[]{:T(128)S(6)} %select_n.16), kind=kOutput, calls=%fused_computation.1.clone.1 | convolution fusion | flops 201392128 | bytes 8667141 | tf_op jit(solution)/shard_map/while/body/eval_jaxpr/dot_general | solution.py:20
  160.6 7.2 %fusion.22 = f32[8,8192]{1,0:T(8,128)S(1)} fusion(f32[8,8192]{1,0:T(8,128)S(1)} %get-tuple-element.283, s32[]{:T(128)S(6)} %select_n.16, f32[512,4096]{1,0:T(8,128)S(1)} %copy-done, f32[8,4096]{1,0:T(8,128)S(1)} %copy-done.1), kind=kOutput, calls=%fused_computation.3.clone.1 | convolution fusion | flops 201326592 | bytes 8536068 | tf_op jit(solution)/shard_map/while/body/eval_jaxpr/dot_general | solution.py:20
  167.8 0.1 dynamic_slice.38
  167.9 10.2 %multiply_exponential_fusion.2 = f32[512,4096]{1,0:T(8,128)} fusion(f32[16,4096]{1,0:T(8,128)S(1)} %get-tuple-element.301, f32[4096]{0:T(1024)S(1)} %get-tuple-element.299, f32[512]{0:T(512)S(1)} %dynamic_slice.38, f32[16,8192]{1,0:T(8,128)S(1)} %get-tuple-element.300, s32[]{:T(128)S(6)} %select_n.16), kind=kOutput, calls=%fused_computation.clone.1 | convolution fusion | flops 411041792 | bytes 8701956 | tf_op jit(solution)/shard_map/while/body/eval_jaxpr/fa,fh->ah/dot_general | solution.py:15
  178.1 6.5 %convolution_add_fusion.2 = f32[8,4096]{1,0:T(8,128)S(1)} fusion(f32[512,4096]{1,0:T(8,128)} %multiply_exponential_fusion.2, f32[8,4096]{1,0:T(8,128)S(1)} %get-tuple-element.282, pred[]{:T(512)S(6)} %compare.3, f32[8,8192]{1,0:T(8,128)S(1)} %get-tuple-element.297, s32[]{:T(128)S(6)} %select_n.16), kind=kOutput, calls=%fused_computation.1.clone.1 | convolution fusion | flops 201392128 | bytes 8667141 | tf_op jit(solution)/shard_map/while/body/eval_jaxpr/dot_general | solution.py:20
  184.6 7.2 %fusion.22 = f32[8,8192]{1,0:T(8,128)S(1)} fusion(f32[8,8192]{1,0:T(8,128)S(1)} %get-tuple-element.283, s32[]{:T(128)S(6)} %select_n.16, f32[512,4096]{1,0:T(8,128)S(1)} %copy-done, f32[8,4096]{1,0:T(8,128)S(1)} %copy-done.1), kind=kOutput, calls=%fused_computation.3.clone.1 | convolution fusion | flops 201326592 | bytes 8536068 | tf_op jit(solution)/shard_map/while/body/eval_jaxpr/dot_general | solution.py:20
  191.8 0.1 dynamic_slice.38
  191.9 10.2 %multiply_exponential_fusion.2 = f32[512,4096]{1,0:T(8,128)} fusion(f32[16,4096]{1,0:T(8,128)S(1)} %get-tuple-element.301, f32[4096]{0:T(1024)S(1)} %get-tuple-element.299, f32[512]{0:T(512)S(1)} %dynamic_slice.38, f32[16,8192]{1,0:T(8,128)S(1)} %get-tuple-element.300, s32[]{:T(128)S(6)} %select_n.16), kind=kOutput, calls=%fused_computation.clone.1 | convolution fusion | flops 411041792 | bytes 8701956 | tf_op jit(solution)/shard_map/while/body/eval_jaxpr/fa,fh->ah/dot_general | solution.py:15
  202.0 6.5 %convolution_add_fusion.2 = f32[8,4096]{1,0:T(8,128)S(1)} fusion(f32[512,4096]{1,0:T(8,128)} %multiply_exponential_fusion.2, f32[8,4096]{1,0:T(8,128)S(1)} %get-tuple-element.282, pred[]{:T(512)S(6)} %compare.3, f32[8,8192]{1,0:T(8,128)S(1)} %get-tuple-element.297, s32[]{:T(128)S(6)} %select_n.16), kind=kOutput, calls=%fused_computation.1.clone.1 | convolution fusion | flops 201392128 | bytes 8667141 | tf_op jit(solution)/shard_map/while/body/eval_jaxpr/dot_general | solution.py:20
  208.5 7.2 %fusion.22 = f32[8,8192]{1,0:T(8,128)S(1)} fusion(f32[8,8192]{1,0:T(8,128)S(1)} %get-tuple-element.283, s32[]{:T(128)S(6)} %select_n.16, f32[512,4096]{1,0:T(8,128)S(1)} %copy-done, f32[8,4096]{1,0:T(8,128)S(1)} %copy-done.1), kind=kOutput, calls=%fused_computation.3.clone.1 | convolution fusion | flops 201326592 | bytes 8536068 | tf_op jit(solution)/shard_map/while/body/eval_jaxpr/dot_general | solution.py:20
  215.7 0.1 dynamic_slice.38
  215.8 10.2 %multiply_exponential_fusion.2 = f32[512,4096]{1,0:T(8,128)} fusion(f32[16,4096]{1,0:T(8,128)S(1)} %get-tuple-element.301, f32[4096]{0:T(1024)S(1)} %get-tuple-element.299, f32[512]{0:T(512)S(1)} %dynamic_slice.38, f32[16,8192]{1,0:T(8,128)S(1)} %get-tuple-element.300, s32[]{:T(128)S(6)} %select_n.16), kind=kOutput, calls=%fused_computation.clone.1 | convolution fusion | flops 411041792 | bytes 8701956 | tf_op jit(solution)/shard_map/while/body/eval_jaxpr/fa,fh->ah/dot_general | solution.py:15
  226.0 6.5 %convolution_add_fusion.2 = f32[8,4096]{1,0:T(8,128)S(1)} fusion(f32[512,4096]{1,0:T(8,128)} %multiply_exponential_fusion.2, f32[8,4096]{1,0:T(8,128)S(1)} %get-tuple-element.282, pred[]{:T(512)S(6)} %compare.3, f32[8,8192]{1,0:T(8,128)S(1)} %get-tuple-element.297, s32[]{:T(128)S(6)} %select_n.16), kind=kOutput, calls=%fused_computation.1.clone.1 | convolution fusion | flops 201392128 | bytes 8667141 | tf_op jit(solution)/shard_map/while/body/eval_jaxpr/dot_general | solution.py:20
  232.5 7.2 %fusion.22 = f32[8,8192]{1,0:T(8,128)S(1)} fusion(f32[8,8192]{1,0:T(8,128)S(1)} %get-tuple-element.283, s32[]{:T(128)S(6)} %select_n.16, f32[512,4096]{1,0:T(8,128)S(1)} %copy-done, f32[8,4096]{1,0:T(8,128)S(1)} %copy-done.1), kind=kOutput, calls=%fused_computation.3.clone.1 | convolution fusion | flops 201326592 | bytes 8536068 | tf_op jit(solution)/shard_map/while/body/eval_jaxpr/dot_general | solution.py:20
  239.8 10.2 %multiply_exponential_fusion.2 = f32[512,4096]{1,0:T(8,128)} fusion(f32[16,4096]{1,0:T(8,128)S(1)} %get-tuple-element.301, f32[4096]{0:T(1024)S(1)} %get-tuple-element.299, f32[512]{0:T(512)S(1)} %dynamic_slice.38, f32[16,8192]{1,0:T(8,128)S(1)} %get-tuple-element.300, s32[]{:T(128)S(6)} %select_n.16), kind=kOutput, calls=%fused_computation.clone.1 | convolution fusion | flops 411041792 | bytes 8701956 | tf_op jit(solution)/shard_map/while/body/eval_jaxpr/fa,fh->ah/dot_general | solution.py:15
  249.9 6.5 %convolution_add_fusion.2 = f32[8,4096]{1,0:T(8,128)S(1)} fusion(f32[512,4096]{1,0:T(8,128)} %multiply_exponential_fusion.2, f32[8,4096]{1,0:T(8,128)S(1)} %get-tuple-element.282, pred[]{:T(512)S(6)} %compare.3, f32[8,8192]{1,0:T(8,128)S(1)} %get-tuple-element.297, s32[]{:T(128)S(6)} %select_n.16), kind=kOutput, calls=%fused_computation.1.clone.1 | convolution fusion | flops 201392128 | bytes 8667141 | tf_op jit(solution)/shard_map/while/body/eval_jaxpr/dot_general | solution.py:20
  256.4 7.2 %fusion.22 = f32[8,8192]{1,0:T(8,128)S(1)} fusion(f32[8,8192]{1,0:T(8,128)S(1)} %get-tuple-element.283, s32[]{:T(128)S(6)} %select_n.16, f32[512,4096]{1,0:T(8,128)S(1)} %copy-done, f32[8,4096]{1,0:T(8,128)S(1)} %copy-done.1), kind=kOutput, calls=%fused_computation.3.clone.1 | convolution fusion | flops 201326592 | bytes 8536068 | tf_op jit(solution)/shard_map/while/body/eval_jaxpr/dot_general | solution.py:20
  263.7 10.2 %multiply_exponential_fusion.2 = f32[512,4096]{1,0:T(8,128)} fusion(f32[16,4096]{1,0:T(8,128)S(1)} %get-tuple-element.301, f32[4096]{0:T(1024)S(1)} %get-tuple-element.299, f32[512]{0:T(512)S(1)} %dynamic_slice.38, f32[16,8192]{1,0:T(8,128)S(1)} %get-tuple-element.300, s32[]{:T(128)S(6)} %select_n.16), kind=kOutput, calls=%fused_computation.clone.1 | convolution fusion | flops 411041792 | bytes 8701956 | tf_op jit(solution)/shard_map/while/body/eval_jaxpr/fa,fh->ah/dot_general | solution.py:15
  273.9 6.5 %convolution_add_fusion.2 = f32[8,4096]{1,0:T(8,128)S(1)} fusion(f32[512,4096]{1,0:T(8,128)} %multiply_exponential_fusion.2, f32[8,4096]{1,0:T(8,128)S(1)} %get-tuple-element.282, pred[]{:T(512)S(6)} %compare.3, f32[8,8192]{1,0:T(8,128)S(1)} %get-tuple-element.297, s32[]{:T(128)S(6)} %select_n.16), kind=kOutput, calls=%fused_computation.1.clone.1 | convolution fusion | flops 201392128 | bytes 8667141 | tf_op jit(solution)/shard_map/while/body/eval_jaxpr/dot_general | solution.py:20
  280.4 7.2 %fusion.22 = f32[8,8192]{1,0:T(8,128)S(1)} fusion(f32[8,8192]{1,0:T(8,128)S(1)} %get-tuple-element.283, s32[]{:T(128)S(6)} %select_n.16, f32[512,4096]{1,0:T(8,128)S(1)} %copy-done, f32[8,4096]{1,0:T(8,128)S(1)} %copy-done.1), kind=kOutput, calls=%fused_computation.3.clone.1 | convolution fusion | flops 201326592 | bytes 8536068 | tf_op jit(solution)/shard_map/while/body/eval_jaxpr/dot_general | solution.py:20
  287.7 10.2 %multiply_exponential_fusion.2 = f32[512,4096]{1,0:T(8,128)} fusion(f32[16,4096]{1,0:T(8,128)S(1)} %get-tuple-element.301, f32[4096]{0:T(1024)S(1)} %get-tuple-element.299, f32[512]{0:T(512)S(1)} %dynamic_slice.38, f32[16,8192]{1,0:T(8,128)S(1)} %get-tuple-element.300, s32[]{:T(128)S(6)} %select_n.16), kind=kOutput, calls=%fused_computation.clone.1 | convolution fusion | flops 411041792 | bytes 8701956 | tf_op jit(solution)/shard_map/while/body/eval_jaxpr/fa,fh->ah/dot_general | solution.py:15
  297.9 6.5 %convolution_add_fusion.2 = f32[8,4096]{1,0:T(8,128)S(1)} fusion(f32[512,4096]{1,0:T(8,128)} %multiply_exponential_fusion.2, f32[8,4096]{1,0:T(8,128)S(1)} %get-tuple-element.282, pred[]{:T(512)S(6)} %compare.3, f32[8,8192]{1,0:T(8,128)S(1)} %get-tuple-element.297, s32[]{:T(128)S(6)} %select_n.16), kind=kOutput, calls=%fused_computation.1.clone.1 | convolution fusion | flops 201392128 | bytes 8667141 | tf_op jit(solution)/shard_map/while/body/eval_jaxpr/dot_general | solution.py:20
  304.4 7.2 %fusion.22 = f32[8,8192]{1,0:T(8,128)S(1)} fusion(f32[8,8192]{1,0:T(8,128)S(1)} %get-tuple-element.283, s32[]{:T(128)S(6)} %select_n.16, f32[512,4096]{1,0:T(8,128)S(1)} %copy-done, f32[8,4096]{1,0:T(8,128)S(1)} %copy-done.1), kind=kOutput, calls=%fused_computation.3.clone.1 | convolution fusion | flops 201326592 | bytes 8536068 | tf_op jit(solution)/shard_map/while/body/eval_jaxpr/dot_general | solution.py:20
  311.5 0.1 dynamic_slice.38
  311.6 10.2 %multiply_exponential_fusion.2 = f32[512,4096]{1,0:T(8,128)} fusion(f32[16,4096]{1,0:T(8,128)S(1)} %get-tuple-element.301, f32[4096]{0:T(1024)S(1)} %get-tuple-element.299, f32[512]{0:T(512)S(1)} %dynamic_slice.38, f32[16,8192]{1,0:T(8,128)S(1)} %get-tuple-element.300, s32[]{:T(128)S(6)} %select_n.16), kind=kOutput, calls=%fused_computation.clone.1 | convolution fusion | flops 411041792 | bytes 8701956 | tf_op jit(solution)/shard_map/while/body/eval_jaxpr/fa,fh->ah/dot_general | solution.py:15
  321.8 6.5 %convolution_add_fusion.2 = f32[8,4096]{1,0:T(8,128)S(1)} fusion(f32[512,4096]{1,0:T(8,128)} %multiply_exponential_fusion.2, f32[8,4096]{1,0:T(8,128)S(1)} %get-tuple-element.282, pred[]{:T(512)S(6)} %compare.3, f32[8,8192]{1,0:T(8,128)S(1)} %get-tuple-element.297, s32[]{:T(128)S(6)} %select_n.16), kind=kOutput, calls=%fused_computation.1.clone.1 | convolution fusion | flops 201392128 | bytes 8667141 | tf_op jit(solution)/shard_map/while/body/eval_jaxpr/dot_general | solution.py:20
  328.3 7.2 %fusion.22 = f32[8,8192]{1,0:T(8,128)S(1)} fusion(f32[8,8192]{1,0:T(8,128)S(1)} %get-tuple-element.283, s32[]{:T(128)S(6)} %select_n.16, f32[512,4096]{1,0:T(8,128)S(1)} %copy-done, f32[8,4096]{1,0:T(8,128)S(1)} %copy-done.1), kind=kOutput, calls=%fused_computation.3.clone.1 | convolution fusion | flops 201326592 | bytes 8536068 | tf_op jit(solution)/shard_map/while/body/eval_jaxpr/dot_general | solution.py:20
  335.5 0.1 dynamic_slice.38
  335.6 10.2 %multiply_exponential_fusion.2 = f32[512,4096]{1,0:T(8,128)} fusion(f32[16,4096]{1,0:T(8,128)S(1)} %get-tuple-element.301, f32[4096]{0:T(1024)S(1)} %get-tuple-element.299, f32[512]{0:T(512)S(1)} %dynamic_slice.38, f32[16,8192]{1,0:T(8,128)S(1)} %get-tuple-element.300, s32[]{:T(128)S(6)} %select_n.16), kind=kOutput, calls=%fused_computation.clone.1 | convolution fusion | flops 411041792 | bytes 8701956 | tf_op jit(solution)/shard_map/while/body/eval_jaxpr/fa,fh->ah/dot_general | solution.py:15
  345.8 6.5 %convolution_add_fusion.2 = f32[8,4096]{1,0:T(8,128)S(1)} fusion(f32[512,4096]{1,0:T(8,128)} %multiply_exponential_fusion.2, f32[8,4096]{1,0:T(8,128)S(1)} %get-tuple-element.282, pred[]{:T(512)S(6)} %compare.3, f32[8,8192]{1,0:T(8,128)S(1)} %get-tuple-element.297, s32[]{:T(128)S(6)} %select_n.16), kind=kOutput, calls=%fused_computation.1.clone.1 | convolution fusion | flops 201392128 | bytes 8667141 | tf_op jit(solution)/shard_map/while/body/eval_jaxpr/dot_general | solution.py:20
  352.3 7.2 %fusion.22 = f32[8,8192]{1,0:T(8,128)S(1)} fusion(f32[8,8192]{1,0:T(8,128)S(1)} %get-tuple-element.283, s32[]{:T(128)S(6)} %select_n.16, f32[512,4096]{1,0:T(8,128)S(1)} %copy-done, f32[8,4096]{1,0:T(8,128)S(1)} %copy-done.1), kind=kOutput, calls=%fused_computation.3.clone.1 | convolution fusion | flops 201326592 | bytes 8536068 | tf_op jit(solution)/shard_map/while/body/eval_jaxpr/dot_general | solution.py:20
  359.5 10.2 %multiply_exponential_fusion.2 = f32[512,4096]{1,0:T(8,128)} fusion(f32[16,4096]{1,0:T(8,128)S(1)} %get-tuple-element.301, f32[4096]{0:T(1024)S(1)} %get-tuple-element.299, f32[512]{0:T(512)S(1)} %dynamic_slice.38, f32[16,8192]{1,0:T(8,128)S(1)} %get-tuple-element.300, s32[]{:T(128)S(6)} %select_n.16), kind=kOutput, calls=%fused_computation.clone.1 | convolution fusion | flops 411041792 | bytes 8701956 | tf_op jit(solution)/shard_map/while/body/eval_jaxpr/fa,fh->ah/dot_general | solution.py:15
  369.7 6.5 %convolution_add_fusion.2 = f32[8,4096]{1,0:T(8,128)S(1)} fusion(f32[512,4096]{1,0:T(8,128)} %multiply_exponential_fusion.2, f32[8,4096]{1,0:T(8,128)S(1)} %get-tuple-element.282, pred[]{:T(512)S(6)} %compare.3, f32[8,8192]{1,0:T(8,128)S(1)} %get-tuple-element.297, s32[]{:T(128)S(6)} %select_n.16), kind=kOutput, calls=%fused_computation.1.clone.1 | convolution fusion | flops 201392128 | bytes 8667141 | tf_op jit(solution)/shard_map/while/body/eval_jaxpr/dot_general | solution.py:20
  376.2 7.2 %fusion.22 = f32[8,8192]{1,0:T(8,128)S(1)} fusion(f32[8,8192]{1,0:T(8,128)S(1)} %get-tuple-element.283, s32[]{:T(128)S(6)} %select_n.16, f32[512,4096]{1,0:T(8,128)S(1)} %copy-done, f32[8,4096]{1,0:T(8,128)S(1)} %copy-done.1), kind=kOutput, calls=%fused_computation.3.clone.1 | convolution fusion | flops 201326592 | bytes 8536068 | tf_op jit(solution)/shard_map/while/body/eval_jaxpr/dot_general | solution.py:20
  383.5 10.2 %multiply_exponential_fusion.2 = f32[512,4096]{1,0:T(8,128)} fusion(f32[16,4096]{1,0:T(8,128)S(1)} %get-tuple-element.301, f32[4096]{0:T(1024)S(1)} %get-tuple-element.299, f32[512]{0:T(512)S(1)} %dynamic_slice.38, f32[16,8192]{1,0:T(8,128)S(1)} %get-tuple-element.300, s32[]{:T(128)S(6)} %select_n.16), kind=kOutput, calls=%fused_computation.clone.1 | convolution fusion | flops 411041792 | bytes 8701956 | tf_op jit(solution)/shard_map/while/body/eval_jaxpr/fa,fh->ah/dot_general | solution.py:15
  393.7 6.5 %convolution_add_fusion.2 = f32[8,4096]{1,0:T(8,128)S(1)} fusion(f32[512,4096]{1,0:T(8,128)} %multiply_exponential_fusion.2, f32[8,4096]{1,0:T(8,128)S(1)} %get-tuple-element.282, pred[]{:T(512)S(6)} %compare.3, f32[8,8192]{1,0:T(8,128)S(1)} %get-tuple-element.297, s32[]{:T(128)S(6)} %select_n.16), kind=kOutput, calls=%fused_computation.1.clone.1 | convolution fusion | flops 201392128 | bytes 8667141 | tf_op jit(solution)/shard_map/while/body/eval_jaxpr/dot_general | solution.py:20
  400.2 7.2 %fusion.22 = f32[8,8192]{1,0:T(8,128)S(1)} fusion(f32[8,8192]{1,0:T(8,128)S(1)} %get-tuple-element.283, s32[]{:T(128)S(6)} %select_n.16, f32[512,4096]{1,0:T(8,128)S(1)} %copy-done, f32[8,4096]{1,0:T(8,128)S(1)} %copy-done.1), kind=kOutput, calls=%fused_computation.3.clone.1 | convolution fusion | flops 201326592 | bytes 8536068 | tf_op jit(solution)/shard_map/while/body/eval_jaxpr/dot_general | solution.py:20
  407.4 0.7 copy-done.2
  408.1 0.7 broadcast_multiply_fusion
  408.9 125.9 %all-reduce.2.cloned.1.call-done = f32[8,8192]{1,0:T(8,128)} async-done(((f32[8,8192]{1,0:T(8,128)}), f32[8,8192]{1,0:T(8,128)}) %all-reduce.2.cloned.1.call-update) | async-done | bytes 262160 | tf_op jit(solution)/shard_map/psum | solution.py:54
  534.7 1.5 dynamic-slice_multiply_fusion
  (81 shorter events, 1.0 us)
Async XLA Ops:
  7.2 527.6 %all-reduce.2.cloned.1.call-start = ((), (), s32[]{:S(2)}) async-start(), calls=%async_computation | async-start | bytes 524288 | tf_op jit(solution)/shard_map/psum | solution.py:54
  24.1 384.0 %copy-start.3 = (f32[8]{0:T(128)S(1)}, f32[8]{0:T(128)}, u32[]{:S(2)}) copy-start(f32[8]{0:T(128)} %param.13) | copy-start | bytes 100
  24.2 16.7 %copy-start.1 = (f32[8,4096]{1,0:T(8,128)S(1)}, f32[8,4096]{1,0:T(8,128)}, u32[]{:S(2)}) copy-start(f32[8,4096]{1,0:T(8,128)} %get-tuple-element.302) | copy-start | bytes 393220 | tf_op jit(solution)/shard_map/while
  34.4 6.5 %copy-start = (f32[512,4096]{1,0:T(8,128)S(1)}, f32[512,4096]{1,0:T(8,128)}, u32[]{:S(2)}) copy-start(f32[512,4096]{1,0:T(8,128)} %multiply_exponential_fusion.2) | copy-start | bytes 25165828 | tf_op jit(solution)/shard_map/while
  48.1 16.7 %copy-start.1 = (f32[8,4096]{1,0:T(8,128)S(1)}, f32[8,4096]{1,0:T(8,128)}, u32[]{:S(2)}) copy-start(f32[8,4096]{1,0:T(8,128)} %get-tuple-element.302) | copy-start | bytes 393220 | tf_op jit(solution)/shard_map/while
  58.3 6.5 %copy-start = (f32[512,4096]{1,0:T(8,128)S(1)}, f32[512,4096]{1,0:T(8,128)}, u32[]{:S(2)}) copy-start(f32[512,4096]{1,0:T(8,128)} %multiply_exponential_fusion.2) | copy-start | bytes 25165828 | tf_op jit(solution)/shard_map/while
  72.1 16.7 %copy-start.1 = (f32[8,4096]{1,0:T(8,128)S(1)}, f32[8,4096]{1,0:T(8,128)}, u32[]{:S(2)}) copy-start(f32[8,4096]{1,0:T(8,128)} %get-tuple-element.302) | copy-start | bytes 393220 | tf_op jit(solution)/shard_map/while
  82.3 6.5 %copy-start = (f32[512,4096]{1,0:T(8,128)S(1)}, f32[512,4096]{1,0:T(8,128)}, u32[]{:S(2)}) copy-start(f32[512,4096]{1,0:T(8,128)} %multiply_exponential_fusion.2) | copy-start | bytes 25165828 | tf_op jit(solution)/shard_map/while
  96.0 16.7 %copy-start.1 = (f32[8,4096]{1,0:T(8,128)S(1)}, f32[8,4096]{1,0:T(8,128)}, u32[]{:S(2)}) copy-start(f32[8,4096]{1,0:T(8,128)} %get-tuple-element.302) | copy-start | bytes 393220 | tf_op jit(solution)/shard_map/while
  106.2 6.5 %copy-start = (f32[512,4096]{1,0:T(8,128)S(1)}, f32[512,4096]{1,0:T(8,128)}, u32[]{:S(2)}) copy-start(f32[512,4096]{1,0:T(8,128)} %multiply_exponential_fusion.2) | copy-start | bytes 25165828 | tf_op jit(solution)/shard_map/while
  120.0 16.7 %copy-start.1 = (f32[8,4096]{1,0:T(8,128)S(1)}, f32[8,4096]{1,0:T(8,128)}, u32[]{:S(2)}) copy-start(f32[8,4096]{1,0:T(8,128)} %get-tuple-element.302) | copy-start | bytes 393220 | tf_op jit(solution)/shard_map/while
  130.2 6.5 %copy-start = (f32[512,4096]{1,0:T(8,128)S(1)}, f32[512,4096]{1,0:T(8,128)}, u32[]{:S(2)}) copy-start(f32[512,4096]{1,0:T(8,128)} %multiply_exponential_fusion.2) | copy-start | bytes 25165828 | tf_op jit(solution)/shard_map/while
  143.9 16.7 %copy-start.1 = (f32[8,4096]{1,0:T(8,128)S(1)}, f32[8,4096]{1,0:T(8,128)}, u32[]{:S(2)}) copy-start(f32[8,4096]{1,0:T(8,128)} %get-tuple-element.302) | copy-start | bytes 393220 | tf_op jit(solution)/shard_map/while
  154.1 6.5 %copy-start = (f32[512,4096]{1,0:T(8,128)S(1)}, f32[512,4096]{1,0:T(8,128)}, u32[]{:S(2)}) copy-start(f32[512,4096]{1,0:T(8,128)} %multiply_exponential_fusion.2) | copy-start | bytes 25165828 | tf_op jit(solution)/shard_map/while
  167.9 16.7 %copy-start.1 = (f32[8,4096]{1,0:T(8,128)S(1)}, f32[8,4096]{1,0:T(8,128)}, u32[]{:S(2)}) copy-start(f32[8,4096]{1,0:T(8,128)} %get-tuple-element.302) | copy-start | bytes 393220 | tf_op jit(solution)/shard_map/while
  178.1 6.5 %copy-start = (f32[512,4096]{1,0:T(8,128)S(1)}, f32[512,4096]{1,0:T(8,128)}, u32[]{:S(2)}) copy-start(f32[512,4096]{1,0:T(8,128)} %multiply_exponential_fusion.2) | copy-start | bytes 25165828 | tf_op jit(solution)/shard_map/while
  191.9 16.7 %copy-start.1 = (f32[8,4096]{1,0:T(8,128)S(1)}, f32[8,4096]{1,0:T(8,128)}, u32[]{:S(2)}) copy-start(f32[8,4096]{1,0:T(8,128)} %get-tuple-element.302) | copy-start | bytes 393220 | tf_op jit(solution)/shard_map/while
  202.0 6.5 %copy-start = (f32[512,4096]{1,0:T(8,128)S(1)}, f32[512,4096]{1,0:T(8,128)}, u32[]{:S(2)}) copy-start(f32[512,4096]{1,0:T(8,128)} %multiply_exponential_fusion.2) | copy-start | bytes 25165828 | tf_op jit(solution)/shard_map/while
  215.8 16.7 %copy-start.1 = (f32[8,4096]{1,0:T(8,128)S(1)}, f32[8,4096]{1,0:T(8,128)}, u32[]{:S(2)}) copy-start(f32[8,4096]{1,0:T(8,128)} %get-tuple-element.302) | copy-start | bytes 393220 | tf_op jit(solution)/shard_map/while
  226.0 6.5 %copy-start = (f32[512,4096]{1,0:T(8,128)S(1)}, f32[512,4096]{1,0:T(8,128)}, u32[]{:S(2)}) copy-start(f32[512,4096]{1,0:T(8,128)} %multiply_exponential_fusion.2) | copy-start | bytes 25165828 | tf_op jit(solution)/shard_map/while
  239.8 16.7 %copy-start.1 = (f32[8,4096]{1,0:T(8,128)S(1)}, f32[8,4096]{1,0:T(8,128)}, u32[]{:S(2)}) copy-start(f32[8,4096]{1,0:T(8,128)} %get-tuple-element.302) | copy-start | bytes 393220 | tf_op jit(solution)/shard_map/while
  249.9 6.5 %copy-start = (f32[512,4096]{1,0:T(8,128)S(1)}, f32[512,4096]{1,0:T(8,128)}, u32[]{:S(2)}) copy-start(f32[512,4096]{1,0:T(8,128)} %multiply_exponential_fusion.2) | copy-start | bytes 25165828 | tf_op jit(solution)/shard_map/while
  263.7 16.7 %copy-start.1 = (f32[8,4096]{1,0:T(8,128)S(1)}, f32[8,4096]{1,0:T(8,128)}, u32[]{:S(2)}) copy-start(f32[8,4096]{1,0:T(8,128)} %get-tuple-element.302) | copy-start | bytes 393220 | tf_op jit(solution)/shard_map/while
  273.9 6.5 %copy-start = (f32[512,4096]{1,0:T(8,128)S(1)}, f32[512,4096]{1,0:T(8,128)}, u32[]{:S(2)}) copy-start(f32[512,4096]{1,0:T(8,128)} %multiply_exponential_fusion.2) | copy-start | bytes 25165828 | tf_op jit(solution)/shard_map/while
  287.7 16.7 %copy-start.1 = (f32[8,4096]{1,0:T(8,128)S(1)}, f32[8,4096]{1,0:T(8,128)}, u32[]{:S(2)}) copy-start(f32[8,4096]{1,0:T(8,128)} %get-tuple-element.302) | copy-start | bytes 393220 | tf_op jit(solution)/shard_map/while
  297.9 6.5 %copy-start = (f32[512,4096]{1,0:T(8,128)S(1)}, f32[512,4096]{1,0:T(8,128)}, u32[]{:S(2)}) copy-start(f32[512,4096]{1,0:T(8,128)} %multiply_exponential_fusion.2) | copy-start | bytes 25165828 | tf_op jit(solution)/shard_map/while
  311.6 16.7 %copy-start.1 = (f32[8,4096]{1,0:T(8,128)S(1)}, f32[8,4096]{1,0:T(8,128)}, u32[]{:S(2)}) copy-start(f32[8,4096]{1,0:T(8,128)} %get-tuple-element.302) | copy-start | bytes 393220 | tf_op jit(solution)/shard_map/while
  321.8 6.5 %copy-start = (f32[512,4096]{1,0:T(8,128)S(1)}, f32[512,4096]{1,0:T(8,128)}, u32[]{:S(2)}) copy-start(f32[512,4096]{1,0:T(8,128)} %multiply_exponential_fusion.2) | copy-start | bytes 25165828 | tf_op jit(solution)/shard_map/while
  335.6 16.7 %copy-start.1 = (f32[8,4096]{1,0:T(8,128)S(1)}, f32[8,4096]{1,0:T(8,128)}, u32[]{:S(2)}) copy-start(f32[8,4096]{1,0:T(8,128)} %get-tuple-element.302) | copy-start | bytes 393220 | tf_op jit(solution)/shard_map/while
  345.8 6.5 %copy-start = (f32[512,4096]{1,0:T(8,128)S(1)}, f32[512,4096]{1,0:T(8,128)}, u32[]{:S(2)}) copy-start(f32[512,4096]{1,0:T(8,128)} %multiply_exponential_fusion.2) | copy-start | bytes 25165828 | tf_op jit(solution)/shard_map/while
  359.5 16.7 %copy-start.1 = (f32[8,4096]{1,0:T(8,128)S(1)}, f32[8,4096]{1,0:T(8,128)}, u32[]{:S(2)}) copy-start(f32[8,4096]{1,0:T(8,128)} %get-tuple-element.302) | copy-start | bytes 393220 | tf_op jit(solution)/shard_map/while
  369.7 6.5 %copy-start = (f32[512,4096]{1,0:T(8,128)S(1)}, f32[512,4096]{1,0:T(8,128)}, u32[]{:S(2)}) copy-start(f32[512,4096]{1,0:T(8,128)} %multiply_exponential_fusion.2) | copy-start | bytes 25165828 | tf_op jit(solution)/shard_map/while
  383.5 16.7 %copy-start.1 = (f32[8,4096]{1,0:T(8,128)S(1)}, f32[8,4096]{1,0:T(8,128)}, u32[]{:S(2)}) copy-start(f32[8,4096]{1,0:T(8,128)} %get-tuple-element.302) | copy-start | bytes 393220 | tf_op jit(solution)/shard_map/while
  393.7 6.5 %copy-start = (f32[512,4096]{1,0:T(8,128)S(1)}, f32[512,4096]{1,0:T(8,128)}, u32[]{:S(2)}) copy-start(f32[512,4096]{1,0:T(8,128)} %multiply_exponential_fusion.2) | copy-start | bytes 25165828 | tf_op jit(solution)/shard_map/while
  407.3 0.7 copy-start.2
Sparse Core Ops, SparseCore 0:
  408.2 126.4 all-reduce.1
where the time goes:
time: 543 us
  matrix products  382 us (70%)
  waiting for transfers between devices  126 us (23%)
  blocking collectives  14.9 us (3%)
  between operations  14.1 us (3%)
    dot_general x32, matrix products, product(): jnp.dot(left, right, precision=lax.Precision.HIGHEST, preferred_element_t...  219 us
    dot_general x16, matrix products, kernel_tile(): jnp.einsum('fa,fh->ah', left, right, precision=lax.Precision.HIGHEST)  163 us
    psum x1, waiting for transfers between devices, on_device(): totals = lax.psum(partial_sums, ('wide', 'narrow'))  126 us
  transfers between devices with their start and end apart: 1, of which 1 were waited for; matrix products, arithmetic and copies ran while one was open for 0% of the time, Pallas kernels for 0%

commit v1 on v0

v1 whole, which is shorter than its diff:
```python
import functools
import math

import jax
import jax.numpy as jnp
from jax import lax
from jax.experimental import pallas as pl
from jax.experimental.pallas import tpu as pltpu
from jax.sharding import PartitionSpec as P

F32 = jnp.float32
BF16 = jnp.bfloat16
DEPTH = 128
ROWS = 256
COLS = 256
AHEAD = 2


def round_bf16(x):
    return x.astype(BF16).astype(F32)


def split3(x):
    first = round_bf16(x)
    rest = x - first
    second = round_bf16(rest)
    return first, second, round_bf16(rest - second)


def scale_features(features, lengthscale):
    return features / lengthscale * math.sqrt(math.log2(math.e))


def norm_rows(scaled, own_first):
    norms = jnp.sum(scaled * scaled, axis=0, keepdims=True) * -0.5
    parts = split3(norms)
    row = lax.broadcasted_iota(jnp.int32, (16, scaled.shape[1]), 0)
    base = 0 if own_first else 3
    out = jnp.where(row < 6, 1.0, 0.0).astype(F32)
    for k, part in enumerate(parts):
        out = jnp.where(row == base + k, part, out)
    return out


def stack_anal(scaled):
    p1, p2, p3 = split3(scaled)
    zero = jnp.zeros((16, scaled.shape[1]), F32)
    return [p1, p1, p2, p2, p1, p3, norm_rows(scaled, True), zero]


def stack_hist(scaled):
    p1, p2, p3 = split3(scaled)
    zero = jnp.zeros((16, scaled.shape[1]), F32)
    return [p1, p2, p1, p2, p3, p1, norm_rows(scaled, False), zero]


def hi_lo(x):
    hi = x.astype(BF16)
    return hi, (x - hi.astype(F32)).astype(BF16)


def dot(left, right):
    return jnp.dot(left, right, preferred_element_type=F32)


def dot_nt(left, right):
    dims = (((1,), (1,)), ((), ()))
    return lax.dot_general(left, right, dims, preferred_element_type=F32)


def column(row):
    size = row.shape[1]
    at = lax.broadcasted_iota(jnp.int32, (size, size), 0)
    to = lax.broadcasted_iota(jnp.int32, (size, size), 1)
    return jnp.sum(jnp.where(at == to, row, 0.0), axis=1, keepdims=True)


def prep_kernel(fwd_scale, trans_scale, *refs):
    sources, (bst_ref, w_ref, own_ref) = refs[:6], refs[6:9]
    held, sems = refs[9:15], refs[15]
    copies = [
        pltpu.make_async_copy(source, target, sems.at[k])
        for k, (source, target) in enumerate(zip(sources, held))
    ]
    for copy in copies:
        copy.start()
    for copy in copies:
        copy.wait()
    hf_ref, hw_ref, af_ref, aw_ref, ls_ref, amp_ref = held
    hist = hf_ref.shape[1]
    lengthscale = column(ls_ref[...])
    amplitude = column(amp_ref[...])
    own_ref[0:16, :] = scale_features(af_ref[...], lengthscale)
    own_ref[16:24, :] = aw_ref[...] * (amplitude * trans_scale)
    for start in range(0, hist, COLS):
        cols = slice(start, start + COLS)
        stack = stack_hist(scale_features(hf_ref[:, cols], lengthscale))
        for k, rows in enumerate(stack):
            bst_ref[k * 16 : (k + 1) * 16, cols] = rows.astype(BF16)
        weights = hw_ref[:, cols] * (amplitude * fwd_scale)
        hi = round_bf16(weights)
        w_ref[:, cols] = jnp.concatenate([hi, weights - hi], axis=0).astype(BF16)


def tile_kernel(offset, length, want_fwd, want_trans, has_total, counts, *refs):
    refs = list(refs)
    pieces = [refs.pop(0) for _ in counts]
    bst_ref, w_ref = refs.pop(0), refs.pop(0)
    total_ref = refs.pop(0) if has_total else None
    fwd_refs = [refs.pop(0) for _ in counts] if want_fwd else []
    trans_ref = refs.pop(0) if want_trans else None
    anal_ref, left_refs, u_ref, tile_refs, fwd_ref, acc_ref = (
        refs[0],
        refs[1:3],
        refs[3],
        refs[4:6],
        refs[6],
        refs[7],
    )
    hist = bst_ref.shape[1]
    half = hist // 2
    blocks = length // ROWS

    for k, piece in enumerate(pieces):
        size = length // len(pieces)
        anal_ref[:, k * size : (k + 1) * size] = piece[:, offset : offset + size]
    if want_trans:
        u_hi, u_lo = hi_lo(anal_ref[16:24, :])
        u_ref[...] = jnp.concatenate([u_hi.astype(F32), u_lo.astype(F32)], axis=0).astype(BF16)
        acc_ref[...] = jnp.zeros_like(acc_ref)

    def rows_of(block):
        return pl.ds(pl.multiple_of(block * ROWS, ROWS), ROWS)

    def prep(block, slot):
        stack = jnp.concatenate(stack_anal(anal_ref[0:16, rows_of(block)]), axis=0)
        left_refs[slot][...] = stack.T.astype(BF16)

    def produce(slot, part, start):
        at = part * half + start
        exponent = dot(left_refs[slot][...], bst_ref[:, at : at + COLS])
        hi, lo = hi_lo(jnp.exp2(exponent))
        tile_refs[part][0:ROWS, start : start + COLS] = hi
        tile_refs[part][ROWS : 2 * ROWS, start : start + COLS] = lo

    def consume(part, start, u, fwd):
        tile = tile_refs[part][:, start : start + COLS]
        at = part * half + start
        if want_trans:
            acc_ref[:, at : at + COLS] += dot(u, tile)
        if want_fwd:
            fwd += dot_nt(w_ref[:, at : at + COLS], tile)
        return fwd

    def vectors(block):
        u = u_ref[:, rows_of(block)]
        return jnp.concatenate([u, u], axis=1)

    starts = range(0, half, COLS)
    made = [(0, 1), (1, 0), (1, 1), (0, 0)]
    makes = [(slot, part, start) for slot, part in made for start in starts]
    uses = [(k, part, start) for k in range(2) for part in range(2) for start in starts]

    prep(0, 0)
    for start in starts:
        produce(0, 0, start)

    @pl.loop(0, blocks // 2)
    def _(pair):
        block = pair * 2
        prep(block + 1, 1)
        us = [vectors(block), vectors(block + 1)]
        fwds = [jnp.zeros((16, 2 * ROWS), F32)] * 2
        for n in range(len(makes) + AHEAD):
            if n == len(makes) // 2:
                prep(jnp.minimum(block + 2, blocks - 1), 0)
            if n < len(makes):
                produce(*makes[n])
            if n >= AHEAD:
                k, part, start = uses[n - AHEAD]
                fwds[k] = consume(part, start, us[k], fwds[k])
        if want_fwd:
            for k, fwd in enumerate(fwds):
                flat = fwd[:, 0:ROWS] + fwd[:, ROWS : 2 * ROWS]
                fwd_ref[:, rows_of(block + k)] = flat[0:8] + flat[8:16]

    for k, ref in enumerate(fwd_refs):
        size = length // len(pieces)
        ref[...] = fwd_ref[:, k * size : (k + 1) * size]
    if want_trans:
        total = acc_ref[0:8, :] + acc_ref[8:16, :]
        trans_ref[...] = total + total_ref[...] if has_total else total


VMEM = pl.BlockSpec(memory_space=pltpu.VMEM)
PARAMS = pltpu.CompilerParams(vmem_limit_bytes=40 * 1024 * 1024)


def prepare(fwd_scale, trans_scale, *args):
    hist = args[0].shape[1]
    count = args[2].shape[1]
    return pl.pallas_call(
        functools.partial(prep_kernel, fwd_scale, trans_scale),
        out_shape=(
            jax.ShapeDtypeStruct((DEPTH, hist), BF16),
            jax.ShapeDtypeStruct((16, hist), BF16),
            jax.ShapeDtypeStruct((24, count), F32),
        ),
        in_specs=[pl.BlockSpec(memory_space=pltpu.HBM)] * 6,
        out_specs=(VMEM,) * 3,
        scratch_shapes=[pltpu.VMEM(arg.shape, F32) for arg in args]
        + [pltpu.SemaphoreType.DMA((6,))],
        compiler_params=PARAMS,
        name="prepare",
    )(*[pltpu.with_memory_space_constraint(arg, pltpu.HBM) for arg in args])


def tile_call(pieces, offset, length, total, bst, w, want_fwd=True, want_trans=True):
    hist = bst.shape[1]
    rows = length * len(pieces)
    kernel = functools.partial(
        tile_kernel, offset, rows, want_fwd, want_trans, total is not None, [length] * len(pieces)
    )
    args = [*pieces, bst, w]
    if total is not None:
        args.append(total)
    outs = []
    if want_fwd:
        outs += [jax.ShapeDtypeStruct((8, length), F32)] * len(pieces)
    if want_trans:
        outs.append(jax.ShapeDtypeStruct((8, hist), F32))
    out = pl.pallas_call(
        kernel,
        out_shape=tuple(outs),
        in_specs=[VMEM] * len(args),
        out_specs=(VMEM,) * len(outs),
        scratch_shapes=[
            pltpu.VMEM((24, rows), F32),
            pltpu.VMEM((ROWS, DEPTH), BF16),
            pltpu.VMEM((ROWS, DEPTH), BF16),
            pltpu.VMEM((16, rows), BF16),
            pltpu.VMEM((2 * ROWS, hist // 2), BF16),
            pltpu.VMEM((2 * ROWS, hist // 2), BF16),
            pltpu.VMEM((8, rows), F32),
            pltpu.VMEM((16, hist), F32),
        ],
        compiler_params=PARAMS,
        cost_estimate=pl.CostEstimate(
            flops=(1 + 2 * want_fwd + 2 * want_trans) * 2 * 256 * rows * hist,
            bytes_accessed=4 * 24 * rows + 4 * DEPTH * hist,
            transcendentals=rows * hist,
        ),
        name="covariance_tiles",
    )(*args)
    fwd = list(out[: len(pieces)]) if want_fwd else []
    return fwd, out[-1] if want_trans else total


def exchange(x, axis, distance):
    size = lax.axis_size(axis)
    return lax.ppermute(x, axis, [(k, k ^ distance) for k in range(size)])


def on_device(hist_features, hist_weights, anal_features, anal_weights, lengthscale, amplitude):
    hist = hist_features.shape[1]
    count = anal_features.shape[1]
    narrow = lax.axis_size("narrow")
    wide = lax.axis_size("wide")
    fwd_scale = 1.0 / math.sqrt(hist * wide * narrow)
    trans_scale = 1.0 / math.sqrt(count * narrow)
    bst, w, own = prepare(
        fwd_scale,
        trans_scale,
        hist_features,
        hist_weights,
        anal_features,
        anal_weights,
        lengthscale[None, :],
        amplitude[None, :],
    )
    pieces = [exchange(own, "narrow", k) for k in range(1, narrow)]
    call = functools.partial(tile_call, bst=bst, w=w)
    first = count // 2
    fwd_a, total = call([own], 0, first, None)
    others, total = call(pieces, 0, count, total)
    received = [exchange(fwd, "narrow", k + 1) for k, fwd in enumerate(others)]
    fwd_b, hist_out = call([own], first, count - first, total)
    forward = jnp.concatenate(fwd_a + fwd_b, axis=1)
    for term in received:
        forward = forward + term
    distance = 1
    while distance < wide:
        forward = forward + exchange(forward, "wide", distance)
        distance *= 2
    return forward, hist_out


def solution(mesh):
    in_specs = (
        P(None, ("wide", "narrow")),
        P(None, ("wide", "narrow")),
        P(None, "narrow"),
        P(None, "narrow"),
        P(),
        P(),
    )
    out_specs = (P(None, "narrow"), P(None, ("wide", "narrow")))
    return jax.shard_map(
        on_device, mesh=mesh, in_specs=in_specs, out_specs=out_specs, check_vma=False
    )
```

time: 543 us -> 93 us (0.17)
  matrix products: 382 us -> 0 us
  waiting for transfers between devices: 126 us -> 7.45 us
  Pallas kernels: 0 us -> 72 us
  blocking collectives: 14.9 us -> 0 us
  between operations: 14.1 us -> 0.7 us
  starting transfers between devices: 0.04 us -> 12 us
    dot_general x48 -> x0, matrix products: 382 us -> none  [the longest x32 219 us: product(): jnp.dot(left, right, precision=lax.Precision.HIGHEST, preferred_element_t...]
    psum x1 -> x0, waiting for transfers between devices: 126 us -> none  [on_device(): totals = lax.psum(partial_sums, ('wide', 'narrow'))]
    pallas_call x0 -> x4, Pallas kernels: none -> 72 us  [the longest x3 70.6 us: tile_call(): pl.pallas_call(kernel, out_shape=tuple(outs), in_specs=[VMEM] * len(args)...]
    all_gather x2 -> x0, blocking collectives: 14.9 us -> none  [the longest x1 7.49 us: on_device(): piece_features = lax.all_gather(anal_features, 'narrow', axis=1, tiled=True)]
    ppermute x0 -> x9, starting transfers between devices: none -> 12 us  [exchange(): return lax.ppermute(x, axis, [(k, k ^ distance) for k in range(size)])]
    ppermute x0 -> x9, waiting for transfers between devices: none -> 7.45 us  [exchange(): return lax.ppermute(x, axis, [(k, k ^ distance) for k in range(size)])]
  transfers between devices with their start and end apart: 1 -> 9, of which waited for: 1 -> 3; matrix products, arithmetic and copies ran while one was open for 0% -> 0% of each run, Pallas kernels for 0% -> 21%
where the time goes in v1:
time: 93 us; the launch traced here: 92.9 us
  Pallas kernels  72 us (77%)
  starting transfers between devices  12 us (13%)
  waiting for transfers between devices  7.45 us (8%)
    pallas_call x3, Pallas kernels, tile_call(): pl.pallas_call(kernel, out_shape=tuple(outs), in_specs=[VMEM] * len(args)...  70.6 us
    ppermute x9, starting transfers between devices, exchange(): return lax.ppermute(x, axis, [(k, k ^ distance) for k in range(size)])  12 us
    ppermute x9, waiting for transfers between devices, exchange(): return lax.ppermute(x, axis, [(k, k ^ distance) for k in range(size)])  7.45 us
  transfers between devices with their start and end apart: 9, of which 3 were waited for; matrix products, arithmetic and copies ran while one was open for 0% of the time, Pallas kernels for 21%

profile of v1, /device:TPU:0, one launch (start us, length us, event | category | flops | bytes accessed | tf_op | source)
XLA Modules:
  0.0 92.9 jit_solution(9511638680958435821)
XLA Ops:
  0.6 1.4 %prepare.1 = (bf16[128,4096]{1,0:T(8,128)(2,1)S(1)}, bf16[16,4096]{1,0:T(8,128)(2,1)S(1)}, f32[24,2048]{1,0:T(8,128)S(1)}) custom-call(f32[16,4096]{1,0:T(8,128)} %refs_0_.1, f32[8,4096]{1,0:T(8,128)} %refs_1_.1, f32[16,2048]{1,0:T(8,128)} %refs_2_.1, f32[8,2048]{1,0:T(8,128)} %refs_3_.1, f32[1,16]{1,0:T(1,128)} %bitcast.2, f32[1,8]{1,0:T(1,128)} %bitcast.3), custom_call_target="tpu_custom_call" | custom-call | tf_op jit(solution)/shard_map/prepare/pallas_call | solution.py:202
  2.0 2.4 %collective-permute-start.2 = (f32[24,2048]{1,0:T(8,128)S(1)}, f32[24,2048]{1,0:T(8,128)S(1)}, u32[]{:S(2)}, u32[]{:S(2)}) collective-permute-start(f32[24,2048]{1,0:T(8,128)S(1)} %get-tuple-element.13.refs_0_), channel_id=1, source_target_pairs={{0,3},{1,2},{2,1},{3,0},{4,7},{5,6},{6,5},{7,4},{8,11},{9,10},{10,... | collective-permute-start | bytes 589832 | tf_op jit(solution)/shard_map/ppermute | solution.py:261
  4.5 0.6 collective-permute-start.1
  5.1 0.0 collective-permute-start
  5.2 9.1 %covariance_tiles.3 = (f32[8,1024]{1,0:T(8,128)S(1)}, f32[8,4096]{1,0:T(8,128)S(1)}) custom-call(f32[24,2048]{1,0:T(8,128)S(1)} %get-tuple-element.13.refs_0_, bf16[128,4096]{1,0:T(8,128)(2,1)S(1)} %get-tuple-element.14.refs_1_.refs_3_, bf16[16,4096]{1,0:T(8,128)(2,1)S(1)} %get-tuple-element.15.refs_2_.refs_4_), custom_call_target="tpu_custom_call" | custom-call | flops 10737418240 | bytes 2195456 | tf_op jit(solution)/shard_map/covariance_tiles/pallas_call | solution.py:232
  14.3 0.0 collective-permute-done.2.refs_2_
  14.3 0.0 collective-permute-done.1.refs_1_
  14.3 0.0 collective-permute-done.refs_0_
  14.3 51.6 %covariance_tiles.4 = (f32[8,2048]{1,0:T(8,128)S(1)}, f32[8,2048]{1,0:T(8,128)S(1)}, f32[8,2048]{1,0:T(8,128)S(1)}, f32[8,4096]{1,0:T(8,128)S(1)}) custom-call(f32[24,2048]{1,0:T(8,128)S(1)} %collective-permute-done.refs_0_, f32[24,2048]{1,0:T(8,128)S(1)} %collective-permute-done.1.refs_1_, f32[24,2048]{1,0:T(8,128)S(1)} %collective-permute-done.2.refs_2_, ...), custom_call_target="tpu_custom_call" | custom-call | flops 64424509440 | bytes 2686976 | tf_op jit(solution)/shard_map/covariance_tiles/pallas_call | solution.py:232
  65.9 0.5 collective-permute-start.3
  66.4 1.8 %collective-permute-start.4 = (f32[8,2048]{1,0:T(8,128)S(1)}, f32[8,2048]{1,0:T(8,128)S(1)}, u32[]{:S(2)}, u32[]{:S(2)}) collective-permute-start(f32[8,2048]{1,0:T(8,128)S(1)} %get-tuple-element.21), channel_id=1, source_target_pairs={{0,2},{1,3},{2,0},{3,1},{4,6},{5,7},{6,4},{7,5},{8,10},{9,11},{10,... | collective-permute-start | bytes 196616 | tf_op jit(solution)/shard_map/ppermute | solution.py:261
  68.2 0.1 collective-permute-start.5
  68.2 10.0 %covariance_tiles.5 = (f32[8,1024]{1,0:T(8,128)S(1)}, f32[8,4096]{1,0:T(8,128)}) custom-call(f32[24,2048]{1,0:T(8,128)S(1)} %get-tuple-element.13.refs_0_, bf16[128,4096]{1,0:T(8,128)(2,1)S(1)} %get-tuple-element.14.refs_1_.refs_3_, bf16[16,4096]{1,0:T(8,128)(2,1)S(1)} %get-tuple-element.15.refs_2_.refs_4_, f32[8,4096]{1,0:T(8,128)S(1)} %get-tuple-element.18.refs_3_), custom_call_target="tpu_custom_call" | custom-call | flops 10737418240 | bytes 2195456 | tf_op jit(solution)/shard_map/covariance_tiles/pallas_call | solution.py:232
  78.2 0.0 collective-permute-done.3
  78.2 0.0 collective-permute-done.4
  78.2 0.0 collective-permute-done.5
  78.2 1.8 %collective-permute-start.6 = (f32[8,2048]{1,0:T(8,128)S(1)}, f32[8,2048]{1,0:T(8,128)S(1)}, u32[]{:S(2)}, u32[]{:S(2)}) collective-permute-start(f32[8,2048]{1,0:T(8,128)S(1)} %fusion.1), channel_id=1, source_target_pairs={{0,4},{4,0},{8,12},{12,8},{16,20},{20,16},{24,28},{28,24},{1,5},{5... | collective-permute-start | bytes 196616 | tf_op jit(solution)/shard_map/ppermute | solution.py:261
  80.1 2.6 %collective-permute-done.6 = f32[8,2048]{1,0:T(8,128)S(1)} collective-permute-done((f32[8,2048]{1,0:T(8,128)S(1)}, f32[8,2048]{1,0:T(8,128)S(1)}, u32[]{:S(2)}, u32[]{:S(2)}) %collective-permute-start.6) | collective-permute-done | bytes 65568 | tf_op jit(solution)/shard_map/ppermute | solution.py:261
  82.7 1.9 %collective-permute-start.7 = (f32[8,2048]{1,0:T(8,128)S(1)}, f32[8,2048]{1,0:T(8,128)S(1)}, u32[]{:S(2)}, u32[]{:S(2)}) collective-permute-start(f32[8,2048]{1,0:T(8,128)S(1)} %add.21), channel_id=1, source_target_pairs={{0,8},{4,12},{8,0},{12,4},{16,24},{20,28},{24,16},{28,20},{1,9},{5... | collective-permute-start | bytes 196616 | tf_op jit(solution)/shard_map/ppermute | solution.py:261
  84.5 2.5 %collective-permute-done.7 = f32[8,2048]{1,0:T(8,128)S(1)} collective-permute-done((f32[8,2048]{1,0:T(8,128)S(1)}, f32[8,2048]{1,0:T(8,128)S(1)}, u32[]{:S(2)}, u32[]{:S(2)}) %collective-permute-start.7) | collective-permute-done | bytes 65568 | tf_op jit(solution)/shard_map/ppermute | solution.py:261
  87.0 2.9 %collective-permute-start.8 = (f32[8,2048]{1,0:T(8,128)S(1)}, f32[8,2048]{1,0:T(8,128)S(1)}, u32[]{:S(2)}, u32[]{:S(2)}) collective-permute-start(f32[8,2048]{1,0:T(8,128)S(1)} %add.22), channel_id=1, source_target_pairs={{0,16},{4,20},{8,24},{12,28},{16,0},{20,4},{24,8},{28,12},{1,17},{... | collective-permute-start | bytes 196616 | tf_op jit(solution)/shard_map/ppermute | solution.py:261
  89.9 2.4 %collective-permute-done.8 = f32[8,2048]{1,0:T(8,128)S(1)} collective-permute-done((f32[8,2048]{1,0:T(8,128)S(1)}, f32[8,2048]{1,0:T(8,128)S(1)}, u32[]{:S(2)}, u32[]{:S(2)}) %collective-permute-start.8) | collective-permute-done | bytes 65568 | tf_op jit(solution)/shard_map/ppermute | solution.py:261
  92.2 0.6 add.23
  (3 shorter events, 0.0 us)
Async XLA Ops:
  2.0 12.2 %collective-permute-start.2 = (f32[24,2048]{1,0:T(8,128)S(1)}, f32[24,2048]{1,0:T(8,128)S(1)}, u32[]{:S(2)}, u32[]{:S(2)}) collective-permute-start(f32[24,2048]{1,0:T(8,128)S(1)} %get-tuple-element.13.refs_0_), channel_id=1, source_target_pairs={{0,3},{1,2},{2,1},{3,0},{4,7},{5,6},{6,5},{7,4},{8,11},{9,10},{10,... | collective-permute-start | bytes 589832 | tf_op jit(solution)/shard_map/ppermute | solution.py:261
  4.5 9.8 %collective-permute-start.1 = (f32[24,2048]{1,0:T(8,128)S(1)}, f32[24,2048]{1,0:T(8,128)S(1)}, u32[]{:S(2)}, u32[]{:S(2)}) collective-permute-start(f32[24,2048]{1,0:T(8,128)S(1)} %get-tuple-element.13.refs_0_), channel_id=1, source_target_pairs={{0,2},{1,3},{2,0},{3,1},{4,6},{5,7},{6,4},{7,5},{8,10},{9,11},{10,... | collective-permute-start | bytes 589832 | tf_op jit(solution)/shard_map/ppermute | solution.py:261
  5.1 9.2 %collective-permute-start = (f32[24,2048]{1,0:T(8,128)S(1)}, f32[24,2048]{1,0:T(8,128)S(1)}, u32[]{:S(2)}, u32[]{:S(2)}) collective-permute-start(f32[24,2048]{1,0:T(8,128)S(1)} %get-tuple-element.13.refs_0_), channel_id=1, source_target_pairs={{0,1},{1,0},{2,3},{3,2},{4,5},{5,4},{6,7},{7,6},{8,9},{9,8},{10,11... | collective-permute-start | bytes 589832 | tf_op jit(solution)/shard_map/ppermute | solution.py:261
  65.9 12.3 %collective-permute-start.3 = (f32[8,2048]{1,0:T(8,128)S(1)}, f32[8,2048]{1,0:T(8,128)S(1)}, u32[]{:S(2)}, u32[]{:S(2)}) collective-permute-start(f32[8,2048]{1,0:T(8,128)S(1)} %get-tuple-element.20), channel_id=1, source_target_pairs={{0,1},{1,0},{2,3},{3,2},{4,5},{5,4},{6,7},{7,6},{8,9},{9,8},{10,11... | collective-permute-start | bytes 196616 | tf_op jit(solution)/shard_map/ppermute | solution.py:261
  66.4 11.8 %collective-permute-start.4 = (f32[8,2048]{1,0:T(8,128)S(1)}, f32[8,2048]{1,0:T(8,128)S(1)}, u32[]{:S(2)}, u32[]{:S(2)}) collective-permute-start(f32[8,2048]{1,0:T(8,128)S(1)} %get-tuple-element.21), channel_id=1, source_target_pairs={{0,2},{1,3},{2,0},{3,1},{4,6},{5,7},{6,4},{7,5},{8,10},{9,11},{10,... | collective-permute-start | bytes 196616 | tf_op jit(solution)/shard_map/ppermute | solution.py:261
  68.2 10.0 %collective-permute-start.5 = (f32[8,2048]{1,0:T(8,128)S(1)}, f32[8,2048]{1,0:T(8,128)S(1)}, u32[]{:S(2)}, u32[]{:S(2)}) collective-permute-start(f32[8,2048]{1,0:T(8,128)S(1)} %get-tuple-element.22), channel_id=1, source_target_pairs={{0,3},{1,2},{2,1},{3,0},{4,7},{5,6},{6,5},{7,4},{8,11},{9,10},{10,... | collective-permute-start | bytes 196616 | tf_op jit(solution)/shard_map/ppermute | solution.py:261
  78.2 4.4 %collective-permute-start.6 = (f32[8,2048]{1,0:T(8,128)S(1)}, f32[8,2048]{1,0:T(8,128)S(1)}, u32[]{:S(2)}, u32[]{:S(2)}) collective-permute-start(f32[8,2048]{1,0:T(8,128)S(1)} %fusion.1), channel_id=1, source_target_pairs={{0,4},{4,0},{8,12},{12,8},{16,20},{20,16},{24,28},{28,24},{1,5},{5... | collective-permute-start | bytes 196616 | tf_op jit(solution)/shard_map/ppermute | solution.py:261
  82.7 4.3 %collective-permute-start.7 = (f32[8,2048]{1,0:T(8,128)S(1)}, f32[8,2048]{1,0:T(8,128)S(1)}, u32[]{:S(2)}, u32[]{:S(2)}) collective-permute-start(f32[8,2048]{1,0:T(8,128)S(1)} %add.21), channel_id=1, source_target_pairs={{0,8},{4,12},{8,0},{12,4},{16,24},{20,28},{24,16},{28,20},{1,9},{5... | collective-permute-start | bytes 196616 | tf_op jit(solution)/shard_map/ppermute | solution.py:261
  87.0 5.2 %collective-permute-start.8 = (f32[8,2048]{1,0:T(8,128)S(1)}, f32[8,2048]{1,0:T(8,128)S(1)}, u32[]{:S(2)}, u32[]{:S(2)}) collective-permute-start(f32[8,2048]{1,0:T(8,128)S(1)} %add.22), channel_id=1, source_target_pairs={{0,16},{4,20},{8,24},{12,28},{16,0},{20,4},{24,8},{28,12},{1,17},{... | collective-permute-start | bytes 196616 | tf_op jit(solution)/shard_map/ppermute | solution.py:261

commit v2 on v1

--- a/solution.py
+++ b/solution.py
@@ -28,7 +28,7 @@
 
 
 def scale_features(features, lengthscale):
-    return features / lengthscale * math.sqrt(math.log2(math.e))
+    return features / lengthscale
 
 
 def norm_rows(scaled, own_first):
@@ -139,7 +139,7 @@
     def produce(slot, part, start):
         at = part * half + start
         exponent = dot(left_refs[slot][...], bst_ref[:, at : at + COLS])
-        hi, lo = hi_lo(jnp.exp2(exponent))
+        hi, lo = hi_lo(jnp.exp(exponent))
         tile_refs[part][0:ROWS, start : start + COLS] = hi
         tile_refs[part][ROWS : 2 * ROWS, start : start + COLS] = lo
 
@@ -290,8 +290,11 @@
         forward = forward + term
     distance = 1
     while distance < wide:
-        forward = forward + exchange(forward, "wide", distance)
-        distance *= 2
+        steps = [k * distance for k in range(1, min(4, wide // distance))]
+        arrived = [exchange(forward, "wide", step) for step in steps]
+        for term in arrived:
+            forward = forward + term
+        distance *= 4
     return forward, hist_out
 
 

time: 93 us -> 91.8 us (0.987)
    ppermute x9 -> x10, waiting for transfers between devices: 7.45 us -> 6.57 us  [exchange(): return lax.ppermute(x, axis, [(k, k ^ distance) for k in range(size)])]
    ppermute x9 -> x10, starting transfers between devices: 12 us -> 11.7 us  [exchange(): return lax.ppermute(x, axis, [(k, k ^ distance) for k in range(size)])]
  transfers between devices with their start and end apart: 9 -> 10, of which waited for: 3 -> 4; matrix products, arithmetic and copies ran while one was open for 0% -> 0% of each run, Pallas kernels for 21% -> 21%
where the time goes in v2:
time: 91.8 us; the launch traced here: 91.7 us
  Pallas kernels  72.1 us (79%)
  starting transfers between devices  11.7 us (13%)
  waiting for transfers between devices  6.57 us (7%)
    pallas_call x3, Pallas kernels, tile_call(): pl.pallas_call(kernel, out_shape=tuple(outs), in_specs=[VMEM] * len(args)...  70.7 us
    ppermute x10, starting transfers between devices, exchange(): return lax.ppermute(x, axis, [(k, k ^ distance) for k in range(size)])  11.7 us
    ppermute x10, waiting for transfers between devices, exchange(): return lax.ppermute(x, axis, [(k, k ^ distance) for k in range(size)])  6.57 us
  transfers between devices with their start and end apart: 10, of which 4 were waited for; matrix products, arithmetic and copies ran while one was open for 0% of the time, Pallas kernels for 21%

profile of v2, /device:TPU:0, one launch (start us, length us, event | category | flops | bytes accessed | tf_op | source)
XLA Modules:
  0.0 91.7 jit_solution(5672513963199036384)
XLA Ops:
  0.6 1.4 %prepare.1 = (bf16[128,4096]{1,0:T(8,128)(2,1)S(1)}, bf16[16,4096]{1,0:T(8,128)(2,1)S(1)}, f32[24,2048]{1,0:T(8,128)S(1)}) custom-call(f32[16,4096]{1,0:T(8,128)} %refs_0_.1, f32[8,4096]{1,0:T(8,128)} %refs_1_.1, f32[16,2048]{1,0:T(8,128)} %refs_2_.1, f32[8,2048]{1,0:T(8,128)} %refs_3_.1, f32[1,16]{1,0:T(1,128)} %bitcast.2, f32[1,8]{1,0:T(1,128)} %bitcast.3), custom_call_target="tpu_custom_call" | custom-call | tf_op jit(solution)/shard_map/prepare/pallas_call | solution.py:202
  2.0 2.4 %collective-permute-start.2 = (f32[24,2048]{1,0:T(8,128)S(1)}, f32[24,2048]{1,0:T(8,128)S(1)}, u32[]{:S(2)}, u32[]{:S(2)}) collective-permute-start(f32[24,2048]{1,0:T(8,128)S(1)} %get-tuple-element.13.refs_0_), channel_id=1, source_target_pairs={{0,3},{1,2},{2,1},{3,0},{4,7},{5,6},{6,5},{7,4},{8,11},{9,10},{10,... | collective-permute-start | bytes 589832 | tf_op jit(solution)/shard_map/ppermute | solution.py:261
  4.5 0.6 collective-permute-start.1
  5.1 0.0 collective-permute-start
  5.1 9.2 %covariance_tiles.3 = (f32[8,1024]{1,0:T(8,128)S(1)}, f32[8,4096]{1,0:T(8,128)S(1)}) custom-call(f32[24,2048]{1,0:T(8,128)S(1)} %get-tuple-element.13.refs_0_, bf16[128,4096]{1,0:T(8,128)(2,1)S(1)} %get-tuple-element.14.refs_1_.refs_3_, bf16[16,4096]{1,0:T(8,128)(2,1)S(1)} %get-tuple-element.15.refs_2_.refs_4_), custom_call_target="tpu_custom_call" | custom-call | flops 10737418240 | bytes 2195456 | tf_op jit(solution)/shard_map/covariance_tiles/pallas_call | solution.py:232
  14.3 0.0 collective-permute-done.2.refs_2_
  14.3 0.0 collective-permute-done.1.refs_1_
  14.3 0.0 collective-permute-done.refs_0_
  14.3 51.6 %covariance_tiles.4 = (f32[8,2048]{1,0:T(8,128)S(1)}, f32[8,2048]{1,0:T(8,128)S(1)}, f32[8,2048]{1,0:T(8,128)S(1)}, f32[8,4096]{1,0:T(8,128)S(1)}) custom-call(f32[24,2048]{1,0:T(8,128)S(1)} %collective-permute-done.refs_0_, f32[24,2048]{1,0:T(8,128)S(1)} %collective-permute-done.1.refs_1_, f32[24,2048]{1,0:T(8,128)S(1)} %collective-permute-done.2.refs_2_, ...), custom_call_target="tpu_custom_call" | custom-call | flops 64424509440 | bytes 2686976 | tf_op jit(solution)/shard_map/covariance_tiles/pallas_call | solution.py:232
  65.9 0.5 collective-permute-start.3
  66.4 1.7 %collective-permute-start.4 = (f32[8,2048]{1,0:T(8,128)S(1)}, f32[8,2048]{1,0:T(8,128)S(1)}, u32[]{:S(2)}, u32[]{:S(2)}) collective-permute-start(f32[8,2048]{1,0:T(8,128)S(1)} %get-tuple-element.21), channel_id=1, source_target_pairs={{0,2},{1,3},{2,0},{3,1},{4,6},{5,7},{6,4},{7,5},{8,10},{9,11},{10,... | collective-permute-start | bytes 196616 | tf_op jit(solution)/shard_map/ppermute | solution.py:261
  68.2 0.1 collective-permute-start.5
  68.2 10.0 %covariance_tiles.5 = (f32[8,1024]{1,0:T(8,128)S(1)}, f32[8,4096]{1,0:T(8,128)}) custom-call(f32[24,2048]{1,0:T(8,128)S(1)} %get-tuple-element.13.refs_0_, bf16[128,4096]{1,0:T(8,128)(2,1)S(1)} %get-tuple-element.14.refs_1_.refs_3_, bf16[16,4096]{1,0:T(8,128)(2,1)S(1)} %get-tuple-element.15.refs_2_.refs_4_, f32[8,4096]{1,0:T(8,128)S(1)} %get-tuple-element.18.refs_3_), custom_call_target="tpu_custom_call" | custom-call | flops 10737418240 | bytes 2195456 | tf_op jit(solution)/shard_map/covariance_tiles/pallas_call | solution.py:232
  78.2 0.0 collective-permute-done.3
  78.2 0.0 collective-permute-done.4
  78.2 0.0 collective-permute-done.5
  78.3 2.8 %collective-permute-start.8 = (f32[8,2048]{1,0:T(8,128)S(1)}, f32[8,2048]{1,0:T(8,128)S(1)}, u32[]{:S(2)}, u32[]{:S(2)}) collective-permute-start(f32[8,2048]{1,0:T(8,128)S(1)} %fusion.1), channel_id=1, source_target_pairs={{0,12},{4,8},{8,4},{12,0},{16,28},{20,24},{24,20},{28,16},{1,13},{... | collective-permute-start | bytes 196616 | tf_op jit(solution)/shard_map/ppermute | solution.py:261
  81.1 0.4 collective-permute-start.7
  81.5 0.3 collective-permute-start.6
  81.8 1.9 %collective-permute-done.8 = f32[8,2048]{1,0:T(8,128)S(1)} collective-permute-done((f32[8,2048]{1,0:T(8,128)S(1)}, f32[8,2048]{1,0:T(8,128)S(1)}, u32[]{:S(2)}, u32[]{:S(2)}) %collective-permute-start.8) | collective-permute-done | bytes 65568 | tf_op jit(solution)/shard_map/ppermute | solution.py:261
  83.7 1.7 %collective-permute-done.7 = f32[8,2048]{1,0:T(8,128)S(1)} collective-permute-done((f32[8,2048]{1,0:T(8,128)S(1)}, f32[8,2048]{1,0:T(8,128)S(1)}, u32[]{:S(2)}, u32[]{:S(2)}) %collective-permute-start.7) | collective-permute-done | bytes 65568 | tf_op jit(solution)/shard_map/ppermute | solution.py:261
  85.4 0.4 collective-permute-done.6
  85.8 2.7 %collective-permute-start.9 = (f32[8,2048]{1,0:T(8,128)S(1)}, f32[8,2048]{1,0:T(8,128)S(1)}, u32[]{:S(2)}, u32[]{:S(2)}) collective-permute-start(f32[8,2048]{1,0:T(8,128)S(1)} %add_add_fusion), channel_id=1, source_target_pairs={{0,16},{4,20},{8,24},{12,28},{16,0},{20,4},{24,8},{28,12},{1,17},{... | collective-permute-start | bytes 196616 | tf_op jit(solution)/shard_map/ppermute | solution.py:261
  88.5 2.6 %collective-permute-done.9 = f32[8,2048]{1,0:T(8,128)S(1)} collective-permute-done((f32[8,2048]{1,0:T(8,128)S(1)}, f32[8,2048]{1,0:T(8,128)S(1)}, u32[]{:S(2)}, u32[]{:S(2)}) %collective-permute-start.9) | collective-permute-done | bytes 65568 | tf_op jit(solution)/shard_map/ppermute | solution.py:261
  91.1 0.6 add.27
  (2 shorter events, 0.0 us)
Async XLA Ops:
  2.0 12.3 %collective-permute-start.2 = (f32[24,2048]{1,0:T(8,128)S(1)}, f32[24,2048]{1,0:T(8,128)S(1)}, u32[]{:S(2)}, u32[]{:S(2)}) collective-permute-start(f32[24,2048]{1,0:T(8,128)S(1)} %get-tuple-element.13.refs_0_), channel_id=1, source_target_pairs={{0,3},{1,2},{2,1},{3,0},{4,7},{5,6},{6,5},{7,4},{8,11},{9,10},{10,... | collective-permute-start | bytes 589832 | tf_op jit(solution)/shard_map/ppermute | solution.py:261
  4.5 9.9 %collective-permute-start.1 = (f32[24,2048]{1,0:T(8,128)S(1)}, f32[24,2048]{1,0:T(8,128)S(1)}, u32[]{:S(2)}, u32[]{:S(2)}) collective-permute-start(f32[24,2048]{1,0:T(8,128)S(1)} %get-tuple-element.13.refs_0_), channel_id=1, source_target_pairs={{0,2},{1,3},{2,0},{3,1},{4,6},{5,7},{6,4},{7,5},{8,10},{9,11},{10,... | collective-permute-start | bytes 589832 | tf_op jit(solution)/shard_map/ppermute | solution.py:261
  5.1 9.2 %collective-permute-start = (f32[24,2048]{1,0:T(8,128)S(1)}, f32[24,2048]{1,0:T(8,128)S(1)}, u32[]{:S(2)}, u32[]{:S(2)}) collective-permute-start(f32[24,2048]{1,0:T(8,128)S(1)} %get-tuple-element.13.refs_0_), channel_id=1, source_target_pairs={{0,1},{1,0},{2,3},{3,2},{4,5},{5,4},{6,7},{7,6},{8,9},{9,8},{10,11... | collective-permute-start | bytes 589832 | tf_op jit(solution)/shard_map/ppermute | solution.py:261
  65.9 12.3 %collective-permute-start.3 = (f32[8,2048]{1,0:T(8,128)S(1)}, f32[8,2048]{1,0:T(8,128)S(1)}, u32[]{:S(2)}, u32[]{:S(2)}) collective-permute-start(f32[8,2048]{1,0:T(8,128)S(1)} %get-tuple-element.20), channel_id=1, source_target_pairs={{0,1},{1,0},{2,3},{3,2},{4,5},{5,4},{6,7},{7,6},{8,9},{9,8},{10,11... | collective-permute-start | bytes 196616 | tf_op jit(solution)/shard_map/ppermute | solution.py:261
  66.4 11.8 %collective-permute-start.4 = (f32[8,2048]{1,0:T(8,128)S(1)}, f32[8,2048]{1,0:T(8,128)S(1)}, u32[]{:S(2)}, u32[]{:S(2)}) collective-permute-start(f32[8,2048]{1,0:T(8,128)S(1)} %get-tuple-element.21), channel_id=1, source_target_pairs={{0,2},{1,3},{2,0},{3,1},{4,6},{5,7},{6,4},{7,5},{8,10},{9,11},{10,... | collective-permute-start | bytes 196616 | tf_op jit(solution)/shard_map/ppermute | solution.py:261
  68.2 10.0 %collective-permute-start.5 = (f32[8,2048]{1,0:T(8,128)S(1)}, f32[8,2048]{1,0:T(8,128)S(1)}, u32[]{:S(2)}, u32[]{:S(2)}) collective-permute-start(f32[8,2048]{1,0:T(8,128)S(1)} %get-tuple-element.22), channel_id=1, source_target_pairs={{0,3},{1,2},{2,1},{3,0},{4,7},{5,6},{6,5},{7,4},{8,11},{9,10},{10,... | collective-permute-start | bytes 196616 | tf_op jit(solution)/shard_map/ppermute | solution.py:261
  78.3 5.4 %collective-permute-start.8 = (f32[8,2048]{1,0:T(8,128)S(1)}, f32[8,2048]{1,0:T(8,128)S(1)}, u32[]{:S(2)}, u32[]{:S(2)}) collective-permute-start(f32[8,2048]{1,0:T(8,128)S(1)} %fusion.1), channel_id=1, source_target_pairs={{0,12},{4,8},{8,4},{12,0},{16,28},{20,24},{24,20},{28,16},{1,13},{... | collective-permute-start | bytes 196616 | tf_op jit(solution)/shard_map/ppermute | solution.py:261
  81.1 4.3 %collective-permute-start.7 = (f32[8,2048]{1,0:T(8,128)S(1)}, f32[8,2048]{1,0:T(8,128)S(1)}, u32[]{:S(2)}, u32[]{:S(2)}) collective-permute-start(f32[8,2048]{1,0:T(8,128)S(1)} %fusion.1), channel_id=1, source_target_pairs={{0,8},{4,12},{8,0},{12,4},{16,24},{20,28},{24,16},{28,20},{1,9},{5... | collective-permute-start | bytes 196616 | tf_op jit(solution)/shard_map/ppermute | solution.py:261
  81.5 4.3 %collective-permute-start.6 = (f32[8,2048]{1,0:T(8,128)S(1)}, f32[8,2048]{1,0:T(8,128)S(1)}, u32[]{:S(2)}, u32[]{:S(2)}) collective-permute-start(f32[8,2048]{1,0:T(8,128)S(1)} %fusion.1), channel_id=1, source_target_pairs={{0,4},{4,0},{8,12},{12,8},{16,20},{20,16},{24,28},{28,24},{1,5},{5... | collective-permute-start | bytes 196616 | tf_op jit(solution)/shard_map/ppermute | solution.py:261
  85.8 5.2 %collective-permute-start.9 = (f32[8,2048]{1,0:T(8,128)S(1)}, f32[8,2048]{1,0:T(8,128)S(1)}, u32[]{:S(2)}, u32[]{:S(2)}) collective-permute-start(f32[8,2048]{1,0:T(8,128)S(1)} %add_add_fusion), channel_id=1, source_target_pairs={{0,16},{4,20},{8,24},{12,28},{16,0},{20,4},{24,8},{28,12},{1,17},{... | collective-permute-start | bytes 196616 | tf_op jit(solution)/shard_map/ppermute | solution.py:261

commit v3 on v2

--- a/solution.py
+++ b/solution.py
@@ -13,6 +13,7 @@
 DEPTH = 128
 ROWS = 256
 COLS = 256
+GROUP = 1024
 AHEAD = 2
 
 
@@ -28,7 +29,7 @@
 
 
 def scale_features(features, lengthscale):
-    return features / lengthscale
+    return features / lengthscale * math.sqrt(math.log2(math.e))
 
 
 def norm_rows(scaled, own_first):
@@ -61,11 +62,6 @@
 
 def dot(left, right):
     return jnp.dot(left, right, preferred_element_type=F32)
-
-
-def dot_nt(left, right):
-    dims = (((1,), (1,)), ((), ()))
-    return lax.dot_general(left, right, dims, preferred_element_type=F32)
 
 
 def column(row):
@@ -99,7 +95,8 @@
             bst_ref[k * 16 : (k + 1) * 16, cols] = rows.astype(BF16)
         weights = hw_ref[:, cols] * (amplitude * fwd_scale)
         hi = round_bf16(weights)
-        w_ref[:, cols] = jnp.concatenate([hi, weights - hi], axis=0).astype(BF16)
+        pad = jnp.zeros((DEPTH - 16, COLS), F32)
+        w_ref[cols, :] = jnp.concatenate([hi, weights - hi, pad], axis=0).T.astype(BF16)
 
 
 def tile_kernel(offset, length, want_fwd, want_trans, has_total, counts, *refs):
@@ -119,6 +116,7 @@
     )
     hist = bst_ref.shape[1]
     half = hist // 2
+    group = min(GROUP, half)
     blocks = length // ROWS
 
     for k, piece in enumerate(pieces):
@@ -139,18 +137,21 @@
     def produce(slot, part, start):
         at = part * half + start
         exponent = dot(left_refs[slot][...], bst_ref[:, at : at + COLS])
-        hi, lo = hi_lo(jnp.exp(exponent))
+        hi, lo = hi_lo(jnp.exp2(exponent))
         tile_refs[part][0:ROWS, start : start + COLS] = hi
         tile_refs[part][ROWS : 2 * ROWS, start : start + COLS] = lo
 
-    def consume(part, start, u, fwd):
-        tile = tile_refs[part][:, start : start + COLS]
+    def consume(part, start, u, sums):
         at = part * half + start
         if want_trans:
-            acc_ref[:, at : at + COLS] += dot(u, tile)
+            acc_ref[:, at : at + COLS] += dot(u, tile_refs[part][:, start : start + COLS])
         if want_fwd:
-            fwd += dot_nt(w_ref[:, at : at + COLS], tile)
-        return fwd
+            first, step = start // group * group, start % group // COLS
+            share = 2 * ROWS * COLS // group
+            rows = slice(step * share, (step + 1) * share)
+            left = tile_refs[part][rows, first : first + group]
+            value = dot(left, w_ref[part * half + first : part * half + first + group, :])
+            sums[step] = value if sums[step] is None else sums[step] + value
 
     def vectors(block):
         u = u_ref[:, rows_of(block)]
@@ -170,7 +171,7 @@
         block = pair * 2
         prep(block + 1, 1)
         us = [vectors(block), vectors(block + 1)]
-        fwds = [jnp.zeros((16, 2 * ROWS), F32)] * 2
+        fwds = [[None] * (group // COLS) for _ in us]
         for n in range(len(makes) + AHEAD):
             if n == len(makes) // 2:
                 prep(jnp.minimum(block + 2, blocks - 1), 0)
@@ -178,10 +179,11 @@
                 produce(*makes[n])
             if n >= AHEAD:
                 k, part, start = uses[n - AHEAD]
-                fwds[k] = consume(part, start, us[k], fwds[k])
+                consume(part, start, us[k], fwds[k])
         if want_fwd:
-            for k, fwd in enumerate(fwds):
-                flat = fwd[:, 0:ROWS] + fwd[:, ROWS : 2 * ROWS]
+            for k, sums in enumerate(fwds):
+                fwd = jnp.concatenate(sums, axis=0)
+                flat = (fwd[0:ROWS] + fwd[ROWS : 2 * ROWS]).T
                 fwd_ref[:, rows_of(block + k)] = flat[0:8] + flat[8:16]
 
     for k, ref in enumerate(fwd_refs):
@@ -203,7 +205,7 @@
         functools.partial(prep_kernel, fwd_scale, trans_scale),
         out_shape=(
             jax.ShapeDtypeStruct((DEPTH, hist), BF16),
-            jax.ShapeDtypeStruct((16, hist), BF16),
+            jax.ShapeDtypeStruct((hist, DEPTH), BF16),
             jax.ShapeDtypeStruct((24, count), F32),
         ),
         in_specs=[pl.BlockSpec(memory_space=pltpu.HBM)] * 6,

time: 91.8 us -> 93.1 us (1.014)
  Pallas kernels: 72.1 us -> 73.5 us
    pallas_call x3, Pallas kernels: 70.7 us -> 71.8 us  [tile_call(): pl.pallas_call(kernel, out_shape=tuple(outs), in_specs=[VMEM] * len(args)...]
where the time goes in v3:
time: 93.1 us; the launch traced here: 93 us
  Pallas kernels  73.5 us (79%)
  starting transfers between devices  11.6 us (12%)
  waiting for transfers between devices  6.58 us (7%)
    pallas_call x3, Pallas kernels, tile_call(): pl.pallas_call(kernel, out_shape=tuple(outs), in_specs=[VMEM] * len(args)...  71.8 us
    ppermute x10, starting transfers between devices, exchange(): return lax.ppermute(x, axis, [(k, k ^ distance) for k in range(size)])  11.6 us
    ppermute x10, waiting for transfers between devices, exchange(): return lax.ppermute(x, axis, [(k, k ^ distance) for k in range(size)])  6.58 us
  transfers between devices with their start and end apart: 10, of which 4 were waited for; matrix products, arithmetic and copies ran while one was open for 0% of the time, Pallas kernels for 21%

profile of v3, /device:TPU:0, one launch (start us, length us, event | category | flops | bytes accessed | tf_op | source)
XLA Modules:
  0.0 93.0 jit_solution(18418417550067713527)
XLA Ops:
  0.6 1.7 %prepare.1 = (bf16[128,4096]{1,0:T(8,128)(2,1)S(1)}, bf16[4096,128]{1,0:T(8,128)(2,1)S(1)}, f32[24,2048]{1,0:T(8,128)S(1)}) custom-call(f32[16,4096]{1,0:T(8,128)} %refs_0_.1, f32[8,4096]{1,0:T(8,128)} %refs_1_.1, f32[16,2048]{1,0:T(8,128)} %refs_2_.1, f32[8,2048]{1,0:T(8,128)} %refs_3_.1, f32[1,16]{1,0:T(1,128)} %bitcast.2, f32[1,8]{1,0:T(1,128)} %bitcast.3), custom_call_target="tpu_custom_call" | custom-call | tf_op jit(solution)/shard_map/prepare/pallas_call | solution.py:204
  2.3 2.4 %collective-permute-start.2 = (f32[24,2048]{1,0:T(8,128)S(1)}, f32[24,2048]{1,0:T(8,128)S(1)}, u32[]{:S(2)}, u32[]{:S(2)}) collective-permute-start(f32[24,2048]{1,0:T(8,128)S(1)} %get-tuple-element.13.refs_0_), channel_id=1, source_target_pairs={{0,3},{1,2},{2,1},{3,0},{4,7},{5,6},{6,5},{7,4},{8,11},{9,10},{10,... | collective-permute-start | bytes 589832 | tf_op jit(solution)/shard_map/ppermute | solution.py:263
  4.7 0.6 collective-permute-start.1
  5.4 0.0 collective-permute-start
  5.4 9.3 %covariance_tiles.3 = (f32[8,1024]{1,0:T(8,128)S(1)}, f32[8,4096]{1,0:T(8,128)S(1)}) custom-call(f32[24,2048]{1,0:T(8,128)S(1)} %get-tuple-element.13.refs_0_, bf16[128,4096]{1,0:T(8,128)(2,1)S(1)} %get-tuple-element.14.refs_1_.refs_3_, bf16[4096,128]{1,0:T(8,128)(2,1)S(1)} %get-tuple-element.15.refs_2_.refs_4_), custom_call_target="tpu_custom_call" | custom-call | flops 10737418240 | bytes 2195456 | tf_op jit(solution)/shard_map/covariance_tiles/pallas_call | solution.py:234
  14.7 0.0 collective-permute-done.2.refs_2_
  14.7 0.0 collective-permute-done.1.refs_1_
  14.7 0.0 collective-permute-done.refs_0_
  14.7 52.5 %covariance_tiles.4 = (f32[8,2048]{1,0:T(8,128)S(1)}, f32[8,2048]{1,0:T(8,128)S(1)}, f32[8,2048]{1,0:T(8,128)S(1)}, f32[8,4096]{1,0:T(8,128)S(1)}) custom-call(f32[24,2048]{1,0:T(8,128)S(1)} %collective-permute-done.refs_0_, f32[24,2048]{1,0:T(8,128)S(1)} %collective-permute-done.1.refs_1_, f32[24,2048]{1,0:T(8,128)S(1)} %collective-permute-done.2.refs_2_, ...), custom_call_target="tpu_custom_call" | custom-call | flops 64424509440 | bytes 2686976 | tf_op jit(solution)/shard_map/covariance_tiles/pallas_call | solution.py:234
  67.2 0.5 collective-permute-start.3
  67.7 1.6 %collective-permute-start.4 = (f32[8,2048]{1,0:T(8,128)S(1)}, f32[8,2048]{1,0:T(8,128)S(1)}, u32[]{:S(2)}, u32[]{:S(2)}) collective-permute-start(f32[8,2048]{1,0:T(8,128)S(1)} %get-tuple-element.21), channel_id=1, source_target_pairs={{0,2},{1,3},{2,0},{3,1},{4,6},{5,7},{6,4},{7,5},{8,10},{9,11},{10,... | collective-permute-start | bytes 196616 | tf_op jit(solution)/shard_map/ppermute | solution.py:263
  69.4 0.1 collective-permute-start.5
  69.4 10.1 %covariance_tiles.5 = (f32[8,1024]{1,0:T(8,128)S(1)}, f32[8,4096]{1,0:T(8,128)}) custom-call(f32[24,2048]{1,0:T(8,128)S(1)} %get-tuple-element.13.refs_0_, bf16[128,4096]{1,0:T(8,128)(2,1)S(1)} %get-tuple-element.14.refs_1_.refs_3_, bf16[4096,128]{1,0:T(8,128)(2,1)S(1)} %get-tuple-element.15.refs_2_.refs_4_, f32[8,4096]{1,0:T(8,128)S(1)} %get-tuple-element.18.refs_3_), custom_call_target="tpu_custom_call" | custom-call | flops 10737418240 | bytes 2195456 | tf_op jit(solution)/shard_map/covariance_tiles/pallas_call | solution.py:234
  79.5 0.0 collective-permute-done.3
  79.5 0.0 collective-permute-done.4
  79.5 0.0 collective-permute-done.5
  79.5 2.8 %collective-permute-start.8 = (f32[8,2048]{1,0:T(8,128)S(1)}, f32[8,2048]{1,0:T(8,128)S(1)}, u32[]{:S(2)}, u32[]{:S(2)}) collective-permute-start(f32[8,2048]{1,0:T(8,128)S(1)} %fusion.1), channel_id=1, source_target_pairs={{0,12},{4,8},{8,4},{12,0},{16,28},{20,24},{24,20},{28,16},{1,13},{... | collective-permute-start | bytes 196616 | tf_op jit(solution)/shard_map/ppermute | solution.py:263
  82.4 0.4 collective-permute-start.7
  82.8 0.3 collective-permute-start.6
  83.1 1.9 %collective-permute-done.8 = f32[8,2048]{1,0:T(8,128)S(1)} collective-permute-done((f32[8,2048]{1,0:T(8,128)S(1)}, f32[8,2048]{1,0:T(8,128)S(1)}, u32[]{:S(2)}, u32[]{:S(2)}) %collective-permute-start.8) | collective-permute-done | bytes 65568 | tf_op jit(solution)/shard_map/ppermute | solution.py:263
  85.0 1.7 %collective-permute-done.7 = f32[8,2048]{1,0:T(8,128)S(1)} collective-permute-done((f32[8,2048]{1,0:T(8,128)S(1)}, f32[8,2048]{1,0:T(8,128)S(1)}, u32[]{:S(2)}, u32[]{:S(2)}) %collective-permute-start.7) | collective-permute-done | bytes 65568 | tf_op jit(solution)/shard_map/ppermute | solution.py:263
  86.6 0.4 collective-permute-done.6
  87.1 2.7 %collective-permute-start.9 = (f32[8,2048]{1,0:T(8,128)S(1)}, f32[8,2048]{1,0:T(8,128)S(1)}, u32[]{:S(2)}, u32[]{:S(2)}) collective-permute-start(f32[8,2048]{1,0:T(8,128)S(1)} %add_add_fusion), channel_id=1, source_target_pairs={{0,16},{4,20},{8,24},{12,28},{16,0},{20,4},{24,8},{28,12},{1,17},{... | collective-permute-start | bytes 196616 | tf_op jit(solution)/shard_map/ppermute | solution.py:263
  89.8 2.6 %collective-permute-done.9 = f32[8,2048]{1,0:T(8,128)S(1)} collective-permute-done((f32[8,2048]{1,0:T(8,128)S(1)}, f32[8,2048]{1,0:T(8,128)S(1)}, u32[]{:S(2)}, u32[]{:S(2)}) %collective-permute-start.9) | collective-permute-done | bytes 65568 | tf_op jit(solution)/shard_map/ppermute | solution.py:263
  92.3 0.6 add.27
  (2 shorter events, 0.0 us)
Async XLA Ops:
  2.3 12.4 %collective-permute-start.2 = (f32[24,2048]{1,0:T(8,128)S(1)}, f32[24,2048]{1,0:T(8,128)S(1)}, u32[]{:S(2)}, u32[]{:S(2)}) collective-permute-start(f32[24,2048]{1,0:T(8,128)S(1)} %get-tuple-element.13.refs_0_), channel_id=1, source_target_pairs={{0,3},{1,2},{2,1},{3,0},{4,7},{5,6},{6,5},{7,4},{8,11},{9,10},{10,... | collective-permute-start | bytes 589832 | tf_op jit(solution)/shard_map/ppermute | solution.py:263
  4.7 9.9 %collective-permute-start.1 = (f32[24,2048]{1,0:T(8,128)S(1)}, f32[24,2048]{1,0:T(8,128)S(1)}, u32[]{:S(2)}, u32[]{:S(2)}) collective-permute-start(f32[24,2048]{1,0:T(8,128)S(1)} %get-tuple-element.13.refs_0_), channel_id=1, source_target_pairs={{0,2},{1,3},{2,0},{3,1},{4,6},{5,7},{6,4},{7,5},{8,10},{9,11},{10,... | collective-permute-start | bytes 589832 | tf_op jit(solution)/shard_map/ppermute | solution.py:263
  5.4 9.3 %collective-permute-start = (f32[24,2048]{1,0:T(8,128)S(1)}, f32[24,2048]{1,0:T(8,128)S(1)}, u32[]{:S(2)}, u32[]{:S(2)}) collective-permute-start(f32[24,2048]{1,0:T(8,128)S(1)} %get-tuple-element.13.refs_0_), channel_id=1, source_target_pairs={{0,1},{1,0},{2,3},{3,2},{4,5},{5,4},{6,7},{7,6},{8,9},{9,8},{10,11... | collective-permute-start | bytes 589832 | tf_op jit(solution)/shard_map/ppermute | solution.py:263
  67.2 12.3 %collective-permute-start.3 = (f32[8,2048]{1,0:T(8,128)S(1)}, f32[8,2048]{1,0:T(8,128)S(1)}, u32[]{:S(2)}, u32[]{:S(2)}) collective-permute-start(f32[8,2048]{1,0:T(8,128)S(1)} %get-tuple-element.20), channel_id=1, source_target_pairs={{0,1},{1,0},{2,3},{3,2},{4,5},{5,4},{6,7},{7,6},{8,9},{9,8},{10,11... | collective-permute-start | bytes 196616 | tf_op jit(solution)/shard_map/ppermute | solution.py:263
  67.7 11.8 %collective-permute-start.4 = (f32[8,2048]{1,0:T(8,128)S(1)}, f32[8,2048]{1,0:T(8,128)S(1)}, u32[]{:S(2)}, u32[]{:S(2)}) collective-permute-start(f32[8,2048]{1,0:T(8,128)S(1)} %get-tuple-element.21), channel_id=1, source_target_pairs={{0,2},{1,3},{2,0},{3,1},{4,6},{5,7},{6,4},{7,5},{8,10},{9,11},{10,... | collective-permute-start | bytes 196616 | tf_op jit(solution)/shard_map/ppermute | solution.py:263
  69.4 10.2 %collective-permute-start.5 = (f32[8,2048]{1,0:T(8,128)S(1)}, f32[8,2048]{1,0:T(8,128)S(1)}, u32[]{:S(2)}, u32[]{:S(2)}) collective-permute-start(f32[8,2048]{1,0:T(8,128)S(1)} %get-tuple-element.22), channel_id=1, source_target_pairs={{0,3},{1,2},{2,1},{3,0},{4,7},{5,6},{6,5},{7,4},{8,11},{9,10},{10,... | collective-permute-start | bytes 196616 | tf_op jit(solution)/shard_map/ppermute | solution.py:263
  79.5 5.4 %collective-permute-start.8 = (f32[8,2048]{1,0:T(8,128)S(1)}, f32[8,2048]{1,0:T(8,128)S(1)}, u32[]{:S(2)}, u32[]{:S(2)}) collective-permute-start(f32[8,2048]{1,0:T(8,128)S(1)} %fusion.1), channel_id=1, source_target_pairs={{0,12},{4,8},{8,4},{12,0},{16,28},{20,24},{24,20},{28,16},{1,13},{... | collective-permute-start | bytes 196616 | tf_op jit(solution)/shard_map/ppermute | solution.py:263
  82.4 4.3 %collective-permute-start.7 = (f32[8,2048]{1,0:T(8,128)S(1)}, f32[8,2048]{1,0:T(8,128)S(1)}, u32[]{:S(2)}, u32[]{:S(2)}) collective-permute-start(f32[8,2048]{1,0:T(8,128)S(1)} %fusion.1), channel_id=1, source_target_pairs={{0,8},{4,12},{8,0},{12,4},{16,24},{20,28},{24,16},{28,20},{1,9},{5... | collective-permute-start | bytes 196616 | tf_op jit(solution)/shard_map/ppermute | solution.py:263
  82.8 4.3 %collective-permute-start.6 = (f32[8,2048]{1,0:T(8,128)S(1)}, f32[8,2048]{1,0:T(8,128)S(1)}, u32[]{:S(2)}, u32[]{:S(2)}) collective-permute-start(f32[8,2048]{1,0:T(8,128)S(1)} %fusion.1), channel_id=1, source_target_pairs={{0,4},{4,0},{8,12},{12,8},{16,20},{20,16},{24,28},{28,24},{1,5},{5... | collective-permute-start | bytes 196616 | tf_op jit(solution)/shard_map/ppermute | solution.py:263
  87.1 5.2 %collective-permute-start.9 = (f32[8,2048]{1,0:T(8,128)S(1)}, f32[8,2048]{1,0:T(8,128)S(1)}, u32[]{:S(2)}, u32[]{:S(2)}) collective-permute-start(f32[8,2048]{1,0:T(8,128)S(1)} %add_add_fusion), channel_id=1, source_target_pairs={{0,16},{4,20},{8,24},{12,28},{16,0},{20,4},{24,8},{28,12},{1,17},{... | collective-permute-start | bytes 196616 | tf_op jit(solution)/shard_map/ppermute | solution.py:263

commit v4 on v3

--- a/solution.py
+++ b/solution.py
@@ -13,7 +13,7 @@
 DEPTH = 128
 ROWS = 256
 COLS = 256
-GROUP = 1024
+GROUP = 512
 AHEAD = 2
 
 
@@ -64,6 +64,11 @@
     return jnp.dot(left, right, preferred_element_type=F32)
 
 
+def dot_nt(left, right):
+    dims = (((1,), (1,)), ((), ()))
+    return lax.dot_general(left, right, dims, preferred_element_type=F32)
+
+
 def column(row):
     size = row.shape[1]
     at = lax.broadcasted_iota(jnp.int32, (size, size), 0)
@@ -72,8 +77,8 @@
 
 
 def prep_kernel(fwd_scale, trans_scale, *refs):
-    sources, (bst_ref, w_ref, own_ref) = refs[:6], refs[6:9]
-    held, sems = refs[9:15], refs[15]
+    sources, (bst_ref, w_ref, wt_ref, own_ref) = refs[:6], refs[6:10]
+    held, sems = refs[10:16], refs[16]
     copies = [
         pltpu.make_async_copy(source, target, sems.at[k])
         for k, (source, target) in enumerate(zip(sources, held))
@@ -96,13 +101,14 @@
         weights = hw_ref[:, cols] * (amplitude * fwd_scale)
         hi = round_bf16(weights)
         pad = jnp.zeros((DEPTH - 16, COLS), F32)
-        w_ref[cols, :] = jnp.concatenate([hi, weights - hi, pad], axis=0).T.astype(BF16)
+        w_ref[:, cols] = jnp.concatenate([hi, weights - hi], axis=0).astype(BF16)
+        wt_ref[cols, :] = jnp.concatenate([hi, weights - hi, pad], axis=0).T.astype(BF16)
 
 
 def tile_kernel(offset, length, want_fwd, want_trans, has_total, counts, *refs):
     refs = list(refs)
     pieces = [refs.pop(0) for _ in counts]
-    bst_ref, w_ref = refs.pop(0), refs.pop(0)
+    bst_ref, w_ref, wt_ref = refs.pop(0), refs.pop(0), refs.pop(0)
     total_ref = refs.pop(0) if has_total else None
     fwd_refs = [refs.pop(0) for _ in counts] if want_fwd else []
     trans_ref = refs.pop(0) if want_trans else None
@@ -147,11 +153,13 @@
             acc_ref[:, at : at + COLS] += dot(u, tile_refs[part][:, start : start + COLS])
         if want_fwd:
             first, step = start // group * group, start % group // COLS
-            share = 2 * ROWS * COLS // group
-            rows = slice(step * share, (step + 1) * share)
-            left = tile_refs[part][rows, first : first + group]
-            value = dot(left, w_ref[part * half + first : part * half + first + group, :])
+            share = ROWS * COLS // group
+            left = tile_refs[part][step * share : (step + 1) * share, first : first + group]
+            value = dot(left, wt_ref[part * half + first : part * half + first + group, :])
             sums[step] = value if sums[step] is None else sums[step] + value
+            low = tile_refs[part][ROWS : 2 * ROWS, start : start + COLS]
+            value = dot_nt(w_ref[:, at : at + COLS], low)
+            sums[-1] = value if sums[-1] is None else sums[-1] + value
 
     def vectors(block):
         u = u_ref[:, rows_of(block)]
@@ -171,7 +179,7 @@
         block = pair * 2
         prep(block + 1, 1)
         us = [vectors(block), vectors(block + 1)]
-        fwds = [[None] * (group // COLS) for _ in us]
+        fwds = [[None] * (group // COLS + 1) for _ in us]
         for n in range(len(makes) + AHEAD):
             if n == len(makes) // 2:
                 prep(jnp.minimum(block + 2, blocks - 1), 0)
@@ -182,8 +190,7 @@
                 consume(part, start, us[k], fwds[k])
         if want_fwd:
             for k, sums in enumerate(fwds):
-                fwd = jnp.concatenate(sums, axis=0)
-                flat = (fwd[0:ROWS] + fwd[ROWS : 2 * ROWS]).T
+                flat = jnp.concatenate(sums[:-1], axis=0).T[0:16] + sums[-1]
                 fwd_ref[:, rows_of(block + k)] = flat[0:8] + flat[8:16]
 
     for k, ref in enumerate(fwd_refs):
@@ -205,11 +212,12 @@
         functools.partial(prep_kernel, fwd_scale, trans_scale),
         out_shape=(
             jax.ShapeDtypeStruct((DEPTH, hist), BF16),
+            jax.ShapeDtypeStruct((16, hist), BF16),
             jax.ShapeDtypeStruct((hist, DEPTH), BF16),
             jax.ShapeDtypeStruct((24, count), F32),
         ),
         in_specs=[pl.BlockSpec(memory_space=pltpu.HBM)] * 6,
-        out_specs=(VMEM,) * 3,
+        out_specs=(VMEM,) * 4,
         scratch_shapes=[pltpu.VMEM(arg.shape, F32) for arg in args]
         + [pltpu.SemaphoreType.DMA((6,))],
         compiler_params=PARAMS,
@@ -217,13 +225,13 @@
     )(*[pltpu.with_memory_space_constraint(arg, pltpu.HBM) for arg in args])
 
 
-def tile_call(pieces, offset, length, total, bst, w, want_fwd=True, want_trans=True):
+def tile_call(pieces, offset, length, total, bst, w, wt, want_fwd=True, want_trans=True):
     hist = bst.shape[1]
     rows = length * len(pieces)
     kernel = functools.partial(
         tile_kernel, offset, rows, want_fwd, want_trans, total is not None, [length] * len(pieces)
     )
-    args = [*pieces, bst, w]
+    args = [*pieces, bst, w, wt]
     if total is not None:
         args.append(total)
     outs = []
@@ -270,7 +278,7 @@
     wide = lax.axis_size("wide")
     fwd_scale = 1.0 / math.sqrt(hist * wide * narrow)
     trans_scale = 1.0 / math.sqrt(count * narrow)
-    bst, w, own = prepare(
+    bst, w, wt, own = prepare(
         fwd_scale,
         trans_scale,
         hist_features,
@@ -281,7 +289,7 @@
         amplitude[None, :],
     )
     pieces = [exchange(own, "narrow", k) for k in range(1, narrow)]
-    call = functools.partial(tile_call, bst=bst, w=w)
+    call = functools.partial(tile_call, bst=bst, w=w, wt=wt)
     first = count // 2
     fwd_a, total = call([own], 0, first, None)
     others, total = call(pieces, 0, count, total)

time: 93.1 us -> 95.3 us (1.024)
  Pallas kernels: 73.5 us -> 75.9 us
    pallas_call x3, Pallas kernels: 71.8 us -> 74.2 us  [tile_call(): pl.pallas_call(kernel, out_shape=tuple(outs), in_specs=[VMEM] * len(args)...]
where the time goes in v4:
time: 95.3 us; the launch traced here: 95.2 us
  Pallas kernels  75.9 us (80%)
  starting transfers between devices  11.5 us (12%)
  waiting for transfers between devices  6.46 us (7%)
    pallas_call x3, Pallas kernels, tile_call(): pl.pallas_call(kernel, out_shape=tuple(outs), in_specs=[VMEM] * len(args)...  74.2 us
    ppermute x10, starting transfers between devices, exchange(): return lax.ppermute(x, axis, [(k, k ^ distance) for k in range(size)])  11.5 us
    ppermute x10, waiting for transfers between devices, exchange(): return lax.ppermute(x, axis, [(k, k ^ distance) for k in range(size)])  6.46 us
  transfers between devices with their start and end apart: 10, of which 4 were waited for; matrix products, arithmetic and copies ran while one was open for 0% of the time, Pallas kernels for 21%

profile of v4, /device:TPU:0, one launch (start us, length us, event | category | flops | bytes accessed | tf_op | source)
XLA Modules:
  0.0 95.2 jit_solution(18415718819051952310)
XLA Ops:
  0.6 1.7 %prepare.1 = (bf16[128,4096]{1,0:T(8,128)(2,1)S(1)}, bf16[16,4096]{1,0:T(8,128)(2,1)S(1)}, bf16[4096,128]{1,0:T(8,128)(2,1)S(1)}, f32[24,2048]{1,0:T(8,128)S(1)}) custom-call(f32[16,4096]{1,0:T(8,128)} %refs_0_.1, f32[8,4096]{1,0:T(8,128)} %refs_1_.1, f32[16,2048]{1,0:T(8,128)} %refs_2_.1, f32[8,2048]{1,0:T(8,128)} %refs_3_.1, f32[1,16]{1,0:T(1,128)} %bitcast.2, ...), custom_call_target="tpu_custom_call" | custom-call | tf_op jit(solution)/shard_map/prepare/pallas_call | solution.py:211
  2.3 2.4 %collective-permute-start.2 = (f32[24,2048]{1,0:T(8,128)S(1)}, f32[24,2048]{1,0:T(8,128)S(1)}, u32[]{:S(2)}, u32[]{:S(2)}) collective-permute-start(f32[24,2048]{1,0:T(8,128)S(1)} %get-tuple-element.14.refs_0_), channel_id=1, source_target_pairs={{0,3},{1,2},{2,1},{3,0},{4,7},{5,6},{6,5},{7,4},{8,11},{9,10},{10,... | collective-permute-start | bytes 589832 | tf_op jit(solution)/shard_map/ppermute | solution.py:271
  4.7 0.6 collective-permute-start.1
  5.4 0.0 collective-permute-start
  5.4 9.6 %covariance_tiles.3 = (f32[8,1024]{1,0:T(8,128)S(1)}, f32[8,4096]{1,0:T(8,128)S(1)}) custom-call(f32[24,2048]{1,0:T(8,128)S(1)} %get-tuple-element.14.refs_0_, bf16[128,4096]{1,0:T(8,128)(2,1)S(1)} %get-tuple-element.15.refs_1_.refs_3_, bf16[16,4096]{1,0:T(8,128)(2,1)S(1)} %get-tuple-element.16.refs_2_.refs_4_, ...), custom_call_target="tpu_custom_call" | custom-call | flops 10737418240 | bytes 2195456 | tf_op jit(solution)/shard_map/covariance_tiles/pallas_call | solution.py:242
  15.0 0.0 collective-permute-done.2.refs_2_
  15.0 0.0 collective-permute-done.1.refs_1_
  15.0 0.0 collective-permute-done.refs_0_
  15.0 54.2 %covariance_tiles.4 = (f32[8,2048]{1,0:T(8,128)S(1)}, f32[8,2048]{1,0:T(8,128)S(1)}, f32[8,2048]{1,0:T(8,128)S(1)}, f32[8,4096]{1,0:T(8,128)S(1)}) custom-call(f32[24,2048]{1,0:T(8,128)S(1)} %collective-permute-done.refs_0_, f32[24,2048]{1,0:T(8,128)S(1)} %collective-permute-done.1.refs_1_, f32[24,2048]{1,0:T(8,128)S(1)} %collective-permute-done.2.refs_2_, ...), custom_call_target="tpu_custom_call" | custom-call | flops 64424509440 | bytes 2686976 | tf_op jit(solution)/shard_map/covariance_tiles/pallas_call | solution.py:242
  69.3 0.5 collective-permute-start.3
  69.8 1.4 %collective-permute-start.4 = (f32[8,2048]{1,0:T(8,128)S(1)}, f32[8,2048]{1,0:T(8,128)S(1)}, u32[]{:S(2)}, u32[]{:S(2)}) collective-permute-start(f32[8,2048]{1,0:T(8,128)S(1)} %get-tuple-element.23), channel_id=1, source_target_pairs={{0,2},{1,3},{2,0},{3,1},{4,6},{5,7},{6,4},{7,5},{8,10},{9,11},{10,... | collective-permute-start | bytes 196616 | tf_op jit(solution)/shard_map/ppermute | solution.py:271
  71.2 0.1 collective-permute-start.5
  71.3 10.4 %covariance_tiles.5 = (f32[8,1024]{1,0:T(8,128)S(1)}, f32[8,4096]{1,0:T(8,128)}) custom-call(f32[24,2048]{1,0:T(8,128)S(1)} %get-tuple-element.14.refs_0_, bf16[128,4096]{1,0:T(8,128)(2,1)S(1)} %get-tuple-element.15.refs_1_.refs_3_, bf16[16,4096]{1,0:T(8,128)(2,1)S(1)} %get-tuple-element.16.refs_2_.refs_4_, ...), custom_call_target="tpu_custom_call" | custom-call | flops 10737418240 | bytes 2195456 | tf_op jit(solution)/shard_map/covariance_tiles/pallas_call | solution.py:242
  81.7 0.0 collective-permute-done.3
  81.7 0.0 collective-permute-done.4
  81.7 0.0 collective-permute-done.5
  81.7 2.8 %collective-permute-start.8 = (f32[8,2048]{1,0:T(8,128)S(1)}, f32[8,2048]{1,0:T(8,128)S(1)}, u32[]{:S(2)}, u32[]{:S(2)}) collective-permute-start(f32[8,2048]{1,0:T(8,128)S(1)} %fusion.1), channel_id=1, source_target_pairs={{0,12},{4,8},{8,4},{12,0},{16,28},{20,24},{24,20},{28,16},{1,13},{... | collective-permute-start | bytes 196616 | tf_op jit(solution)/shard_map/ppermute | solution.py:271
  84.5 0.4 collective-permute-start.7
  84.9 0.4 collective-permute-start.6
  85.3 2.1 %collective-permute-done.8 = f32[8,2048]{1,0:T(8,128)S(1)} collective-permute-done((f32[8,2048]{1,0:T(8,128)S(1)}, f32[8,2048]{1,0:T(8,128)S(1)}, u32[]{:S(2)}, u32[]{:S(2)}) %collective-permute-start.8) | collective-permute-done | bytes 65568 | tf_op jit(solution)/shard_map/ppermute | solution.py:271
  87.4 1.4 %collective-permute-done.7 = f32[8,2048]{1,0:T(8,128)S(1)} collective-permute-done((f32[8,2048]{1,0:T(8,128)S(1)}, f32[8,2048]{1,0:T(8,128)S(1)}, u32[]{:S(2)}, u32[]{:S(2)}) %collective-permute-start.7) | collective-permute-done | bytes 65568 | tf_op jit(solution)/shard_map/ppermute | solution.py:271
  88.8 0.4 collective-permute-done.6
  89.2 2.8 %collective-permute-start.9 = (f32[8,2048]{1,0:T(8,128)S(1)}, f32[8,2048]{1,0:T(8,128)S(1)}, u32[]{:S(2)}, u32[]{:S(2)}) collective-permute-start(f32[8,2048]{1,0:T(8,128)S(1)} %add_add_fusion), channel_id=1, source_target_pairs={{0,16},{4,20},{8,24},{12,28},{16,0},{20,4},{24,8},{28,12},{1,17},{... | collective-permute-start | bytes 196616 | tf_op jit(solution)/shard_map/ppermute | solution.py:271
  92.0 2.6 %collective-permute-done.9 = f32[8,2048]{1,0:T(8,128)S(1)} collective-permute-done((f32[8,2048]{1,0:T(8,128)S(1)}, f32[8,2048]{1,0:T(8,128)S(1)}, u32[]{:S(2)}, u32[]{:S(2)}) %collective-permute-start.9) | collective-permute-done | bytes 65568 | tf_op jit(solution)/shard_map/ppermute | solution.py:271
  94.5 0.6 add.27
  (2 shorter events, 0.0 us)
Async XLA Ops:
  2.3 12.7 %collective-permute-start.2 = (f32[24,2048]{1,0:T(8,128)S(1)}, f32[24,2048]{1,0:T(8,128)S(1)}, u32[]{:S(2)}, u32[]{:S(2)}) collective-permute-start(f32[24,2048]{1,0:T(8,128)S(1)} %get-tuple-element.14.refs_0_), channel_id=1, source_target_pairs={{0,3},{1,2},{2,1},{3,0},{4,7},{5,6},{6,5},{7,4},{8,11},{9,10},{10,... | collective-permute-start | bytes 589832 | tf_op jit(solution)/shard_map/ppermute | solution.py:271
  4.7 10.3 %collective-permute-start.1 = (f32[24,2048]{1,0:T(8,128)S(1)}, f32[24,2048]{1,0:T(8,128)S(1)}, u32[]{:S(2)}, u32[]{:S(2)}) collective-permute-start(f32[24,2048]{1,0:T(8,128)S(1)} %get-tuple-element.14.refs_0_), channel_id=1, source_target_pairs={{0,2},{1,3},{2,0},{3,1},{4,6},{5,7},{6,4},{7,5},{8,10},{9,11},{10,... | collective-permute-start | bytes 589832 | tf_op jit(solution)/shard_map/ppermute | solution.py:271
  5.4 9.6 %collective-permute-start = (f32[24,2048]{1,0:T(8,128)S(1)}, f32[24,2048]{1,0:T(8,128)S(1)}, u32[]{:S(2)}, u32[]{:S(2)}) collective-permute-start(f32[24,2048]{1,0:T(8,128)S(1)} %get-tuple-element.14.refs_0_), channel_id=1, source_target_pairs={{0,1},{1,0},{2,3},{3,2},{4,5},{5,4},{6,7},{7,6},{8,9},{9,8},{10,11... | collective-permute-start | bytes 589832 | tf_op jit(solution)/shard_map/ppermute | solution.py:271
  69.3 12.4 %collective-permute-start.3 = (f32[8,2048]{1,0:T(8,128)S(1)}, f32[8,2048]{1,0:T(8,128)S(1)}, u32[]{:S(2)}, u32[]{:S(2)}) collective-permute-start(f32[8,2048]{1,0:T(8,128)S(1)} %get-tuple-element.22), channel_id=1, source_target_pairs={{0,1},{1,0},{2,3},{3,2},{4,5},{5,4},{6,7},{7,6},{8,9},{9,8},{10,11... | collective-permute-start | bytes 196616 | tf_op jit(solution)/shard_map/ppermute | solution.py:271
  69.8 11.9 %collective-permute-start.4 = (f32[8,2048]{1,0:T(8,128)S(1)}, f32[8,2048]{1,0:T(8,128)S(1)}, u32[]{:S(2)}, u32[]{:S(2)}) collective-permute-start(f32[8,2048]{1,0:T(8,128)S(1)} %get-tuple-element.23), channel_id=1, source_target_pairs={{0,2},{1,3},{2,0},{3,1},{4,6},{5,7},{6,4},{7,5},{8,10},{9,11},{10,... | collective-permute-start | bytes 196616 | tf_op jit(solution)/shard_map/ppermute | solution.py:271
  71.2 10.5 %collective-permute-start.5 = (f32[8,2048]{1,0:T(8,128)S(1)}, f32[8,2048]{1,0:T(8,128)S(1)}, u32[]{:S(2)}, u32[]{:S(2)}) collective-permute-start(f32[8,2048]{1,0:T(8,128)S(1)} %get-tuple-element.24), channel_id=1, source_target_pairs={{0,3},{1,2},{2,1},{3,0},{4,7},{5,6},{6,5},{7,4},{8,11},{9,10},{10,... | collective-permute-start | bytes 196616 | tf_op jit(solution)/shard_map/ppermute | solution.py:271
  81.7 5.7 %collective-permute-start.8 = (f32[8,2048]{1,0:T(8,128)S(1)}, f32[8,2048]{1,0:T(8,128)S(1)}, u32[]{:S(2)}, u32[]{:S(2)}) collective-permute-start(f32[8,2048]{1,0:T(8,128)S(1)} %fusion.1), channel_id=1, source_target_pairs={{0,12},{4,8},{8,4},{12,0},{16,28},{20,24},{24,20},{28,16},{1,13},{... | collective-permute-start | bytes 196616 | tf_op jit(solution)/shard_map/ppermute | solution.py:271
  84.5 4.3 %collective-permute-start.7 = (f32[8,2048]{1,0:T(8,128)S(1)}, f32[8,2048]{1,0:T(8,128)S(1)}, u32[]{:S(2)}, u32[]{:S(2)}) collective-permute-start(f32[8,2048]{1,0:T(8,128)S(1)} %fusion.1), channel_id=1, source_target_pairs={{0,8},{4,12},{8,0},{12,4},{16,24},{20,28},{24,16},{28,20},{1,9},{5... | collective-permute-start | bytes 196616 | tf_op jit(solution)/shard_map/ppermute | solution.py:271
  84.9 4.3 %collective-permute-start.6 = (f32[8,2048]{1,0:T(8,128)S(1)}, f32[8,2048]{1,0:T(8,128)S(1)}, u32[]{:S(2)}, u32[]{:S(2)}) collective-permute-start(f32[8,2048]{1,0:T(8,128)S(1)} %fusion.1), channel_id=1, source_target_pairs={{0,4},{4,0},{8,12},{12,8},{16,20},{20,16},{24,28},{28,24},{1,5},{5... | collective-permute-start | bytes 196616 | tf_op jit(solution)/shard_map/ppermute | solution.py:271
  89.2 5.3 %collective-permute-start.9 = (f32[8,2048]{1,0:T(8,128)S(1)}, f32[8,2048]{1,0:T(8,128)S(1)}, u32[]{:S(2)}, u32[]{:S(2)}) collective-permute-start(f32[8,2048]{1,0:T(8,128)S(1)} %add_add_fusion), channel_id=1, source_target_pairs={{0,16},{4,20},{8,24},{12,28},{16,0},{20,4},{24,8},{28,12},{1,17},{... | collective-permute-start | bytes 196616 | tf_op jit(solution)/shard_map/ppermute | solution.py:271

commit v5 on v2

--- a/solution.py
+++ b/solution.py
@@ -13,6 +13,8 @@
 DEPTH = 128
 ROWS = 256
 COLS = 256
+FLIP_ROUND = 2
+FLIP_HI = 2
 AHEAD = 2
 
 
@@ -28,7 +30,7 @@
 
 
 def scale_features(features, lengthscale):
-    return features / lengthscale
+    return features / lengthscale * math.sqrt(math.log2(math.e))
 
 
 def norm_rows(scaled, own_first):
@@ -109,14 +111,8 @@
     total_ref = refs.pop(0) if has_total else None
     fwd_refs = [refs.pop(0) for _ in counts] if want_fwd else []
     trans_ref = refs.pop(0) if want_trans else None
-    anal_ref, left_refs, u_ref, tile_refs, fwd_ref, acc_ref = (
-        refs[0],
-        refs[1:3],
-        refs[3],
-        refs[4:6],
-        refs[6],
-        refs[7],
-    )
+    anal_ref, u_ref, fwd_ref, acc_ref = refs[0:4]
+    left_refs, tile_refs, flip_refs = refs[4:6], refs[6:8], refs[8:10]
     hist = bst_ref.shape[1]
     half = hist // 2
     blocks = length // ROWS
@@ -136,12 +132,19 @@
         stack = jnp.concatenate(stack_anal(anal_ref[0:16, rows_of(block)]), axis=0)
         left_refs[slot][...] = stack.T.astype(BF16)
 
+    def flips_hi(start):
+        return start // COLS % FLIP_ROUND < FLIP_HI
+
     def produce(slot, part, start):
         at = part * half + start
         exponent = dot(left_refs[slot][...], bst_ref[:, at : at + COLS])
-        hi, lo = hi_lo(jnp.exp(exponent))
+        hi, lo = hi_lo(jnp.exp2(exponent))
         tile_refs[part][0:ROWS, start : start + COLS] = hi
         tile_refs[part][ROWS : 2 * ROWS, start : start + COLS] = lo
+        if want_fwd:
+            flip_refs[part][start : start + COLS, ROWS : 2 * ROWS] = lo.T
+            if flips_hi(start):
+                flip_refs[part][start : start + COLS, 0:ROWS] = hi.T
 
     def consume(part, start, u, fwd):
         tile = tile_refs[part][:, start : start + COLS]
@@ -149,7 +152,13 @@
         if want_trans:
             acc_ref[:, at : at + COLS] += dot(u, tile)
         if want_fwd:
-            fwd += dot_nt(w_ref[:, at : at + COLS], tile)
+            w = w_ref[:, at : at + COLS]
+            flip = flip_refs[part][start : start + COLS, :]
+            if flips_hi(start):
+                both = dot(w, flip)
+                fwd += both[:, 0:ROWS] + both[:, ROWS : 2 * ROWS]
+            else:
+                fwd += dot_nt(w, tile[0:ROWS]) + dot(w, flip[:, ROWS : 2 * ROWS])
         return fwd
 
     def vectors(block):
@@ -170,7 +179,7 @@
         block = pair * 2
         prep(block + 1, 1)
         us = [vectors(block), vectors(block + 1)]
-        fwds = [jnp.zeros((16, 2 * ROWS), F32)] * 2
+        fwds = [jnp.zeros((16, ROWS), F32)] * 2
         for n in range(len(makes) + AHEAD):
             if n == len(makes) // 2:
                 prep(jnp.minimum(block + 2, blocks - 1), 0)
@@ -181,8 +190,7 @@
                 fwds[k] = consume(part, start, us[k], fwds[k])
         if want_fwd:
             for k, fwd in enumerate(fwds):
-                flat = fwd[:, 0:ROWS] + fwd[:, ROWS : 2 * ROWS]
-                fwd_ref[:, rows_of(block + k)] = flat[0:8] + flat[8:16]
+                fwd_ref[:, rows_of(block + k)] = fwd[0:8] + fwd[8:16]
 
     for k, ref in enumerate(fwd_refs):
         size = length // len(pieces)
@@ -236,13 +244,15 @@
         out_specs=(VMEM,) * len(outs),
         scratch_shapes=[
             pltpu.VMEM((24, rows), F32),
+            pltpu.VMEM((16, rows), BF16),
+            pltpu.VMEM((8, rows), F32),
+            pltpu.VMEM((16, hist), F32),
             pltpu.VMEM((ROWS, DEPTH), BF16),
             pltpu.VMEM((ROWS, DEPTH), BF16),
-            pltpu.VMEM((16, rows), BF16),
             pltpu.VMEM((2 * ROWS, hist // 2), BF16),
             pltpu.VMEM((2 * ROWS, hist // 2), BF16),
-            pltpu.VMEM((8, rows), F32),
-            pltpu.VMEM((16, hist), F32),
+            pltpu.VMEM((hist // 2, 2 * ROWS), BF16),
+            pltpu.VMEM((hist // 2, 2 * ROWS), BF16),
         ],
         compiler_params=PARAMS,
         cost_estimate=pl.CostEstimate(

time: 91.8 us -> 80.2 us (0.87)
  Pallas kernels: 72.1 us -> 59.1 us
  waiting for transfers between devices: 6.57 us -> 7.79 us
    pallas_call x3, Pallas kernels: 70.7 us -> 57.7 us  [tile_call(): pl.pallas_call(kernel, out_shape=tuple(outs), in_specs=[VMEM] * len(args)...]
    ppermute x10, waiting for transfers between devices: 6.57 us -> 7.79 us  [exchange(): return lax.ppermute(x, axis, [(k, k ^ distance) for k in range(size)])]
  transfers between devices with their start and end apart: 10 -> 10, of which waited for: 4 -> 5; matrix products, arithmetic and copies ran while one was open for 0% -> 0% of each run, Pallas kernels for 21% -> 20%
where the time goes in v5:
time: 80.2 us; the launch traced here: 80.1 us
  Pallas kernels  59.1 us (74%)
  starting transfers between devices  11.8 us (15%)
  waiting for transfers between devices  7.79 us (10%)
    pallas_call x3, Pallas kernels, tile_call(): pl.pallas_call(kernel, out_shape=tuple(outs), in_specs=[VMEM] * len(args)...  57.7 us
    ppermute x10, starting transfers between devices, exchange(): return lax.ppermute(x, axis, [(k, k ^ distance) for k in range(size)])  11.8 us
    ppermute x10, waiting for transfers between devices, exchange(): return lax.ppermute(x, axis, [(k, k ^ distance) for k in range(size)])  7.79 us
  transfers between devices with their start and end apart: 10, of which 5 were waited for; matrix products, arithmetic and copies ran while one was open for 0% of the time, Pallas kernels for 20%

profile of v5, /device:TPU:0, one launch (start us, length us, event | category | flops | bytes accessed | tf_op | source)
XLA Modules:
  0.0 80.1 jit_solution(16818310492428289340)
XLA Ops:
  0.6 1.4 %prepare.1 = (bf16[128,4096]{1,0:T(8,128)(2,1)S(1)}, bf16[16,4096]{1,0:T(8,128)(2,1)S(1)}, f32[24,2048]{1,0:T(8,128)S(1)}) custom-call(f32[16,4096]{1,0:T(8,128)} %refs_0_.1, f32[8,4096]{1,0:T(8,128)} %refs_1_.1, f32[16,2048]{1,0:T(8,128)} %refs_2_.1, f32[8,2048]{1,0:T(8,128)} %refs_3_.1, f32[1,16]{1,0:T(1,128)} %bitcast.2, f32[1,8]{1,0:T(1,128)} %bitcast.3), custom_call_target="tpu_custom_call" | custom-call | tf_op jit(solution)/shard_map/prepare/pallas_call | solution.py:210
  2.0 2.4 %collective-permute-start.2 = (f32[24,2048]{1,0:T(8,128)S(1)}, f32[24,2048]{1,0:T(8,128)S(1)}, u32[]{:S(2)}, u32[]{:S(2)}) collective-permute-start(f32[24,2048]{1,0:T(8,128)S(1)} %get-tuple-element.13.refs_0_), channel_id=1, source_target_pairs={{0,3},{1,2},{2,1},{3,0},{4,7},{5,6},{6,5},{7,4},{8,11},{9,10},{10,... | collective-permute-start | bytes 589832 | tf_op jit(solution)/shard_map/ppermute | solution.py:271
  4.5 0.6 collective-permute-start.1
  5.1 0.0 collective-permute-start
  5.2 7.8 %covariance_tiles.3 = (f32[8,1024]{1,0:T(8,128)S(1)}, f32[8,4096]{1,0:T(8,128)S(1)}) custom-call(f32[24,2048]{1,0:T(8,128)S(1)} %get-tuple-element.13.refs_0_, bf16[128,4096]{1,0:T(8,128)(2,1)S(1)} %get-tuple-element.14.refs_1_.refs_3_, bf16[16,4096]{1,0:T(8,128)(2,1)S(1)} %get-tuple-element.15.refs_2_.refs_4_), custom_call_target="tpu_custom_call" | custom-call | flops 10737418240 | bytes 2195456 | tf_op jit(solution)/shard_map/covariance_tiles/pallas_call | solution.py:240
  12.9 0.0 collective-permute-done.2.refs_2_
  12.9 1.2 %collective-permute-done.1.refs_1_ = f32[24,2048]{1,0:T(8,128)S(1)} collective-permute-done((f32[24,2048]{1,0:T(8,128)S(1)}, f32[24,2048]{1,0:T(8,128)S(1)}, u32[]{:S(2)}, u32[]{:S(2)}) %collective-permute-start.1) | collective-permute-done | bytes 196640 | tf_op jit(solution)/shard_map/ppermute | solution.py:271
  14.2 0.0 collective-permute-done.refs_0_
  14.2 41.3 %covariance_tiles.4 = (f32[8,2048]{1,0:T(8,128)S(1)}, f32[8,2048]{1,0:T(8,128)S(1)}, f32[8,2048]{1,0:T(8,128)S(1)}, f32[8,4096]{1,0:T(8,128)S(1)}) custom-call(f32[24,2048]{1,0:T(8,128)S(1)} %collective-permute-done.refs_0_, f32[24,2048]{1,0:T(8,128)S(1)} %collective-permute-done.1.refs_1_, f32[24,2048]{1,0:T(8,128)S(1)} %collective-permute-done.2.refs_2_, ...), custom_call_target="tpu_custom_call" | custom-call | flops 64424509440 | bytes 2686976 | tf_op jit(solution)/shard_map/covariance_tiles/pallas_call | solution.py:240
  55.5 0.1 collective-permute-start.3
  55.6 2.4 %collective-permute-start.4 = (f32[8,2048]{1,0:T(8,128)S(1)}, f32[8,2048]{1,0:T(8,128)S(1)}, u32[]{:S(2)}, u32[]{:S(2)}) collective-permute-start(f32[8,2048]{1,0:T(8,128)S(1)} %get-tuple-element.21), channel_id=1, source_target_pairs={{0,2},{1,3},{2,0},{3,1},{4,6},{5,7},{6,4},{7,5},{8,10},{9,11},{10,... | collective-permute-start | bytes 196616 | tf_op jit(solution)/shard_map/ppermute | solution.py:271
  58.0 0.1 collective-permute-start.5
  58.0 8.6 %covariance_tiles.5 = (f32[8,1024]{1,0:T(8,128)S(1)}, f32[8,4096]{1,0:T(8,128)}) custom-call(f32[24,2048]{1,0:T(8,128)S(1)} %get-tuple-element.13.refs_0_, bf16[128,4096]{1,0:T(8,128)(2,1)S(1)} %get-tuple-element.14.refs_1_.refs_3_, bf16[16,4096]{1,0:T(8,128)(2,1)S(1)} %get-tuple-element.15.refs_2_.refs_4_, f32[8,4096]{1,0:T(8,128)S(1)} %get-tuple-element.18.refs_3_), custom_call_target="tpu_custom_call" | custom-call | flops 10737418240 | bytes 2195456 | tf_op jit(solution)/shard_map/covariance_tiles/pallas_call | solution.py:240
  66.6 0.0 collective-permute-done.3
  66.6 0.0 collective-permute-done.4
  66.6 0.0 collective-permute-done.5
  66.7 2.8 %collective-permute-start.8 = (f32[8,2048]{1,0:T(8,128)S(1)}, f32[8,2048]{1,0:T(8,128)S(1)}, u32[]{:S(2)}, u32[]{:S(2)}) collective-permute-start(f32[8,2048]{1,0:T(8,128)S(1)} %fusion.1), channel_id=1, source_target_pairs={{0,12},{4,8},{8,4},{12,0},{16,28},{20,24},{24,20},{28,16},{1,13},{... | collective-permute-start | bytes 196616 | tf_op jit(solution)/shard_map/ppermute | solution.py:271
  69.5 0.4 collective-permute-start.7
  69.9 0.3 collective-permute-start.6
  70.2 1.9 %collective-permute-done.8 = f32[8,2048]{1,0:T(8,128)S(1)} collective-permute-done((f32[8,2048]{1,0:T(8,128)S(1)}, f32[8,2048]{1,0:T(8,128)S(1)}, u32[]{:S(2)}, u32[]{:S(2)}) %collective-permute-start.8) | collective-permute-done | bytes 65568 | tf_op jit(solution)/shard_map/ppermute | solution.py:271
  72.1 1.7 %collective-permute-done.7 = f32[8,2048]{1,0:T(8,128)S(1)} collective-permute-done((f32[8,2048]{1,0:T(8,128)S(1)}, f32[8,2048]{1,0:T(8,128)S(1)}, u32[]{:S(2)}, u32[]{:S(2)}) %collective-permute-start.7) | collective-permute-done | bytes 65568 | tf_op jit(solution)/shard_map/ppermute | solution.py:271
  73.8 0.4 collective-permute-done.6
  74.2 2.7 %collective-permute-start.9 = (f32[8,2048]{1,0:T(8,128)S(1)}, f32[8,2048]{1,0:T(8,128)S(1)}, u32[]{:S(2)}, u32[]{:S(2)}) collective-permute-start(f32[8,2048]{1,0:T(8,128)S(1)} %add_add_fusion), channel_id=1, source_target_pairs={{0,16},{4,20},{8,24},{12,28},{16,0},{20,4},{24,8},{28,12},{1,17},{... | collective-permute-start | bytes 196616 | tf_op jit(solution)/shard_map/ppermute | solution.py:271
  76.9 2.6 %collective-permute-done.9 = f32[8,2048]{1,0:T(8,128)S(1)} collective-permute-done((f32[8,2048]{1,0:T(8,128)S(1)}, f32[8,2048]{1,0:T(8,128)S(1)}, u32[]{:S(2)}, u32[]{:S(2)}) %collective-permute-start.9) | collective-permute-done | bytes 65568 | tf_op jit(solution)/shard_map/ppermute | solution.py:271
  79.5 0.6 add.27
  (2 shorter events, 0.0 us)
Async XLA Ops:
  2.0 10.9 %collective-permute-start.2 = (f32[24,2048]{1,0:T(8,128)S(1)}, f32[24,2048]{1,0:T(8,128)S(1)}, u32[]{:S(2)}, u32[]{:S(2)}) collective-permute-start(f32[24,2048]{1,0:T(8,128)S(1)} %get-tuple-element.13.refs_0_), channel_id=1, source_target_pairs={{0,3},{1,2},{2,1},{3,0},{4,7},{5,6},{6,5},{7,4},{8,11},{9,10},{10,... | collective-permute-start | bytes 589832 | tf_op jit(solution)/shard_map/ppermute | solution.py:271
  4.5 9.7 %collective-permute-start.1 = (f32[24,2048]{1,0:T(8,128)S(1)}, f32[24,2048]{1,0:T(8,128)S(1)}, u32[]{:S(2)}, u32[]{:S(2)}) collective-permute-start(f32[24,2048]{1,0:T(8,128)S(1)} %get-tuple-element.13.refs_0_), channel_id=1, source_target_pairs={{0,2},{1,3},{2,0},{3,1},{4,6},{5,7},{6,4},{7,5},{8,10},{9,11},{10,... | collective-permute-start | bytes 589832 | tf_op jit(solution)/shard_map/ppermute | solution.py:271
  5.1 9.0 %collective-permute-start = (f32[24,2048]{1,0:T(8,128)S(1)}, f32[24,2048]{1,0:T(8,128)S(1)}, u32[]{:S(2)}, u32[]{:S(2)}) collective-permute-start(f32[24,2048]{1,0:T(8,128)S(1)} %get-tuple-element.13.refs_0_), channel_id=1, source_target_pairs={{0,1},{1,0},{2,3},{3,2},{4,5},{5,4},{6,7},{7,6},{8,9},{9,8},{10,11... | collective-permute-start | bytes 589832 | tf_op jit(solution)/shard_map/ppermute | solution.py:271
  55.5 11.1 %collective-permute-start.3 = (f32[8,2048]{1,0:T(8,128)S(1)}, f32[8,2048]{1,0:T(8,128)S(1)}, u32[]{:S(2)}, u32[]{:S(2)}) collective-permute-start(f32[8,2048]{1,0:T(8,128)S(1)} %get-tuple-element.20), channel_id=1, source_target_pairs={{0,1},{1,0},{2,3},{3,2},{4,5},{5,4},{6,7},{7,6},{8,9},{9,8},{10,11... | collective-permute-start | bytes 196616 | tf_op jit(solution)/shard_map/ppermute | solution.py:271
  55.6 11.0 %collective-permute-start.4 = (f32[8,2048]{1,0:T(8,128)S(1)}, f32[8,2048]{1,0:T(8,128)S(1)}, u32[]{:S(2)}, u32[]{:S(2)}) collective-permute-start(f32[8,2048]{1,0:T(8,128)S(1)} %get-tuple-element.21), channel_id=1, source_target_pairs={{0,2},{1,3},{2,0},{3,1},{4,6},{5,7},{6,4},{7,5},{8,10},{9,11},{10,... | collective-permute-start | bytes 196616 | tf_op jit(solution)/shard_map/ppermute | solution.py:271
  58.0 8.7 %collective-permute-start.5 = (f32[8,2048]{1,0:T(8,128)S(1)}, f32[8,2048]{1,0:T(8,128)S(1)}, u32[]{:S(2)}, u32[]{:S(2)}) collective-permute-start(f32[8,2048]{1,0:T(8,128)S(1)} %get-tuple-element.22), channel_id=1, source_target_pairs={{0,3},{1,2},{2,1},{3,0},{4,7},{5,6},{6,5},{7,4},{8,11},{9,10},{10,... | collective-permute-start | bytes 196616 | tf_op jit(solution)/shard_map/ppermute | solution.py:271
  66.7 5.4 %collective-permute-start.8 = (f32[8,2048]{1,0:T(8,128)S(1)}, f32[8,2048]{1,0:T(8,128)S(1)}, u32[]{:S(2)}, u32[]{:S(2)}) collective-permute-start(f32[8,2048]{1,0:T(8,128)S(1)} %fusion.1), channel_id=1, source_target_pairs={{0,12},{4,8},{8,4},{12,0},{16,28},{20,24},{24,20},{28,16},{1,13},{... | collective-permute-start | bytes 196616 | tf_op jit(solution)/shard_map/ppermute | solution.py:271
  69.5 4.3 %collective-permute-start.7 = (f32[8,2048]{1,0:T(8,128)S(1)}, f32[8,2048]{1,0:T(8,128)S(1)}, u32[]{:S(2)}, u32[]{:S(2)}) collective-permute-start(f32[8,2048]{1,0:T(8,128)S(1)} %fusion.1), channel_id=1, source_target_pairs={{0,8},{4,12},{8,0},{12,4},{16,24},{20,28},{24,16},{28,20},{1,9},{5... | collective-permute-start | bytes 196616 | tf_op jit(solution)/shard_map/ppermute | solution.py:271
  69.9 4.3 %collective-permute-start.6 = (f32[8,2048]{1,0:T(8,128)S(1)}, f32[8,2048]{1,0:T(8,128)S(1)}, u32[]{:S(2)}, u32[]{:S(2)}) collective-permute-start(f32[8,2048]{1,0:T(8,128)S(1)} %fusion.1), channel_id=1, source_target_pairs={{0,4},{4,0},{8,12},{12,8},{16,20},{20,16},{24,28},{28,24},{1,5},{5... | collective-permute-start | bytes 196616 | tf_op jit(solution)/shard_map/ppermute | solution.py:271
  74.2 5.2 %collective-permute-start.9 = (f32[8,2048]{1,0:T(8,128)S(1)}, f32[8,2048]{1,0:T(8,128)S(1)}, u32[]{:S(2)}, u32[]{:S(2)}) collective-permute-start(f32[8,2048]{1,0:T(8,128)S(1)} %add_add_fusion), channel_id=1, source_target_pairs={{0,16},{4,20},{8,24},{12,28},{16,0},{20,4},{24,8},{28,12},{1,17},{... | collective-permute-start | bytes 196616 | tf_op jit(solution)/shard_map/ppermute | solution.py:271

commit v6 on v5

--- a/solution.py
+++ b/solution.py
@@ -15,7 +15,7 @@
 COLS = 256
 FLIP_ROUND = 2
 FLIP_HI = 2
-AHEAD = 2
+AHEAD = 4
 
 
 def round_bf16(x):
@@ -290,7 +290,7 @@
     )
     pieces = [exchange(own, "narrow", k) for k in range(1, narrow)]
     call = functools.partial(tile_call, bst=bst, w=w)
-    first = count // 2
+    first = count // 4 * 3
     fwd_a, total = call([own], 0, first, None)
     others, total = call(pieces, 0, count, total)
     received = [exchange(fwd, "narrow", k + 1) for k, fwd in enumerate(others)]

time: 80.2 us -> 77.8 us (0.970)
  waiting for transfers between devices: 7.79 us -> 6.61 us
    ppermute x10, waiting for transfers between devices: 7.79 us -> 6.61 us  [exchange(): return lax.ppermute(x, axis, [(k, k ^ distance) for k in range(size)])]
  transfers between devices with their start and end apart: 10 -> 10, of which waited for: 5 -> 4; matrix products, arithmetic and copies ran while one was open for 0% -> 0% of each run, Pallas kernels for 20% -> 20%
where the time goes in v6:
time: 77.8 us; the launch traced here: 77.6 us
  Pallas kernels  58.4 us (75%)
  starting transfers between devices  11.3 us (15%)
  waiting for transfers between devices  6.61 us (8%)
    pallas_call x3, Pallas kernels, tile_call(): pl.pallas_call(kernel, out_shape=tuple(outs), in_specs=[VMEM] * len(args)...  57 us
    ppermute x10, starting transfers between devices, exchange(): return lax.ppermute(x, axis, [(k, k ^ distance) for k in range(size)])  11.3 us
    ppermute x10, waiting for transfers between devices, exchange(): return lax.ppermute(x, axis, [(k, k ^ distance) for k in range(size)])  6.61 us
  transfers between devices with their start and end apart: 10, of which 4 were waited for; matrix products, arithmetic and copies ran while one was open for 0% of the time, Pallas kernels for 20%

profile of v6, /device:TPU:0, one launch (start us, length us, event | category | flops | bytes accessed | tf_op | source)
XLA Modules:
  0.0 77.6 jit_solution(12207534049231358631)
XLA Ops:
  0.6 1.4 %prepare.1 = (bf16[128,4096]{1,0:T(8,128)(2,1)S(1)}, bf16[16,4096]{1,0:T(8,128)(2,1)S(1)}, f32[24,2048]{1,0:T(8,128)S(1)}) custom-call(f32[16,4096]{1,0:T(8,128)} %refs_0_.1, f32[8,4096]{1,0:T(8,128)} %refs_1_.1, f32[16,2048]{1,0:T(8,128)} %refs_2_.1, f32[8,2048]{1,0:T(8,128)} %refs_3_.1, f32[1,16]{1,0:T(1,128)} %bitcast.2, f32[1,8]{1,0:T(1,128)} %bitcast.3), custom_call_target="tpu_custom_call" | custom-call | tf_op jit(solution)/shard_map/prepare/pallas_call | solution.py:210
  2.0 2.4 %collective-permute-start.2 = (f32[24,2048]{1,0:T(8,128)S(1)}, f32[24,2048]{1,0:T(8,128)S(1)}, u32[]{:S(2)}, u32[]{:S(2)}) collective-permute-start(f32[24,2048]{1,0:T(8,128)S(1)} %get-tuple-element.13.refs_0_), channel_id=1, source_target_pairs={{0,3},{1,2},{2,1},{3,0},{4,7},{5,6},{6,5},{7,4},{8,11},{9,10},{10,... | collective-permute-start | bytes 589832 | tf_op jit(solution)/shard_map/ppermute | solution.py:271
  4.5 0.6 collective-permute-start.1
  5.1 0.0 collective-permute-start
  5.2 11.2 %covariance_tiles.3 = (f32[8,1536]{1,0:T(8,128)S(1)}, f32[8,4096]{1,0:T(8,128)S(1)}) custom-call(f32[24,2048]{1,0:T(8,128)S(1)} %get-tuple-element.13.refs_0_, bf16[128,4096]{1,0:T(8,128)(2,1)S(1)} %get-tuple-element.14.refs_1_.refs_3_, bf16[16,4096]{1,0:T(8,128)(2,1)S(1)} %get-tuple-element.15.refs_2_.refs_4_), custom_call_target="tpu_custom_call" | custom-call | flops 16106127360 | bytes 2244608 | tf_op jit(solution)/shard_map/covariance_tiles/pallas_call | solution.py:240
  16.3 0.0 collective-permute-done.2.refs_2_
  16.3 0.0 collective-permute-done.1.refs_1_
  16.3 0.0 collective-permute-done.refs_0_
  16.4 41.4 %covariance_tiles.4 = (f32[8,2048]{1,0:T(8,128)S(1)}, f32[8,2048]{1,0:T(8,128)S(1)}, f32[8,2048]{1,0:T(8,128)S(1)}, f32[8,4096]{1,0:T(8,128)S(1)}) custom-call(f32[24,2048]{1,0:T(8,128)S(1)} %collective-permute-done.refs_0_, f32[24,2048]{1,0:T(8,128)S(1)} %collective-permute-done.1.refs_1_, f32[24,2048]{1,0:T(8,128)S(1)} %collective-permute-done.2.refs_2_, ...), custom_call_target="tpu_custom_call" | custom-call | flops 64424509440 | bytes 2686976 | tf_op jit(solution)/shard_map/covariance_tiles/pallas_call | solution.py:240
  57.8 0.5 collective-permute-start.3
  58.3 1.4 %collective-permute-start.4 = (f32[8,2048]{1,0:T(8,128)S(1)}, f32[8,2048]{1,0:T(8,128)S(1)}, u32[]{:S(2)}, u32[]{:S(2)}) collective-permute-start(f32[8,2048]{1,0:T(8,128)S(1)} %get-tuple-element.21), channel_id=1, source_target_pairs={{0,2},{1,3},{2,0},{3,1},{4,6},{5,7},{6,4},{7,5},{8,10},{9,11},{10,... | collective-permute-start | bytes 196616 | tf_op jit(solution)/shard_map/ppermute | solution.py:271
  59.7 0.1 collective-permute-start.5
  59.8 4.4 %covariance_tiles.5 = (f32[8,512]{1,0:T(8,128)S(1)}, f32[8,4096]{1,0:T(8,128)}) custom-call(f32[24,2048]{1,0:T(8,128)S(1)} %get-tuple-element.13.refs_0_, bf16[128,4096]{1,0:T(8,128)(2,1)S(1)} %get-tuple-element.14.refs_1_.refs_3_, bf16[16,4096]{1,0:T(8,128)(2,1)S(1)} %get-tuple-element.15.refs_2_.refs_4_, f32[8,4096]{1,0:T(8,128)S(1)} %get-tuple-element.18.refs_3_), custom_call_target="tpu_custom_call" | custom-call | flops 5368709120 | bytes 2146304 | tf_op jit(solution)/shard_map/covariance_tiles/pallas_call | solution.py:240
  64.1 0.0 collective-permute-done.3
  64.1 0.0 collective-permute-done.4
  64.2 0.0 collective-permute-done.5
  64.2 2.8 %collective-permute-start.8 = (f32[8,2048]{1,0:T(8,128)S(1)}, f32[8,2048]{1,0:T(8,128)S(1)}, u32[]{:S(2)}, u32[]{:S(2)}) collective-permute-start(f32[8,2048]{1,0:T(8,128)S(1)} %fusion.1), channel_id=1, source_target_pairs={{0,12},{4,8},{8,4},{12,0},{16,28},{20,24},{24,20},{28,16},{1,13},{... | collective-permute-start | bytes 196616 | tf_op jit(solution)/shard_map/ppermute | solution.py:271
  67.0 0.4 collective-permute-start.7
  67.4 0.3 collective-permute-start.6
  67.7 2.2 %collective-permute-done.8 = f32[8,2048]{1,0:T(8,128)S(1)} collective-permute-done((f32[8,2048]{1,0:T(8,128)S(1)}, f32[8,2048]{1,0:T(8,128)S(1)}, u32[]{:S(2)}, u32[]{:S(2)}) %collective-permute-start.8) | collective-permute-done | bytes 65568 | tf_op jit(solution)/shard_map/ppermute | solution.py:271
  69.9 1.4 %collective-permute-done.7 = f32[8,2048]{1,0:T(8,128)S(1)} collective-permute-done((f32[8,2048]{1,0:T(8,128)S(1)}, f32[8,2048]{1,0:T(8,128)S(1)}, u32[]{:S(2)}, u32[]{:S(2)}) %collective-permute-start.7) | collective-permute-done | bytes 65568 | tf_op jit(solution)/shard_map/ppermute | solution.py:271
  71.3 0.4 collective-permute-done.6
  71.7 2.7 %collective-permute-start.9 = (f32[8,2048]{1,0:T(8,128)S(1)}, f32[8,2048]{1,0:T(8,128)S(1)}, u32[]{:S(2)}, u32[]{:S(2)}) collective-permute-start(f32[8,2048]{1,0:T(8,128)S(1)} %add_add_fusion), channel_id=1, source_target_pairs={{0,16},{4,20},{8,24},{12,28},{16,0},{20,4},{24,8},{28,12},{1,17},{... | collective-permute-start | bytes 196616 | tf_op jit(solution)/shard_map/ppermute | solution.py:271
  74.4 2.6 %collective-permute-done.9 = f32[8,2048]{1,0:T(8,128)S(1)} collective-permute-done((f32[8,2048]{1,0:T(8,128)S(1)}, f32[8,2048]{1,0:T(8,128)S(1)}, u32[]{:S(2)}, u32[]{:S(2)}) %collective-permute-start.9) | collective-permute-done | bytes 65568 | tf_op jit(solution)/shard_map/ppermute | solution.py:271
  77.0 0.6 add.27
  (2 shorter events, 0.0 us)
Async XLA Ops:
  2.0 14.3 %collective-permute-start.2 = (f32[24,2048]{1,0:T(8,128)S(1)}, f32[24,2048]{1,0:T(8,128)S(1)}, u32[]{:S(2)}, u32[]{:S(2)}) collective-permute-start(f32[24,2048]{1,0:T(8,128)S(1)} %get-tuple-element.13.refs_0_), channel_id=1, source_target_pairs={{0,3},{1,2},{2,1},{3,0},{4,7},{5,6},{6,5},{7,4},{8,11},{9,10},{10,... | collective-permute-start | bytes 589832 | tf_op jit(solution)/shard_map/ppermute | solution.py:271
  4.5 11.9 %collective-permute-start.1 = (f32[24,2048]{1,0:T(8,128)S(1)}, f32[24,2048]{1,0:T(8,128)S(1)}, u32[]{:S(2)}, u32[]{:S(2)}) collective-permute-start(f32[24,2048]{1,0:T(8,128)S(1)} %get-tuple-element.13.refs_0_), channel_id=1, source_target_pairs={{0,2},{1,3},{2,0},{3,1},{4,6},{5,7},{6,4},{7,5},{8,10},{9,11},{10,... | collective-permute-start | bytes 589832 | tf_op jit(solution)/shard_map/ppermute | solution.py:271
  5.1 11.2 %collective-permute-start = (f32[24,2048]{1,0:T(8,128)S(1)}, f32[24,2048]{1,0:T(8,128)S(1)}, u32[]{:S(2)}, u32[]{:S(2)}) collective-permute-start(f32[24,2048]{1,0:T(8,128)S(1)} %get-tuple-element.13.refs_0_), channel_id=1, source_target_pairs={{0,1},{1,0},{2,3},{3,2},{4,5},{5,4},{6,7},{7,6},{8,9},{9,8},{10,11... | collective-permute-start | bytes 589832 | tf_op jit(solution)/shard_map/ppermute | solution.py:271
  57.8 6.3 %collective-permute-start.3 = (f32[8,2048]{1,0:T(8,128)S(1)}, f32[8,2048]{1,0:T(8,128)S(1)}, u32[]{:S(2)}, u32[]{:S(2)}) collective-permute-start(f32[8,2048]{1,0:T(8,128)S(1)} %get-tuple-element.20), channel_id=1, source_target_pairs={{0,1},{1,0},{2,3},{3,2},{4,5},{5,4},{6,7},{7,6},{8,9},{9,8},{10,11... | collective-permute-start | bytes 196616 | tf_op jit(solution)/shard_map/ppermute | solution.py:271
  58.3 5.8 %collective-permute-start.4 = (f32[8,2048]{1,0:T(8,128)S(1)}, f32[8,2048]{1,0:T(8,128)S(1)}, u32[]{:S(2)}, u32[]{:S(2)}) collective-permute-start(f32[8,2048]{1,0:T(8,128)S(1)} %get-tuple-element.21), channel_id=1, source_target_pairs={{0,2},{1,3},{2,0},{3,1},{4,6},{5,7},{6,4},{7,5},{8,10},{9,11},{10,... | collective-permute-start | bytes 196616 | tf_op jit(solution)/shard_map/ppermute | solution.py:271
  59.7 4.4 %collective-permute-start.5 = (f32[8,2048]{1,0:T(8,128)S(1)}, f32[8,2048]{1,0:T(8,128)S(1)}, u32[]{:S(2)}, u32[]{:S(2)}) collective-permute-start(f32[8,2048]{1,0:T(8,128)S(1)} %get-tuple-element.22), channel_id=1, source_target_pairs={{0,3},{1,2},{2,1},{3,0},{4,7},{5,6},{6,5},{7,4},{8,11},{9,10},{10,... | collective-permute-start | bytes 196616 | tf_op jit(solution)/shard_map/ppermute | solution.py:271
  64.2 5.8 %collective-permute-start.8 = (f32[8,2048]{1,0:T(8,128)S(1)}, f32[8,2048]{1,0:T(8,128)S(1)}, u32[]{:S(2)}, u32[]{:S(2)}) collective-permute-start(f32[8,2048]{1,0:T(8,128)S(1)} %fusion.1), channel_id=1, source_target_pairs={{0,12},{4,8},{8,4},{12,0},{16,28},{20,24},{24,20},{28,16},{1,13},{... | collective-permute-start | bytes 196616 | tf_op jit(solution)/shard_map/ppermute | solution.py:271
  67.0 4.3 %collective-permute-start.7 = (f32[8,2048]{1,0:T(8,128)S(1)}, f32[8,2048]{1,0:T(8,128)S(1)}, u32[]{:S(2)}, u32[]{:S(2)}) collective-permute-start(f32[8,2048]{1,0:T(8,128)S(1)} %fusion.1), channel_id=1, source_target_pairs={{0,8},{4,12},{8,0},{12,4},{16,24},{20,28},{24,16},{28,20},{1,9},{5... | collective-permute-start | bytes 196616 | tf_op jit(solution)/shard_map/ppermute | solution.py:271
  67.4 4.3 %collective-permute-start.6 = (f32[8,2048]{1,0:T(8,128)S(1)}, f32[8,2048]{1,0:T(8,128)S(1)}, u32[]{:S(2)}, u32[]{:S(2)}) collective-permute-start(f32[8,2048]{1,0:T(8,128)S(1)} %fusion.1), channel_id=1, source_target_pairs={{0,4},{4,0},{8,12},{12,8},{16,20},{20,16},{24,28},{28,24},{1,5},{5... | collective-permute-start | bytes 196616 | tf_op jit(solution)/shard_map/ppermute | solution.py:271
  71.7 5.3 %collective-permute-start.9 = (f32[8,2048]{1,0:T(8,128)S(1)}, f32[8,2048]{1,0:T(8,128)S(1)}, u32[]{:S(2)}, u32[]{:S(2)}) collective-permute-start(f32[8,2048]{1,0:T(8,128)S(1)} %add_add_fusion), channel_id=1, source_target_pairs={{0,16},{4,20},{8,24},{12,28},{16,0},{20,4},{24,8},{28,12},{1,17},{... | collective-permute-start | bytes 196616 | tf_op jit(solution)/shard_map/ppermute | solution.py:271

commit v7 on v6

--- a/solution.py
+++ b/solution.py
@@ -166,27 +166,29 @@
         return jnp.concatenate([u, u], axis=1)
 
     starts = range(0, half, COLS)
-    made = [(0, 1), (1, 0), (1, 1), (0, 0)]
+    ahead = min(AHEAD, len(starts) - 1)
+    turn = 4 if blocks % 4 == 0 else 2
+    made = [(slot % 2, part) for k in range(turn) for slot, part in ((k, 1), (k + 1, 0))]
     makes = [(slot, part, start) for slot, part in made for start in starts]
-    uses = [(k, part, start) for k in range(2) for part in range(2) for start in starts]
+    uses = [(k, part, start) for k in range(turn) for part in range(2) for start in starts]
 
     prep(0, 0)
     for start in starts:
         produce(0, 0, start)
 
-    @pl.loop(0, blocks // 2)
-    def _(pair):
-        block = pair * 2
-        prep(block + 1, 1)
-        us = [vectors(block), vectors(block + 1)]
-        fwds = [jnp.zeros((16, ROWS), F32)] * 2
-        for n in range(len(makes) + AHEAD):
-            if n == len(makes) // 2:
-                prep(jnp.minimum(block + 2, blocks - 1), 0)
+    @pl.loop(0, blocks // turn)
+    def _(index):
+        block = index * turn
+        us = [vectors(block + k) for k in range(turn)]
+        fwds = [jnp.zeros((16, ROWS), F32)] * turn
+        for n in range(len(makes) + ahead):
+            k, rest = divmod(n, 2 * len(starts))
+            if rest == 0 and k < turn:
+                prep(jnp.minimum(block + k + 1, blocks - 1), (k + 1) % 2)
             if n < len(makes):
                 produce(*makes[n])
-            if n >= AHEAD:
-                k, part, start = uses[n - AHEAD]
+            if n >= ahead:
+                k, part, start = uses[n - ahead]
                 fwds[k] = consume(part, start, us[k], fwds[k])
         if want_fwd:
             for k, fwd in enumerate(fwds):

time: 77.8 us -> 76.9 us (0.988)
  Pallas kernels: 58.4 us -> 57.5 us
    pallas_call x3, Pallas kernels: 57 us -> 56.1 us  [tile_call(): pl.pallas_call(kernel, out_shape=tuple(outs), in_specs=[VMEM] * len(args)...]
where the time goes in v7:
time: 76.9 us; the launch traced here: 76.8 us
  Pallas kernels  57.5 us (75%)
  starting transfers between devices  11.3 us (15%)
  waiting for transfers between devices  6.63 us (9%)
    pallas_call x3, Pallas kernels, tile_call(): pl.pallas_call(kernel, out_shape=tuple(outs), in_specs=[VMEM] * len(args)...  56.1 us
    ppermute x10, starting transfers between devices, exchange(): return lax.ppermute(x, axis, [(k, k ^ distance) for k in range(size)])  11.3 us
    ppermute x10, waiting for transfers between devices, exchange(): return lax.ppermute(x, axis, [(k, k ^ distance) for k in range(size)])  6.63 us
  transfers between devices with their start and end apart: 10, of which 4 were waited for; matrix products, arithmetic and copies ran while one was open for 0% of the time, Pallas kernels for 20%

profile of v7, /device:TPU:0, one launch (start us, length us, event | category | flops | bytes accessed | tf_op | source)
XLA Modules:
  0.0 76.8 jit_solution(10380056211260133060)
XLA Ops:
  0.6 1.4 %prepare.1 = (bf16[128,4096]{1,0:T(8,128)(2,1)S(1)}, bf16[16,4096]{1,0:T(8,128)(2,1)S(1)}, f32[24,2048]{1,0:T(8,128)S(1)}) custom-call(f32[16,4096]{1,0:T(8,128)} %refs_0_.1, f32[8,4096]{1,0:T(8,128)} %refs_1_.1, f32[16,2048]{1,0:T(8,128)} %refs_2_.1, f32[8,2048]{1,0:T(8,128)} %refs_3_.1, f32[1,16]{1,0:T(1,128)} %bitcast.2, f32[1,8]{1,0:T(1,128)} %bitcast.3), custom_call_target="tpu_custom_call" | custom-call | tf_op jit(solution)/shard_map/prepare/pallas_call | solution.py:212
  2.0 2.4 %collective-permute-start.2 = (f32[24,2048]{1,0:T(8,128)S(1)}, f32[24,2048]{1,0:T(8,128)S(1)}, u32[]{:S(2)}, u32[]{:S(2)}) collective-permute-start(f32[24,2048]{1,0:T(8,128)S(1)} %get-tuple-element.13.refs_0_), channel_id=1, source_target_pairs={{0,3},{1,2},{2,1},{3,0},{4,7},{5,6},{6,5},{7,4},{8,11},{9,10},{10,... | collective-permute-start | bytes 589832 | tf_op jit(solution)/shard_map/ppermute | solution.py:273
  4.5 0.6 collective-permute-start.1
  5.1 0.0 collective-permute-start
  5.2 11.1 %covariance_tiles.3 = (f32[8,1536]{1,0:T(8,128)S(1)}, f32[8,4096]{1,0:T(8,128)S(1)}) custom-call(f32[24,2048]{1,0:T(8,128)S(1)} %get-tuple-element.13.refs_0_, bf16[128,4096]{1,0:T(8,128)(2,1)S(1)} %get-tuple-element.14.refs_1_.refs_3_, bf16[16,4096]{1,0:T(8,128)(2,1)S(1)} %get-tuple-element.15.refs_2_.refs_4_), custom_call_target="tpu_custom_call" | custom-call | flops 16106127360 | bytes 2244608 | tf_op jit(solution)/shard_map/covariance_tiles/pallas_call | solution.py:242
  16.3 0.0 collective-permute-done.2.refs_2_
  16.3 0.0 collective-permute-done.1.refs_1_
  16.3 0.0 collective-permute-done.refs_0_
  16.3 40.5 %covariance_tiles.4 = (f32[8,2048]{1,0:T(8,128)S(1)}, f32[8,2048]{1,0:T(8,128)S(1)}, f32[8,2048]{1,0:T(8,128)S(1)}, f32[8,4096]{1,0:T(8,128)S(1)}) custom-call(f32[24,2048]{1,0:T(8,128)S(1)} %collective-permute-done.refs_0_, f32[24,2048]{1,0:T(8,128)S(1)} %collective-permute-done.1.refs_1_, f32[24,2048]{1,0:T(8,128)S(1)} %collective-permute-done.2.refs_2_, ...), custom_call_target="tpu_custom_call" | custom-call | flops 64424509440 | bytes 2686976 | tf_op jit(solution)/shard_map/covariance_tiles/pallas_call | solution.py:242
  56.9 0.5 collective-permute-start.3
  57.4 1.4 %collective-permute-start.4 = (f32[8,2048]{1,0:T(8,128)S(1)}, f32[8,2048]{1,0:T(8,128)S(1)}, u32[]{:S(2)}, u32[]{:S(2)}) collective-permute-start(f32[8,2048]{1,0:T(8,128)S(1)} %get-tuple-element.21), channel_id=1, source_target_pairs={{0,2},{1,3},{2,0},{3,1},{4,6},{5,7},{6,4},{7,5},{8,10},{9,11},{10,... | collective-permute-start | bytes 196616 | tf_op jit(solution)/shard_map/ppermute | solution.py:273
  58.8 0.1 collective-permute-start.5
  58.9 4.4 %covariance_tiles.5 = (f32[8,512]{1,0:T(8,128)S(1)}, f32[8,4096]{1,0:T(8,128)}) custom-call(f32[24,2048]{1,0:T(8,128)S(1)} %get-tuple-element.13.refs_0_, bf16[128,4096]{1,0:T(8,128)(2,1)S(1)} %get-tuple-element.14.refs_1_.refs_3_, bf16[16,4096]{1,0:T(8,128)(2,1)S(1)} %get-tuple-element.15.refs_2_.refs_4_, f32[8,4096]{1,0:T(8,128)S(1)} %get-tuple-element.18.refs_3_), custom_call_target="tpu_custom_call" | custom-call | flops 5368709120 | bytes 2146304 | tf_op jit(solution)/shard_map/covariance_tiles/pallas_call | solution.py:242
  63.2 0.0 collective-permute-done.3
  63.2 0.0 collective-permute-done.4
  63.3 0.0 collective-permute-done.5
  63.3 2.8 %collective-permute-start.8 = (f32[8,2048]{1,0:T(8,128)S(1)}, f32[8,2048]{1,0:T(8,128)S(1)}, u32[]{:S(2)}, u32[]{:S(2)}) collective-permute-start(f32[8,2048]{1,0:T(8,128)S(1)} %fusion.1), channel_id=1, source_target_pairs={{0,12},{4,8},{8,4},{12,0},{16,28},{20,24},{24,20},{28,16},{1,13},{... | collective-permute-start | bytes 196616 | tf_op jit(solution)/shard_map/ppermute | solution.py:273
  66.1 0.4 collective-permute-start.7
  66.5 0.3 collective-permute-start.6
  66.8 2.2 %collective-permute-done.8 = f32[8,2048]{1,0:T(8,128)S(1)} collective-permute-done((f32[8,2048]{1,0:T(8,128)S(1)}, f32[8,2048]{1,0:T(8,128)S(1)}, u32[]{:S(2)}, u32[]{:S(2)}) %collective-permute-start.8) | collective-permute-done | bytes 65568 | tf_op jit(solution)/shard_map/ppermute | solution.py:273
  69.1 1.4 %collective-permute-done.7 = f32[8,2048]{1,0:T(8,128)S(1)} collective-permute-done((f32[8,2048]{1,0:T(8,128)S(1)}, f32[8,2048]{1,0:T(8,128)S(1)}, u32[]{:S(2)}, u32[]{:S(2)}) %collective-permute-start.7) | collective-permute-done | bytes 65568 | tf_op jit(solution)/shard_map/ppermute | solution.py:273
  70.4 0.4 collective-permute-done.6
  70.8 2.7 %collective-permute-start.9 = (f32[8,2048]{1,0:T(8,128)S(1)}, f32[8,2048]{1,0:T(8,128)S(1)}, u32[]{:S(2)}, u32[]{:S(2)}) collective-permute-start(f32[8,2048]{1,0:T(8,128)S(1)} %add_add_fusion), channel_id=1, source_target_pairs={{0,16},{4,20},{8,24},{12,28},{16,0},{20,4},{24,8},{28,12},{1,17},{... | collective-permute-start | bytes 196616 | tf_op jit(solution)/shard_map/ppermute | solution.py:273
  73.5 2.7 %collective-permute-done.9 = f32[8,2048]{1,0:T(8,128)S(1)} collective-permute-done((f32[8,2048]{1,0:T(8,128)S(1)}, f32[8,2048]{1,0:T(8,128)S(1)}, u32[]{:S(2)}, u32[]{:S(2)}) %collective-permute-start.9) | collective-permute-done | bytes 65568 | tf_op jit(solution)/shard_map/ppermute | solution.py:273
  76.1 0.6 add.27
  (2 shorter events, 0.0 us)
Async XLA Ops:
  2.0 14.3 %collective-permute-start.2 = (f32[24,2048]{1,0:T(8,128)S(1)}, f32[24,2048]{1,0:T(8,128)S(1)}, u32[]{:S(2)}, u32[]{:S(2)}) collective-permute-start(f32[24,2048]{1,0:T(8,128)S(1)} %get-tuple-element.13.refs_0_), channel_id=1, source_target_pairs={{0,3},{1,2},{2,1},{3,0},{4,7},{5,6},{6,5},{7,4},{8,11},{9,10},{10,... | collective-permute-start | bytes 589832 | tf_op jit(solution)/shard_map/ppermute | solution.py:273
  4.5 11.8 %collective-permute-start.1 = (f32[24,2048]{1,0:T(8,128)S(1)}, f32[24,2048]{1,0:T(8,128)S(1)}, u32[]{:S(2)}, u32[]{:S(2)}) collective-permute-start(f32[24,2048]{1,0:T(8,128)S(1)} %get-tuple-element.13.refs_0_), channel_id=1, source_target_pairs={{0,2},{1,3},{2,0},{3,1},{4,6},{5,7},{6,4},{7,5},{8,10},{9,11},{10,... | collective-permute-start | bytes 589832 | tf_op jit(solution)/shard_map/ppermute | solution.py:273
  5.1 11.2 %collective-permute-start = (f32[24,2048]{1,0:T(8,128)S(1)}, f32[24,2048]{1,0:T(8,128)S(1)}, u32[]{:S(2)}, u32[]{:S(2)}) collective-permute-start(f32[24,2048]{1,0:T(8,128)S(1)} %get-tuple-element.13.refs_0_), channel_id=1, source_target_pairs={{0,1},{1,0},{2,3},{3,2},{4,5},{5,4},{6,7},{7,6},{8,9},{9,8},{10,11... | collective-permute-start | bytes 589832 | tf_op jit(solution)/shard_map/ppermute | solution.py:273
  56.9 6.4 %collective-permute-start.3 = (f32[8,2048]{1,0:T(8,128)S(1)}, f32[8,2048]{1,0:T(8,128)S(1)}, u32[]{:S(2)}, u32[]{:S(2)}) collective-permute-start(f32[8,2048]{1,0:T(8,128)S(1)} %get-tuple-element.20), channel_id=1, source_target_pairs={{0,1},{1,0},{2,3},{3,2},{4,5},{5,4},{6,7},{7,6},{8,9},{9,8},{10,11... | collective-permute-start | bytes 196616 | tf_op jit(solution)/shard_map/ppermute | solution.py:273
  57.4 5.8 %collective-permute-start.4 = (f32[8,2048]{1,0:T(8,128)S(1)}, f32[8,2048]{1,0:T(8,128)S(1)}, u32[]{:S(2)}, u32[]{:S(2)}) collective-permute-start(f32[8,2048]{1,0:T(8,128)S(1)} %get-tuple-element.21), channel_id=1, source_target_pairs={{0,2},{1,3},{2,0},{3,1},{4,6},{5,7},{6,4},{7,5},{8,10},{9,11},{10,... | collective-permute-start | bytes 196616 | tf_op jit(solution)/shard_map/ppermute | solution.py:273
  58.8 4.4 %collective-permute-start.5 = (f32[8,2048]{1,0:T(8,128)S(1)}, f32[8,2048]{1,0:T(8,128)S(1)}, u32[]{:S(2)}, u32[]{:S(2)}) collective-permute-start(f32[8,2048]{1,0:T(8,128)S(1)} %get-tuple-element.22), channel_id=1, source_target_pairs={{0,3},{1,2},{2,1},{3,0},{4,7},{5,6},{6,5},{7,4},{8,11},{9,10},{10,... | collective-permute-start | bytes 196616 | tf_op jit(solution)/shard_map/ppermute | solution.py:273
  63.3 5.8 %collective-permute-start.8 = (f32[8,2048]{1,0:T(8,128)S(1)}, f32[8,2048]{1,0:T(8,128)S(1)}, u32[]{:S(2)}, u32[]{:S(2)}) collective-permute-start(f32[8,2048]{1,0:T(8,128)S(1)} %fusion.1), channel_id=1, source_target_pairs={{0,12},{4,8},{8,4},{12,0},{16,28},{20,24},{24,20},{28,16},{1,13},{... | collective-permute-start | bytes 196616 | tf_op jit(solution)/shard_map/ppermute | solution.py:273
  66.1 4.3 %collective-permute-start.7 = (f32[8,2048]{1,0:T(8,128)S(1)}, f32[8,2048]{1,0:T(8,128)S(1)}, u32[]{:S(2)}, u32[]{:S(2)}) collective-permute-start(f32[8,2048]{1,0:T(8,128)S(1)} %fusion.1), channel_id=1, source_target_pairs={{0,8},{4,12},{8,0},{12,4},{16,24},{20,28},{24,16},{28,20},{1,9},{5... | collective-permute-start | bytes 196616 | tf_op jit(solution)/shard_map/ppermute | solution.py:273
  66.5 4.3 %collective-permute-start.6 = (f32[8,2048]{1,0:T(8,128)S(1)}, f32[8,2048]{1,0:T(8,128)S(1)}, u32[]{:S(2)}, u32[]{:S(2)}) collective-permute-start(f32[8,2048]{1,0:T(8,128)S(1)} %fusion.1), channel_id=1, source_target_pairs={{0,4},{4,0},{8,12},{12,8},{16,20},{20,16},{24,28},{28,24},{1,5},{5... | collective-permute-start | bytes 196616 | tf_op jit(solution)/shard_map/ppermute | solution.py:273
  70.8 5.3 %collective-permute-start.9 = (f32[8,2048]{1,0:T(8,128)S(1)}, f32[8,2048]{1,0:T(8,128)S(1)}, u32[]{:S(2)}, u32[]{:S(2)}) collective-permute-start(f32[8,2048]{1,0:T(8,128)S(1)} %add_add_fusion), channel_id=1, source_target_pairs={{0,16},{4,20},{8,24},{12,28},{16,0},{20,4},{24,8},{28,12},{1,17},{... | collective-permute-start | bytes 196616 | tf_op jit(solution)/shard_map/ppermute | solution.py:273

commit v8 on v7

--- a/solution.py
+++ b/solution.py
@@ -13,8 +13,8 @@
 DEPTH = 128
 ROWS = 256
 COLS = 256
-FLIP_ROUND = 2
-FLIP_HI = 2
+FLIP_ROUND = 4
+FLIP_HI = 3
 AHEAD = 4
 
 

time: 76.9 us -> 79.7 us (1.036)
  Pallas kernels: 57.5 us -> 60.3 us
    pallas_call x3, Pallas kernels: 56.1 us -> 58.9 us  [tile_call(): pl.pallas_call(kernel, out_shape=tuple(outs), in_specs=[VMEM] * len(args)...]
where the time goes in v8:
time: 79.7 us; the launch traced here: 79.6 us
  Pallas kernels  60.3 us (76%)
  starting transfers between devices  11.3 us (14%)
  waiting for transfers between devices  6.62 us (8%)
    pallas_call x3, Pallas kernels, tile_call(): pl.pallas_call(kernel, out_shape=tuple(outs), in_specs=[VMEM] * len(args)...  58.9 us
    ppermute x10, starting transfers between devices, exchange(): return lax.ppermute(x, axis, [(k, k ^ distance) for k in range(size)])  11.3 us
    ppermute x10, waiting for transfers between devices, exchange(): return lax.ppermute(x, axis, [(k, k ^ distance) for k in range(size)])  6.62 us
  transfers between devices with their start and end apart: 10, of which 4 were waited for; matrix products, arithmetic and copies ran while one was open for 0% of the time, Pallas kernels for 20%

profile of v8, /device:TPU:0, one launch (start us, length us, event | category | flops | bytes accessed | tf_op | source)
XLA Modules:
  0.0 79.6 jit_solution(11798326557324442524)
XLA Ops:
  0.6 1.4 %prepare.1 = (bf16[128,4096]{1,0:T(8,128)(2,1)S(1)}, bf16[16,4096]{1,0:T(8,128)(2,1)S(1)}, f32[24,2048]{1,0:T(8,128)S(1)}) custom-call(f32[16,4096]{1,0:T(8,128)} %refs_0_.1, f32[8,4096]{1,0:T(8,128)} %refs_1_.1, f32[16,2048]{1,0:T(8,128)} %refs_2_.1, f32[8,2048]{1,0:T(8,128)} %refs_3_.1, f32[1,16]{1,0:T(1,128)} %bitcast.2, f32[1,8]{1,0:T(1,128)} %bitcast.3), custom_call_target="tpu_custom_call" | custom-call | tf_op jit(solution)/shard_map/prepare/pallas_call | solution.py:212
  2.0 2.4 %collective-permute-start.2 = (f32[24,2048]{1,0:T(8,128)S(1)}, f32[24,2048]{1,0:T(8,128)S(1)}, u32[]{:S(2)}, u32[]{:S(2)}) collective-permute-start(f32[24,2048]{1,0:T(8,128)S(1)} %get-tuple-element.13.refs_0_), channel_id=1, source_target_pairs={{0,3},{1,2},{2,1},{3,0},{4,7},{5,6},{6,5},{7,4},{8,11},{9,10},{10,... | collective-permute-start | bytes 589832 | tf_op jit(solution)/shard_map/ppermute | solution.py:273
  4.5 0.6 collective-permute-start.1
  5.1 0.0 collective-permute-start
  5.2 11.5 %covariance_tiles.3 = (f32[8,1536]{1,0:T(8,128)S(1)}, f32[8,4096]{1,0:T(8,128)S(1)}) custom-call(f32[24,2048]{1,0:T(8,128)S(1)} %get-tuple-element.13.refs_0_, bf16[128,4096]{1,0:T(8,128)(2,1)S(1)} %get-tuple-element.14.refs_1_.refs_3_, bf16[16,4096]{1,0:T(8,128)(2,1)S(1)} %get-tuple-element.15.refs_2_.refs_4_), custom_call_target="tpu_custom_call" | custom-call | flops 16106127360 | bytes 2244608 | tf_op jit(solution)/shard_map/covariance_tiles/pallas_call | solution.py:242
  16.6 0.0 collective-permute-done.2.refs_2_
  16.7 0.0 collective-permute-done.1.refs_1_
  16.7 0.0 collective-permute-done.refs_0_
  16.7 42.9 %covariance_tiles.4 = (f32[8,2048]{1,0:T(8,128)S(1)}, f32[8,2048]{1,0:T(8,128)S(1)}, f32[8,2048]{1,0:T(8,128)S(1)}, f32[8,4096]{1,0:T(8,128)S(1)}) custom-call(f32[24,2048]{1,0:T(8,128)S(1)} %collective-permute-done.refs_0_, f32[24,2048]{1,0:T(8,128)S(1)} %collective-permute-done.1.refs_1_, f32[24,2048]{1,0:T(8,128)S(1)} %collective-permute-done.2.refs_2_, ...), custom_call_target="tpu_custom_call" | custom-call | flops 64424509440 | bytes 2686976 | tf_op jit(solution)/shard_map/covariance_tiles/pallas_call | solution.py:242
  59.6 0.5 collective-permute-start.3
  60.1 1.4 %collective-permute-start.4 = (f32[8,2048]{1,0:T(8,128)S(1)}, f32[8,2048]{1,0:T(8,128)S(1)}, u32[]{:S(2)}, u32[]{:S(2)}) collective-permute-start(f32[8,2048]{1,0:T(8,128)S(1)} %get-tuple-element.21), channel_id=1, source_target_pairs={{0,2},{1,3},{2,0},{3,1},{4,6},{5,7},{6,4},{7,5},{8,10},{9,11},{10,... | collective-permute-start | bytes 196616 | tf_op jit(solution)/shard_map/ppermute | solution.py:273
  61.5 0.1 collective-permute-start.5
  61.5 4.5 %covariance_tiles.5 = (f32[8,512]{1,0:T(8,128)S(1)}, f32[8,4096]{1,0:T(8,128)}) custom-call(f32[24,2048]{1,0:T(8,128)S(1)} %get-tuple-element.13.refs_0_, bf16[128,4096]{1,0:T(8,128)(2,1)S(1)} %get-tuple-element.14.refs_1_.refs_3_, bf16[16,4096]{1,0:T(8,128)(2,1)S(1)} %get-tuple-element.15.refs_2_.refs_4_, f32[8,4096]{1,0:T(8,128)S(1)} %get-tuple-element.18.refs_3_), custom_call_target="tpu_custom_call" | custom-call | flops 5368709120 | bytes 2146304 | tf_op jit(solution)/shard_map/covariance_tiles/pallas_call | solution.py:242
  66.0 0.0 collective-permute-done.3
  66.1 0.0 collective-permute-done.4
  66.1 0.0 collective-permute-done.5
  66.1 2.8 %collective-permute-start.8 = (f32[8,2048]{1,0:T(8,128)S(1)}, f32[8,2048]{1,0:T(8,128)S(1)}, u32[]{:S(2)}, u32[]{:S(2)}) collective-permute-start(f32[8,2048]{1,0:T(8,128)S(1)} %fusion.1), channel_id=1, source_target_pairs={{0,12},{4,8},{8,4},{12,0},{16,28},{20,24},{24,20},{28,16},{1,13},{... | collective-permute-start | bytes 196616 | tf_op jit(solution)/shard_map/ppermute | solution.py:273
  68.9 0.4 collective-permute-start.7
  69.3 0.3 collective-permute-start.6
  69.6 2.2 %collective-permute-done.8 = f32[8,2048]{1,0:T(8,128)S(1)} collective-permute-done((f32[8,2048]{1,0:T(8,128)S(1)}, f32[8,2048]{1,0:T(8,128)S(1)}, u32[]{:S(2)}, u32[]{:S(2)}) %collective-permute-start.8) | collective-permute-done | bytes 65568 | tf_op jit(solution)/shard_map/ppermute | solution.py:273
  71.8 1.4 %collective-permute-done.7 = f32[8,2048]{1,0:T(8,128)S(1)} collective-permute-done((f32[8,2048]{1,0:T(8,128)S(1)}, f32[8,2048]{1,0:T(8,128)S(1)}, u32[]{:S(2)}, u32[]{:S(2)}) %collective-permute-start.7) | collective-permute-done | bytes 65568 | tf_op jit(solution)/shard_map/ppermute | solution.py:273
  73.2 0.4 collective-permute-done.6
  73.6 2.7 %collective-permute-start.9 = (f32[8,2048]{1,0:T(8,128)S(1)}, f32[8,2048]{1,0:T(8,128)S(1)}, u32[]{:S(2)}, u32[]{:S(2)}) collective-permute-start(f32[8,2048]{1,0:T(8,128)S(1)} %add_add_fusion), channel_id=1, source_target_pairs={{0,16},{4,20},{8,24},{12,28},{16,0},{20,4},{24,8},{28,12},{1,17},{... | collective-permute-start | bytes 196616 | tf_op jit(solution)/shard_map/ppermute | solution.py:273
  76.3 2.6 %collective-permute-done.9 = f32[8,2048]{1,0:T(8,128)S(1)} collective-permute-done((f32[8,2048]{1,0:T(8,128)S(1)}, f32[8,2048]{1,0:T(8,128)S(1)}, u32[]{:S(2)}, u32[]{:S(2)}) %collective-permute-start.9) | collective-permute-done | bytes 65568 | tf_op jit(solution)/shard_map/ppermute | solution.py:273
  78.9 0.6 add.27
  (2 shorter events, 0.0 us)
Async XLA Ops:
  2.0 14.6 %collective-permute-start.2 = (f32[24,2048]{1,0:T(8,128)S(1)}, f32[24,2048]{1,0:T(8,128)S(1)}, u32[]{:S(2)}, u32[]{:S(2)}) collective-permute-start(f32[24,2048]{1,0:T(8,128)S(1)} %get-tuple-element.13.refs_0_), channel_id=1, source_target_pairs={{0,3},{1,2},{2,1},{3,0},{4,7},{5,6},{6,5},{7,4},{8,11},{9,10},{10,... | collective-permute-start | bytes 589832 | tf_op jit(solution)/shard_map/ppermute | solution.py:273
  4.5 12.2 %collective-permute-start.1 = (f32[24,2048]{1,0:T(8,128)S(1)}, f32[24,2048]{1,0:T(8,128)S(1)}, u32[]{:S(2)}, u32[]{:S(2)}) collective-permute-start(f32[24,2048]{1,0:T(8,128)S(1)} %get-tuple-element.13.refs_0_), channel_id=1, source_target_pairs={{0,2},{1,3},{2,0},{3,1},{4,6},{5,7},{6,4},{7,5},{8,10},{9,11},{10,... | collective-permute-start | bytes 589832 | tf_op jit(solution)/shard_map/ppermute | solution.py:273
  5.1 11.5 %collective-permute-start = (f32[24,2048]{1,0:T(8,128)S(1)}, f32[24,2048]{1,0:T(8,128)S(1)}, u32[]{:S(2)}, u32[]{:S(2)}) collective-permute-start(f32[24,2048]{1,0:T(8,128)S(1)} %get-tuple-element.13.refs_0_), channel_id=1, source_target_pairs={{0,1},{1,0},{2,3},{3,2},{4,5},{5,4},{6,7},{7,6},{8,9},{9,8},{10,11... | collective-permute-start | bytes 589832 | tf_op jit(solution)/shard_map/ppermute | solution.py:273
  59.6 6.5 %collective-permute-start.3 = (f32[8,2048]{1,0:T(8,128)S(1)}, f32[8,2048]{1,0:T(8,128)S(1)}, u32[]{:S(2)}, u32[]{:S(2)}) collective-permute-start(f32[8,2048]{1,0:T(8,128)S(1)} %get-tuple-element.20), channel_id=1, source_target_pairs={{0,1},{1,0},{2,3},{3,2},{4,5},{5,4},{6,7},{7,6},{8,9},{9,8},{10,11... | collective-permute-start | bytes 196616 | tf_op jit(solution)/shard_map/ppermute | solution.py:273
  60.1 6.0 %collective-permute-start.4 = (f32[8,2048]{1,0:T(8,128)S(1)}, f32[8,2048]{1,0:T(8,128)S(1)}, u32[]{:S(2)}, u32[]{:S(2)}) collective-permute-start(f32[8,2048]{1,0:T(8,128)S(1)} %get-tuple-element.21), channel_id=1, source_target_pairs={{0,2},{1,3},{2,0},{3,1},{4,6},{5,7},{6,4},{7,5},{8,10},{9,11},{10,... | collective-permute-start | bytes 196616 | tf_op jit(solution)/shard_map/ppermute | solution.py:273
  61.5 4.6 %collective-permute-start.5 = (f32[8,2048]{1,0:T(8,128)S(1)}, f32[8,2048]{1,0:T(8,128)S(1)}, u32[]{:S(2)}, u32[]{:S(2)}) collective-permute-start(f32[8,2048]{1,0:T(8,128)S(1)} %get-tuple-element.22), channel_id=1, source_target_pairs={{0,3},{1,2},{2,1},{3,0},{4,7},{5,6},{6,5},{7,4},{8,11},{9,10},{10,... | collective-permute-start | bytes 196616 | tf_op jit(solution)/shard_map/ppermute | solution.py:273
  66.1 5.8 %collective-permute-start.8 = (f32[8,2048]{1,0:T(8,128)S(1)}, f32[8,2048]{1,0:T(8,128)S(1)}, u32[]{:S(2)}, u32[]{:S(2)}) collective-permute-start(f32[8,2048]{1,0:T(8,128)S(1)} %fusion.1), channel_id=1, source_target_pairs={{0,12},{4,8},{8,4},{12,0},{16,28},{20,24},{24,20},{28,16},{1,13},{... | collective-permute-start | bytes 196616 | tf_op jit(solution)/shard_map/ppermute | solution.py:273
  68.9 4.3 %collective-permute-start.7 = (f32[8,2048]{1,0:T(8,128)S(1)}, f32[8,2048]{1,0:T(8,128)S(1)}, u32[]{:S(2)}, u32[]{:S(2)}) collective-permute-start(f32[8,2048]{1,0:T(8,128)S(1)} %fusion.1), channel_id=1, source_target_pairs={{0,8},{4,12},{8,0},{12,4},{16,24},{20,28},{24,16},{28,20},{1,9},{5... | collective-permute-start | bytes 196616 | tf_op jit(solution)/shard_map/ppermute | solution.py:273
  69.3 4.3 %collective-permute-start.6 = (f32[8,2048]{1,0:T(8,128)S(1)}, f32[8,2048]{1,0:T(8,128)S(1)}, u32[]{:S(2)}, u32[]{:S(2)}) collective-permute-start(f32[8,2048]{1,0:T(8,128)S(1)} %fusion.1), channel_id=1, source_target_pairs={{0,4},{4,0},{8,12},{12,8},{16,20},{20,16},{24,28},{28,24},{1,5},{5... | collective-permute-start | bytes 196616 | tf_op jit(solution)/shard_map/ppermute | solution.py:273
  73.6 5.3 %collective-permute-start.9 = (f32[8,2048]{1,0:T(8,128)S(1)}, f32[8,2048]{1,0:T(8,128)S(1)}, u32[]{:S(2)}, u32[]{:S(2)}) collective-permute-start(f32[8,2048]{1,0:T(8,128)S(1)} %add_add_fusion), channel_id=1, source_target_pairs={{0,16},{4,20},{8,24},{12,28},{16,0},{20,4},{24,8},{28,12},{1,17},{... | collective-permute-start | bytes 196616 | tf_op jit(solution)/shard_map/ppermute | solution.py:273
